TPU v7x, 256 devices: a whole 4x4x8 slice. The times are simulated.
256 devices in a mesh: win: 16 (over z, x_lo), space: 16 (over x_hi, y, core).
Axes of the slice: x: 4 (x_hi: 2, x_lo: 2; x = x_hi * 2 + x_lo), y: 4, z: 8, core: 2. Of those that a mesh axis runs over, the one named last changes fastest.
Arguments:
- first_guess: float32 [16, 2, 384, 384], P('win', None, 'space'), may hold values from -6 to 6
- forcing: float32 [384, 512], P('space'), may hold values from -6 to 6
- swirl: float32 [384], P('space'), may hold values from 0.1 to 1
- radial_op: float32 [384, 384], replicated, may hold values from -0.3125 to 0.3125
- obs_index: int32 [16, 8, 4096], P('win', None, 'space'), may hold values from 0 to 24575
- obs_value: float32 [16, 8, 4096], P('win', None, 'space'), may hold values from -6 to 6
- start_step: int32 [16], P('win'), may hold values from 0 to 63
Outputs:
- final_state: float32 [16, 2, 384, 384], P('win', None, 'space')
- misfit: float32 [16], P('win')
- forcing_gradient: float32 [384, 512], P('space')
Inputs may be any that keep to these rules, and one draw needn't show every extreme that they name: `obs_index`: values of entries in block b of the last dimension name cells of the field rows held in radial block b, as the steps state.
All inputs are finite; a program needn't handle non-finite values.
Results may differ from a plain program's by a relative error of at most 0.0003.
Values sent between devices are 32-bit elements; how exact they have to be, the bound alone decides.
No kernel may reach another device: no remote copies, remote signals or barrier semaphores. Data moves between devices by JAX's collectives and lax.ppermute only.
A program may use at most 128 MiB of HBM per device.

v0:
```python
import math

import jax
import jax.numpy as jnp
from jax import lax
from jax.sharding import PartitionSpec as P

MODES = 192
STEPS = 8
ROT = 8


step_size = 0.25
radial_scale = 0.4
radial_damping = 0.4
axial_speed = 0.4
advection_gain = 0.2
highest = lax.Precision.HIGHEST


def tables(coeffs, points):
    slot_ids = jnp.arange(coeffs, dtype=jnp.int32)
    wavenumber = jnp.where(slot_ids < MODES, slot_ids, slot_ids - MODES + 1)
    columns = jnp.arange(points, dtype=jnp.int32)
    phases = wavenumber[:, None] * columns[None, :] % points
    angles = 2.0 * math.pi / points * phases.astype(jnp.float32)
    weights = jnp.where(wavenumber == 0, 1.0 / math.sqrt(points), math.sqrt(2.0 / points))[:, None]
    cosine_rows = (slot_ids < MODES)[:, None]
    synthesis = weights * jnp.where(cosine_rows, jnp.cos(angles), jnp.sin(angles))
    factor = weights * (2.0 * math.pi / points) * wavenumber.astype(jnp.float32)[:, None]
    slopes = factor * jnp.where(cosine_rows, -jnp.sin(angles), jnp.cos(angles))
    return (synthesis, jnp.concatenate([synthesis, slopes], 1), wavenumber)


def radial(source_field, matrix, pattern):
    coupled = jnp.einsum(
        pattern,
        matrix,
        lax.all_to_all(source_field, "space", split_axis=2, concat_axis=1, tiled=True),
        precision=highest,
    )
    return lax.all_to_all(coupled, "space", split_axis=1, concat_axis=2, tiled=True)


def per_device(first_guess, forcing, swirl, radial_op, obs_index, obs_value, start_step):
    state = first_guess[0]
    planes = state.shape[0]
    radial_rows = state.shape[1]
    coeffs = state.shape[2]
    points = forcing.shape[1]
    synthesis, paired_table, wavenumber = tables(coeffs, points)
    viscosity = (wavenumber.astype(jnp.float32) / MODES) ** 2
    damping = radial_damping + axial_speed + viscosity
    centre = jnp.arange(planes, dtype=jnp.float32) + 0.5 - planes / 2.0
    profile = jnp.exp(-((centre * (4.0 / planes)) ** 2))
    sample_rows = obs_index[0]
    values = obs_value[0]
    phase_start = start_step[0]
    swirl_column = swirl[None, :, None]

    def expand(current):
        expanded = jnp.einsum("ark,kt->art", current, paired_table, precision=highest)
        return (expanded[..., :points], expanded[..., points:])

    def project(source_field):
        return jnp.einsum("art,kt->ark", source_field, synthesis, precision=highest)

    def inject(instant):
        scattered = (
            jnp.zeros((planes * radial_rows * points,), jnp.float32)
            .at[sample_rows[instant]]
            .add(misses[instant])
        )
        return scattered.reshape(planes, radial_rows, points)

    velocity, derivative = expand(state)
    history = []
    misses = []
    squares = jnp.zeros((), jnp.float32)
    for instant in range(STEPS):
        turn_cells = ROT * (phase_start + instant) % points
        body_force = profile[:, None, None] * jnp.roll(forcing, turn_cells, axis=1)[None]
        tendency = -(swirl_column + advection_gain * velocity) * derivative + body_force
        coupled = radial(velocity, radial_op, "rs,ask->ark")
        change = project(tendency + radial_scale * coupled)
        upstream = jnp.concatenate([jnp.zeros_like(state[:1]), state[:-1]], 0)
        history.append((velocity, derivative))
        state = state + step_size * (change - damping * state + axial_speed * upstream)
        velocity, derivative = expand(state)
        residual = velocity.reshape(-1)[sample_rows[instant]] - values[instant]
        misses.append(residual)
        squares = squares + jnp.sum(residual * residual)
    summed = lax.psum(squares, "space")
    misfit = (summed * (0.5 / (STEPS * sample_rows.shape[1] * lax.axis_size("space")))).reshape(1)
    adjoint = project(inject(STEPS - 1))
    gradient = jnp.zeros_like(forcing)
    for instant in range(STEPS - 1, -1, -1):
        scaled = step_size * adjoint
        pulled = jnp.einsum("ark,kt->art", scaled, synthesis, precision=highest)
        turn_cells = ROT * (phase_start + instant) % points
        weighted = jnp.einsum("a,art->rt", profile, pulled, precision=highest)
        gradient = gradient + jnp.roll(weighted, -turn_cells, axis=1)
        if instant > 0:
            past_velocity, past_derivative = history[instant]
            toward_velocity = inject(instant - 1) - advection_gain * past_derivative * pulled
            toward_slope = -(swirl_column + advection_gain * past_velocity) * pulled
            downstream = jnp.concatenate([scaled[1:], jnp.zeros_like(scaled[:1])], 0)
            coupled = radial(pulled, radial_op, "sr,ask->ark")
            toward_velocity = toward_velocity + radial_scale * coupled
            back = jnp.einsum(
                "art,kt->ark",
                jnp.concatenate([toward_velocity, toward_slope], -1),
                paired_table,
                precision=highest,
            )
            adjoint = adjoint + back - damping * scaled + axial_speed * downstream
    forcing_gradient = lax.psum(gradient, "win")
    return (state[None], misfit, forcing_gradient)


def solution(mesh):
    return jax.shard_map(
        per_device,
        mesh=mesh,
        in_specs=(
            P("win", None, "space", None),
            P("space", None),
            P("space"),
            P(),
            P("win", None, "space"),
            P("win", None, "space"),
            P("win"),
        ),
        out_specs=(P("win", None, "space", None), P("win"), P("space", None)),
        check_vma=False,
    )
```

profile of v0, /device:TPU:2, one launch (start us, length us, event | category | flops | bytes accessed | tf_op | source)
XLA Modules:
  0.0 706.3 jit_solution(9940522005987088990)
XLA Ops:
  7.0 6.1 all-to-all-start
  15.6 5.3 all-to-all-done
  29.6 7.7 %all-to-all-done.1 = f32[16,1,1536]{2,1,0:T(1,128)S(1)} async-done(((f32[16,1,1536]{2,1,0:T(1,128)}), f32[16,1,1536]{2,1,0:T(1,128)S(1)}, u32[]{:S(2)}, u32[]{:S(2)}) %all-to-all-start.1) | async-done | bytes 98336 | tf_op jit(solution)/shard_map/all_to_all | solution.py:42
  46.8 10.4 %all_to_all.405 = f32[16,1,1536]{2,1,0:T(1,128)S(1)} all-to-all(f32[16,1,1536]{2,1,0:T(1,128)S(1)} %reshape.638), channel_id=1, replica_groups=mesh['win'=16,'space'=16] {'space'}, dimensions={0} | all-to-all | bytes 196608 | tf_op jit(solution)/shard_map/all_to_all | solution.py:39
  65.5 7.8 %all-to-all-done.3 = f32[16,1,1536]{2,1,0:T(1,128)S(1)} async-done(((f32[16,1,1536]{2,1,0:T(1,128)}), f32[16,1,1536]{2,1,0:T(1,128)S(1)}, u32[]{:S(2)}, u32[]{:S(2)}) %all-to-all-start.3) | async-done | bytes 98336 | tf_op jit(solution)/shard_map/all_to_all | solution.py:42
  82.6 10.4 %all_to_all.406 = f32[16,1,1536]{2,1,0:T(1,128)S(1)} all-to-all(f32[16,1,1536]{2,1,0:T(1,128)S(1)} %reshape.642), channel_id=1, replica_groups=mesh['win'=16,'space'=16] {'space'}, dimensions={0} | all-to-all | bytes 196608 | tf_op jit(solution)/shard_map/all_to_all | solution.py:39
  101.1 7.8 %all-to-all-done.5 = f32[16,1,1536]{2,1,0:T(1,128)S(1)} async-done(((f32[16,1,1536]{2,1,0:T(1,128)}), f32[16,1,1536]{2,1,0:T(1,128)S(1)}, u32[]{:S(2)}, u32[]{:S(2)}) %all-to-all-start.5) | async-done | bytes 98336 | tf_op jit(solution)/shard_map/all_to_all | solution.py:42
  111.3 5.0 fusion.32
  119.2 10.4 %all_to_all.407 = f32[16,1,1536]{2,1,0:T(1,128)S(1)} all-to-all(f32[16,1,1536]{2,1,0:T(1,128)S(1)} %reshape.646), channel_id=1, replica_groups=mesh['win'=16,'space'=16] {'space'}, dimensions={0} | all-to-all | bytes 196608 | tf_op jit(solution)/shard_map/all_to_all | solution.py:39
  137.7 7.8 %all-to-all-done.7 = f32[16,1,1536]{2,1,0:T(1,128)S(1)} async-done(((f32[16,1,1536]{2,1,0:T(1,128)}), f32[16,1,1536]{2,1,0:T(1,128)S(1)}, u32[]{:S(2)}, u32[]{:S(2)}) %all-to-all-start.7) | async-done | bytes 98336 | tf_op jit(solution)/shard_map/all_to_all | solution.py:42
  160.4 7.1 %all-to-all-done.8 = f32[16,1,1536]{2,1,0:T(1,128)S(1)} async-done(((f32[16,1,1536]{2,1,0:T(1,128)}), f32[16,1,1536]{2,1,0:T(1,128)S(1)}, u32[]{:S(2)}, u32[]{:S(2)}) %all-to-all-start.8) | async-done | bytes 98336 | tf_op jit(solution)/shard_map/all_to_all | solution.py:39
  176.5 7.1 %all-to-all-done.9 = f32[16,1,1536]{2,1,0:T(1,128)S(1)} async-done(((f32[16,1,1536]{2,1,0:T(1,128)}), f32[16,1,1536]{2,1,0:T(1,128)S(1)}, u32[]{:S(2)}, u32[]{:S(2)}) %all-to-all-start.9) | async-done | bytes 98336 | tf_op jit(solution)/shard_map/all_to_all | solution.py:42
  199.3 6.5 all-to-all-done.10
  213.9 7.7 %all-to-all-done.11 = f32[16,1,1536]{2,1,0:T(1,128)S(1)} async-done(((f32[16,1,1536]{2,1,0:T(1,128)}), f32[16,1,1536]{2,1,0:T(1,128)S(1)}, u32[]{:S(2)}, u32[]{:S(2)}) %all-to-all-start.11) | async-done | bytes 98336 | tf_op jit(solution)/shard_map/all_to_all | solution.py:42
  224.0 5.0 fusion.23
  236.6 7.2 %all-to-all-done.12 = f32[16,1,1536]{2,1,0:T(1,128)S(1)} async-done(((f32[16,1,1536]{2,1,0:T(1,128)}), f32[16,1,1536]{2,1,0:T(1,128)S(1)}, u32[]{:S(2)}, u32[]{:S(2)}) %all-to-all-start.12) | async-done | bytes 98336 | tf_op jit(solution)/shard_map/all_to_all | solution.py:39
  252.5 7.1 %all-to-all-done.13 = f32[16,1,1536]{2,1,0:T(1,128)S(1)} async-done(((f32[16,1,1536]{2,1,0:T(1,128)}), f32[16,1,1536]{2,1,0:T(1,128)S(1)}, u32[]{:S(2)}, u32[]{:S(2)}) %all-to-all-start.13) | async-done | bytes 98336 | tf_op jit(solution)/shard_map/all_to_all | solution.py:42
  274.1 7.7 %all-to-all-done.14 = f32[16,1,1536]{2,1,0:T(1,128)S(1)} async-done(((f32[16,1,1536]{2,1,0:T(1,128)}), f32[16,1,1536]{2,1,0:T(1,128)S(1)}, u32[]{:S(2)}, u32[]{:S(2)}) %all-to-all-start.14) | async-done | bytes 98336 | tf_op jit(solution)/shard_map/all_to_all | solution.py:39
  292.5 5.4 all-to-all-done.15
  300.3 5.1 fusion.17
  336.4 6.7 all-to-all-start.17
  379.4 7.2 %all-to-all-start.19 = ((f32[16,1,1536]{2,1,0:T(1,128)}), f32[16,1,1536]{2,1,0:T(1,128)S(1)}, u32[]{:S(2)}, u32[]{:S(2)}) async-start(f32[16,1,1536]{2,1,0:T(1,128)} %reshape.672), calls=%async_computation.19 | async-start | bytes 196608 | tf_op jit(solution)/shard_map/all_to_all | solution.py:42
  422.6 7.4 %all-to-all-start.21 = ((f32[16,1,1536]{2,1,0:T(1,128)}), f32[16,1,1536]{2,1,0:T(1,128)S(1)}, u32[]{:S(2)}, u32[]{:S(2)}) async-start(f32[16,1,1536]{2,1,0:T(1,128)} %reshape.676), calls=%async_computation.21 | async-start | bytes 196608 | tf_op jit(solution)/shard_map/all_to_all | solution.py:42
  466.6 6.5 all-to-all-start.23
  473.6 38.9 %psum.14 = f32[]{:T(128)} all-reduce(f32[]{:T(128)S(6)} %add.754), channel_id=1, replica_groups=mesh['win'=16,'space'=16] {'space'}, use_global_device_ids=true, to_apply=%region_8.10 | all-reduce | flops 1 | bytes 8 | tf_op jit(solution)/shard_map/psum | solution.py:93
  531.9 6.6 all-to-all-done.24
  548.7 5.3 all-to-all-done.25
  570.7 6.6 all-to-all-done.26
  587.5 5.3 all-to-all-done.27
  609.0 7.2 %all-to-all-done.28 = f32[16,1,1536]{2,1,0:T(1,128)S(1)} async-done(((f32[16,1,1536]{2,1,0:T(1,128)}), f32[16,1,1536]{2,1,0:T(1,128)S(1)}, u32[]{:S(2)}, u32[]{:S(2)}) %all-to-all-start.28) | async-done | bytes 98336 | tf_op jit(solution)/shard_map/all_to_all | solution.py:39
  626.4 5.3 all-to-all-done.29
  641.4 63.4 %psum.15 = f32[24,512]{1,0:T(8,128)} all-reduce(f32[24,512]{1,0:T(8,128)S(1)} %fusion.212), channel_id=1, replica_groups=mesh['win'=16,'space'=16] {'win'}, use_global_device_ids=true, to_apply=%region_17.19 | all-reduce | flops 12288 | bytes 98304 | tf_op jit(solution)/shard_map/psum | solution.py:117
  (702 shorter events, 382.2 us)
Async XLA Ops:
  7.0 14.0 %all-to-all-start = ((f32[16,1,1536]{2,1,0:T(1,128)}), f32[16,1,1536]{2,1,0:T(1,128)S(1)}, u32[]{:S(2)}, u32[]{:S(2)}) async-start(f32[16,1,1536]{2,1,0:T(1,128)} %reshape.634), calls=%async_computation | async-start | bytes 196608 | tf_op jit(solution)/shard_map/all_to_all | solution.py:39
  25.9 11.5 %all-to-all-start.1 = ((f32[16,1,1536]{2,1,0:T(1,128)}), f32[16,1,1536]{2,1,0:T(1,128)S(1)}, u32[]{:S(2)}, u32[]{:S(2)}) async-start(f32[16,1,1536]{2,1,0:T(1,128)} %reshape.636), calls=%async_computation.1 | async-start | bytes 196608 | tf_op jit(solution)/shard_map/all_to_all | solution.py:42
  61.6 11.7 %all-to-all-start.3 = ((f32[16,1,1536]{2,1,0:T(1,128)}), f32[16,1,1536]{2,1,0:T(1,128)S(1)}, u32[]{:S(2)}, u32[]{:S(2)}) async-start(f32[16,1,1536]{2,1,0:T(1,128)} %reshape.640), calls=%async_computation.3 | async-start | bytes 196608 | tf_op jit(solution)/shard_map/all_to_all | solution.py:42
  97.4 11.4 %all-to-all-start.5 = ((f32[16,1,1536]{2,1,0:T(1,128)}), f32[16,1,1536]{2,1,0:T(1,128)S(1)}, u32[]{:S(2)}, u32[]{:S(2)}) async-start(f32[16,1,1536]{2,1,0:T(1,128)} %reshape.644), calls=%async_computation.5 | async-start | bytes 196608 | tf_op jit(solution)/shard_map/all_to_all | solution.py:42
  134.0 11.5 %all-to-all-start.7 = ((f32[16,1,1536]{2,1,0:T(1,128)}), f32[16,1,1536]{2,1,0:T(1,128)S(1)}, u32[]{:S(2)}, u32[]{:S(2)}) async-start(f32[16,1,1536]{2,1,0:T(1,128)} %reshape.648), calls=%async_computation.7 | async-start | bytes 196608 | tf_op jit(solution)/shard_map/all_to_all | solution.py:42
  156.3 11.3 %all-to-all-start.8 = ((f32[16,1,1536]{2,1,0:T(1,128)}), f32[16,1,1536]{2,1,0:T(1,128)S(1)}, u32[]{:S(2)}, u32[]{:S(2)}) async-start(f32[16,1,1536]{2,1,0:T(1,128)} %reshape.650), calls=%async_computation.8 | async-start | bytes 196608 | tf_op jit(solution)/shard_map/all_to_all | solution.py:39
  160.4 75.6 %copy-start.101 = (s32[256,1]{0,1:T(1,128)}, s32[256,1]{0,1:T(1,128)S(1)}, u32[]{:S(2)}) copy-start(s32[256,1]{0,1:T(1,128)S(1)} %get-tuple-element.53) | copy-start | bytes 3076
  160.4 75.6 %copy-start.105 = (s32[256,1]{0,1:T(1,128)}, s32[256,1]{0,1:T(1,128)S(1)}, u32[]{:S(2)}) copy-start(s32[256,1]{0,1:T(1,128)S(1)} %get-tuple-element.54) | copy-start | bytes 3076
  160.4 91.5 %copy-start.103 = (s32[256,1]{0,1:T(1,128)}, s32[256,1]{0,1:T(1,128)S(1)}, u32[]{:S(2)}) copy-start(s32[256,1]{0,1:T(1,128)S(1)} %get-tuple-element.52) | copy-start | bytes 3076
  160.4 91.5 %copy-start.107 = (s32[256,1]{0,1:T(1,128)}, s32[256,1]{0,1:T(1,128)S(1)}, u32[]{:S(2)}) copy-start(s32[256,1]{0,1:T(1,128)S(1)} %get-tuple-element.51) | copy-start | bytes 3076
  172.0 11.7 %all-to-all-start.9 = ((f32[16,1,1536]{2,1,0:T(1,128)}), f32[16,1,1536]{2,1,0:T(1,128)S(1)}, u32[]{:S(2)}, u32[]{:S(2)}) async-start(f32[16,1,1536]{2,1,0:T(1,128)} %reshape.652), calls=%async_computation.9 | async-start | bytes 196608 | tf_op jit(solution)/shard_map/all_to_all | solution.py:42
  194.5 11.3 %all-to-all-start.10 = ((f32[16,1,1536]{2,1,0:T(1,128)}), f32[16,1,1536]{2,1,0:T(1,128)S(1)}, u32[]{:S(2)}, u32[]{:S(2)}) async-start(f32[16,1,1536]{2,1,0:T(1,128)} %reshape.654), calls=%async_computation.10 | async-start | bytes 196608 | tf_op jit(solution)/shard_map/all_to_all | solution.py:39
  210.2 11.4 %all-to-all-start.11 = ((f32[16,1,1536]{2,1,0:T(1,128)}), f32[16,1,1536]{2,1,0:T(1,128)S(1)}, u32[]{:S(2)}, u32[]{:S(2)}) async-start(f32[16,1,1536]{2,1,0:T(1,128)} %reshape.656), calls=%async_computation.11 | async-start | bytes 196608 | tf_op jit(solution)/shard_map/all_to_all | solution.py:42
  232.5 11.3 %all-to-all-start.12 = ((f32[16,1,1536]{2,1,0:T(1,128)}), f32[16,1,1536]{2,1,0:T(1,128)S(1)}, u32[]{:S(2)}, u32[]{:S(2)}) async-start(f32[16,1,1536]{2,1,0:T(1,128)} %reshape.658), calls=%async_computation.12 | async-start | bytes 196608 | tf_op jit(solution)/shard_map/all_to_all | solution.py:39
  248.2 11.5 %all-to-all-start.13 = ((f32[16,1,1536]{2,1,0:T(1,128)}), f32[16,1,1536]{2,1,0:T(1,128)S(1)}, u32[]{:S(2)}, u32[]{:S(2)}) async-start(f32[16,1,1536]{2,1,0:T(1,128)} %reshape.660), calls=%async_computation.13 | async-start | bytes 196608 | tf_op jit(solution)/shard_map/all_to_all | solution.py:42
  270.6 11.3 %all-to-all-start.14 = ((f32[16,1,1536]{2,1,0:T(1,128)}), f32[16,1,1536]{2,1,0:T(1,128)S(1)}, u32[]{:S(2)}, u32[]{:S(2)}) async-start(f32[16,1,1536]{2,1,0:T(1,128)} %reshape.662), calls=%async_computation.14 | async-start | bytes 196608 | tf_op jit(solution)/shard_map/all_to_all | solution.py:39
  286.2 11.7 %all-to-all-start.15 = ((f32[16,1,1536]{2,1,0:T(1,128)}), f32[16,1,1536]{2,1,0:T(1,128)S(1)}, u32[]{:S(2)}, u32[]{:S(2)}) async-start(f32[16,1,1536]{2,1,0:T(1,128)} %reshape.664), calls=%async_computation.15 | async-start | bytes 196608 | tf_op jit(solution)/shard_map/all_to_all | solution.py:42
  290.2 306.0 %copy-start.73 = (f32[384]{0:T(512)}, f32[384]{0:T(512)S(1)}, u32[]{:S(2)}) copy-start(f32[384]{0:T(512)S(1)} %fusion.291) | copy-start | bytes 4612
  321.0 11.3 %all-to-all-start.16 = ((f32[16,1,1536]{2,1,0:T(1,128)}), f32[16,1,1536]{2,1,0:T(1,128)S(1)}, u32[]{:S(2)}, u32[]{:S(2)}) async-start(f32[16,1,1536]{2,1,0:T(1,128)} %reshape.666), calls=%async_computation.16 | async-start | bytes 196608 | tf_op jit(solution)/shard_map/all_to_all | solution.py:39
  336.4 14.6 %all-to-all-start.17 = ((f32[16,1,1536]{2,1,0:T(1,128)}), f32[16,1,1536]{2,1,0:T(1,128)S(1)}, u32[]{:S(2)}, u32[]{:S(2)}) async-start(f32[16,1,1536]{2,1,0:T(1,128)} %reshape.668), calls=%async_computation.17 | async-start | bytes 196608 | tf_op jit(solution)/shard_map/all_to_all | solution.py:42
  362.9 12.3 %all-to-all-start.18 = ((f32[16,1,1536]{2,1,0:T(1,128)}), f32[16,1,1536]{2,1,0:T(1,128)S(1)}, u32[]{:S(2)}, u32[]{:S(2)}) async-start(f32[16,1,1536]{2,1,0:T(1,128)} %reshape.670), calls=%async_computation.18 | async-start | bytes 196608 | tf_op jit(solution)/shard_map/all_to_all | solution.py:39
  379.4 15.0 %all-to-all-start.19 = ((f32[16,1,1536]{2,1,0:T(1,128)}), f32[16,1,1536]{2,1,0:T(1,128)S(1)}, u32[]{:S(2)}, u32[]{:S(2)}) async-start(f32[16,1,1536]{2,1,0:T(1,128)} %reshape.672), calls=%async_computation.19 | async-start | bytes 196608 | tf_op jit(solution)/shard_map/all_to_all | solution.py:42
  406.4 12.1 %all-to-all-start.20 = ((f32[16,1,1536]{2,1,0:T(1,128)}), f32[16,1,1536]{2,1,0:T(1,128)S(1)}, u32[]{:S(2)}, u32[]{:S(2)}) async-start(f32[16,1,1536]{2,1,0:T(1,128)} %reshape.674), calls=%async_computation.20 | async-start | bytes 196608 | tf_op jit(solution)/shard_map/all_to_all | solution.py:39
  422.6 15.2 %all-to-all-start.21 = ((f32[16,1,1536]{2,1,0:T(1,128)}), f32[16,1,1536]{2,1,0:T(1,128)S(1)}, u32[]{:S(2)}, u32[]{:S(2)}) async-start(f32[16,1,1536]{2,1,0:T(1,128)} %reshape.676), calls=%async_computation.21 | async-start | bytes 196608 | tf_op jit(solution)/shard_map/all_to_all | solution.py:42
  450.4 12.2 %all-to-all-start.22 = ((f32[16,1,1536]{2,1,0:T(1,128)}), f32[16,1,1536]{2,1,0:T(1,128)S(1)}, u32[]{:S(2)}, u32[]{:S(2)}) async-start(f32[16,1,1536]{2,1,0:T(1,128)} %reshape.678), calls=%async_computation.22 | async-start | bytes 196608 | tf_op jit(solution)/shard_map/all_to_all | solution.py:39
  466.6 48.6 %all-to-all-start.23 = ((f32[16,1,1536]{2,1,0:T(1,128)}), f32[16,1,1536]{2,1,0:T(1,128)S(1)}, u32[]{:S(2)}, u32[]{:S(2)}) async-start(f32[16,1,1536]{2,1,0:T(1,128)} %reshape.680), calls=%async_computation.23 | async-start | bytes 196608 | tf_op jit(solution)/shard_map/all_to_all | solution.py:42
  527.1 11.4 %all-to-all-start.24 = ((f32[16,1,1536]{2,1,0:T(1,128)}), f32[16,1,1536]{2,1,0:T(1,128)S(1)}, u32[]{:S(2)}, u32[]{:S(2)}) async-start(f32[16,1,1536]{2,1,0:T(1,128)} %reshape.682), calls=%async_computation.24 | async-start | bytes 196608 | tf_op jit(solution)/shard_map/all_to_all | solution.py:39
  542.7 11.3 %all-to-all-start.25 = ((f32[16,1,1536]{2,1,0:T(1,128)}), f32[16,1,1536]{2,1,0:T(1,128)S(1)}, u32[]{:S(2)}, u32[]{:S(2)}) async-start(f32[16,1,1536]{2,1,0:T(1,128)} %reshape.684), calls=%async_computation.25 | async-start | bytes 196608 | tf_op jit(solution)/shard_map/all_to_all | solution.py:42
  565.9 11.5 %all-to-all-start.26 = ((f32[16,1,1536]{2,1,0:T(1,128)}), f32[16,1,1536]{2,1,0:T(1,128)S(1)}, u32[]{:S(2)}, u32[]{:S(2)}) async-start(f32[16,1,1536]{2,1,0:T(1,128)} %reshape.686), calls=%async_computation.26 | async-start | bytes 196608 | tf_op jit(solution)/shard_map/all_to_all | solution.py:39
  581.5 11.3 %all-to-all-start.27 = ((f32[16,1,1536]{2,1,0:T(1,128)}), f32[16,1,1536]{2,1,0:T(1,128)S(1)}, u32[]{:S(2)}, u32[]{:S(2)}) async-start(f32[16,1,1536]{2,1,0:T(1,128)} %reshape.688), calls=%async_computation.27 | async-start | bytes 196608 | tf_op jit(solution)/shard_map/all_to_all | solution.py:42
  604.7 11.5 %all-to-all-start.28 = ((f32[16,1,1536]{2,1,0:T(1,128)}), f32[16,1,1536]{2,1,0:T(1,128)S(1)}, u32[]{:S(2)}, u32[]{:S(2)}) async-start(f32[16,1,1536]{2,1,0:T(1,128)} %reshape.690), calls=%async_computation.28 | async-start | bytes 196608 | tf_op jit(solution)/shard_map/all_to_all | solution.py:39
  620.3 11.3 %all-to-all-start.29 = ((f32[16,1,1536]{2,1,0:T(1,128)}), f32[16,1,1536]{2,1,0:T(1,128)S(1)}, u32[]{:S(2)}, u32[]{:S(2)}) async-start(f32[16,1,1536]{2,1,0:T(1,128)} %reshape.692), calls=%async_computation.29 | async-start | bytes 196608 | tf_op jit(solution)/shard_map/all_to_all | solution.py:42
  (147 other events, 841.2 us)
where the time goes:
time: 719 us; the launch traced here: 706 us
  waiting for transfers between devices  141 us (20%)
  blocking collectives  133 us (18%)
  local copies, waits for them, and re-layouts  125 us (17%)
  matrix products  115 us (16%)
  starting transfers between devices  115 us (16%)
  other arithmetic  63.8 us (9%)
  between operations  13.1 us (2%)
    all_to_all x15, waiting for transfers between devices, radial(): lax.all_to_all(coupled, 'space', split_axis=1, concat_axis=2, tiled=True)  85.4 us
    all_to_all x15, starting transfers between devices, radial(): lax.all_to_all(coupled, 'space', split_axis=1, concat_axis=2, tiled=True)  68.5 us
    psum x1, blocking collectives, per_device(): forcing_gradient = lax.psum(gradient, 'win')  63.4 us
    unnamed x359, local copies, waits for them, and re-layouts  61.4 us
    all_to_all x12, waiting for transfers between devices, radial(): lax.all_to_all(source_field, 'space', split_axis=2, concat_axis=1, tiled=...  55.5 us
    all_to_all x12, starting transfers between devices, radial(): lax.all_to_all(source_field, 'space', split_axis=2, concat_axis=1, tiled=...  46.3 us
    dot_general x9, matrix products, project(): return jnp.einsum('art,kt->ark', source_field, synthesis, precision=highest)  42.7 us
    psum x1, blocking collectives, per_device(): summed = lax.psum(squares, 'space')  38.9 us
  transfers between devices with their start and end apart: 27, of which 24 were waited for; matrix products, arithmetic and copies ran while one was open for 8% of the time, Pallas kernels for 0%

commit v1 on v0

v1 whole, which is shorter than its diff:
```python
import math

import jax
import jax.numpy as jnp
import ml_dtypes
import numpy as np
from jax import lax
from jax.experimental import pallas as pl
from jax.experimental.pallas import tpu as pltpu
from jax.sharding import PartitionSpec as P

MODES = 192
STEPS = 8
ROT = 8
NT = 512
NR = 384
AX = 2
HALF = NT // 2
BLOCKS = 16
QR = NR // BLOCKS
OBS = 256
ROWS = AX * NR
COEF = 2 * HALF
VMEM_LIMIT = 60 * 1024 * 1024

step_size = 0.25
radial_scale = 0.4
radial_damping = 0.4
axial_speed = 0.4
advection_gain = 0.2
PROFILE = [math.exp(-(((a + 0.5 - AX / 2.0) * (4.0 / AX)) ** 2)) for a in range(AX)]

OMEGA = 2.0 * math.pi / NT
PHI = OMEGA * np.arange(HALF) / 2.0


def split_np(table):
    high = table.astype(ml_dtypes.bfloat16)
    low = (table - high.astype(np.float64)).astype(ml_dtypes.bfloat16)
    return high, low


def half_tables():
    m = np.arange(HALF)[:, None].astype(np.float64)
    theta = np.arange(HALF)[None, :] + 0.5
    norm = np.where(m == 0, 1.0 / math.sqrt(NT), math.sqrt(2.0 / NT))
    cosine = norm * np.cos(OMEGA * m * theta)
    sine = norm * np.sin(OMEGA * m * theta)
    slope = OMEGA * m
    kept = m < MODES
    last = m == MODES
    sin_phi, cos_phi = math.sin(PHI[MODES]), math.cos(PHI[MODES])
    even_u = np.where(kept, cosine, np.where(last, -sin_phi * cosine, 0.0))
    odd_u = np.where(kept & (m > 0), sine, np.where(last, cos_phi * sine, 0.0))
    odd_v = np.where(kept, -slope * sine, np.where(last, sin_phi * slope * sine, 0.0))
    even_v = np.where(kept & (m > 0), slope * cosine, np.where(last, cos_phi * slope * cosine, 0.0))
    from_cos = np.concatenate([even_u, odd_v], 1)
    from_sin = np.concatenate([odd_u, even_v], 1)
    return from_cos, from_sin


def whole_table():
    m = np.arange(HALF)[:, None].astype(np.float64)
    theta = np.arange(NT)[None, :] + 0.5
    norm = np.where(m == 0, 1.0 / math.sqrt(NT), math.sqrt(2.0 / NT))
    cosine = np.where(m <= MODES, norm * np.cos(OMEGA * m * theta), 0.0)
    sine = np.where((m <= MODES) & (m > 0), norm * np.sin(OMEGA * m * theta), 0.0)
    return np.concatenate([cosine, sine], 0)


def lane_rows():
    m = np.arange(HALF)
    kept = (m >= 1) & (m < MODES)
    last = m == MODES
    cos_phi, sin_phi = np.cos(PHI), np.sin(PHI)
    rows = np.zeros((16, HALF))
    rows[0] = np.where(kept, cos_phi, np.where(m == 0, 1.0, 0.0))
    rows[1] = np.where(kept, -sin_phi, np.where(last, 1.0, 0.0))
    rows[2] = np.where(kept, sin_phi, 0.0)
    rows[3] = np.where(kept, cos_phi, np.where(last, 1.0, 0.0))
    rows[4] = np.where(kept, cos_phi, np.where(m == 0, 1.0, 0.0))
    rows[5] = np.where(kept, sin_phi, 0.0)
    rows[6] = np.where(kept, -sin_phi, 0.0)
    rows[7] = np.where(kept, cos_phi, np.where(last, 1.0, 0.0))
    rows[8] = np.where(m <= MODES, 1.0 - step_size * (radial_damping + axial_speed + (m / MODES) ** 2), 0.0)
    rows[9] = np.where(last, 1.0, 0.0)
    return rows.astype(np.float32)


def turn_tables(phase_start):
    m = jnp.arange(HALF, dtype=jnp.int32)[None, :]
    cells = ROT * (phase_start + jnp.arange(STEPS, dtype=jnp.int32))[:, None]
    angles = OMEGA * ((m * cells) % NT).astype(jnp.float32)
    cosine, sine = jnp.cos(angles), jnp.sin(angles)
    sin_phi, cos_phi = math.sin(PHI[MODES]), math.cos(PHI[MODES])
    last = m == MODES
    first = -sin_phi * cosine + cos_phi * sine
    second = sin_phi * sine + cos_phi * cosine
    forward = [
        jnp.where(last, first, cosine),
        jnp.where(last, second, -sine),
        jnp.where(last, first, sine),
        jnp.where(last, second, cosine),
    ]
    back = [
        forward[0],
        jnp.where(last, 0.0, sine),
        forward[1],
        jnp.where(last, 0.0, cosine),
    ]
    keep = (m <= MODES).astype(jnp.float32)
    return jnp.stack([row * keep for row in forward + back], 1)


def split(x):
    high = x.astype(jnp.bfloat16)
    return high, (x - high.astype(jnp.float32)).astype(jnp.bfloat16)


def mm(a, b):
    return jnp.dot(a, b, preferred_element_type=jnp.float32)


def mm3(xh, xl, th, tl):
    return mm(xh, th) + mm(xl, th) + mm(xh, tl)


def kernel(
    place, turns, lanes, radial_op, tch, tcl, tsh, tsl, bch, bcl, bsh, bsl, fth, ftl, gth, gtl,
    p0, p1, p2, p3, p4, q0, q1, q2, q3, q4,
    final_out, grad_out, miss_out,
    state, high, rad, hist_u, hist_v, inject, rl, rtl, swirl, forced, obs_i, obs_v, gsum, msum,
):
    me = place[0]
    core = me % 2
    across = me // 8
    up = (me // 2) % 4

    def block_of(d, flip_x, flip_core):
        y = (up + 4 - d) % 4
        x = 1 - across if flip_x else across
        c = 1 - core if flip_core else core
        return x * 8 + y * 2 + c

    sources = [(p0, 0, 0, False, False), (p1, 0, 0, True, False), (q0, 0, 0, False, True), (q1, 0, 0, True, True)]
    for d, (pd, qd) in enumerate(((p2, q2), (p3, q3), (p4, q4)), 1):
        sources += [(pd, 0, d, False, False), (pd, QR, d, True, False), (qd, 0, d, False, True), (qd, QR, d, True, True)]

    def lane(i):
        return lanes[i:i + 1, :]

    square = lax.broadcasted_iota(jnp.int32, (QR, 128), 0) == lax.broadcasted_iota(jnp.int32, (QR, 128), 1)
    for ref, row, d, flip_x, flip_core in sources:
        block = block_of(d, flip_x, flip_core)
        at = pl.multiple_of(block * QR, 8)
        for a in range(AX):
            first = ref[row:row + QR, 384 * a:384 * a + HALF]
            second = pltpu.roll(ref[row:row + QR, 384 * a + 128:384 * a + 384], 193, 1)
            spot = pl.multiple_of(a * NR + at, 8)
            state[pl.ds(spot, QR), 0:HALF] = first * lane(0) + second * lane(1)
            state[pl.ds(spot, QR), HALF:COEF] = first * lane(2) + second * lane(3)
        forced[pl.ds(at, QR), :] = ref[row:row + QR, 768:1280]
        spread = jnp.where(square, ref[row + 16:row + 17, 1280:1408], 0.0)
        swirl[pl.ds(at, QR), :] = jnp.broadcast_to(jnp.sum(spread, 1, keepdims=True), (QR, 128))
        if not flip_core:
            slot = pl.multiple_of((block // 2) * STEPS, 8)
            obs_i[pl.ds(slot, STEPS), :] = ref[row:row + 8, 1280:1536].astype(jnp.int32)
            obs_v[pl.ds(slot, STEPS), :] = ref[row + 8:row + 16, 1280:1536]

    fh, fl = split(forced[...])
    forced[...] = mm3(fh, fl, fth[...], ftl[...]) * step_size

    scaled = (step_size * radial_scale) * radial_op[...]
    rh, rlow = split(scaled)
    rl[:, 0:NR], rl[:, NR:2 * NR], rl[:, 2 * NR:] = rh, rlow, rh
    th, tlow = split(scaled.T)
    rtl[:, 0:NR], rtl[:, NR:2 * NR], rtl[:, 2 * NR:] = th, tlow, th
    inject[...] = jnp.zeros_like(inject)
    gsum[...] = jnp.zeros_like(gsum)
    msum[...] = jnp.zeros_like(msum)

    mark = lane(9)
    decay = lane(8)
    reach = step_size * axial_speed

    def store_split(a):
        h, l = split(state[a * NR:(a + 1) * NR, :])
        high[a, 0:NR, :] = h
        high[a, NR:2 * NR, :] = h
        high[a, 2 * NR:, :] = l

    def couple(operator):
        for a in range(AX):
            rad[a] = mm(operator[...], high[a])

    def halves(a, part):
        lanes_of = slice(0, HALF) if part == 0 else slice(HALF, COEF)
        return high[a, 0:NR, lanes_of], high[a, 2 * NR:, lanes_of]

    def fold(pc, ps):
        return pc + mark * ps, ps + mark * pc

    def expand_u(a):
        ch, cl = halves(a, 0)
        sh, sl = halves(a, 1)
        eu = mm3(ch, cl, tch[:, 0:HALF], tcl[:, 0:HALF])
        ou = mm3(sh, sl, tsh[:, 0:HALF], tsl[:, 0:HALF])
        return eu, ou

    def forward_step(k):
        couple(rl)
        body_c = turns[k, 0:1, :] * forced[:, 0:HALF] + turns[k, 1:2, :] * forced[:, HALF:COEF]
        body_s = turns[k, 2:3, :] * forced[:, 0:HALF] + turns[k, 3:4, :] * forced[:, HALF:COEF]
        sw = jnp.concatenate([swirl[...], swirl[...]], 1)
        for a in range(AX - 1, -1, -1):
            rows = slice(a * NR, (a + 1) * NR)
            ch, cl = halves(a, 0)
            sh, sl = halves(a, 1)
            from_cos = mm3(ch, cl, tch[...], tcl[...])
            from_sin = mm3(sh, sl, tsh[...], tsl[...])
            eu, ov = from_cos[:, 0:HALF], from_cos[:, HALF:]
            ou, ev = from_sin[:, 0:HALF], from_sin[:, HALF:]
            hist_u[k, rows, 0:HALF] = eu
            hist_u[k, rows, HALF:] = ou
            hist_v[k, rows, 0:HALF] = ev
            hist_v[k, rows, HALF:] = ov
            speed_e = sw + advection_gain * eu
            speed_o = advection_gain * ou
            ge = -(speed_e * ev + speed_o * ov)
            go = -(speed_e * ov + speed_o * ev)
            geh, gel = split(ge)
            goh, gol = split(go)
            pc, ps = fold(mm3(geh, gel, bch[0:HALF, :], bcl[0:HALF, :]), mm3(goh, gol, bsh[0:HALF, :], bsl[0:HALF, :]))
            new_c = decay * state[rows, 0:HALF] + pc + PROFILE[a] * body_c + rad[a, :, 0:HALF]
            new_s = decay * state[rows, HALF:] + ps + PROFILE[a] * body_s + rad[a, :, HALF:]
            if a > 0:
                before = slice((a - 1) * NR, a * NR)
                new_c = new_c + reach * state[before, 0:HALF]
                new_s = new_s + reach * state[before, HALF:]
            state[rows, 0:HALF] = new_c
            state[rows, HALF:] = new_s
            store_split(a)

    tall = lax.broadcasted_iota(jnp.int32, (NT, OBS), 0)
    short = lax.broadcasted_iota(jnp.int32, (AX * QR, OBS), 0)

    def sample(k):
        held = k % STEPS

        def one(b, total):
            block = 2 * b + core
            cell = obs_i[pl.ds(b * STEPS + k - 1, 1), :]
            value = obs_v[pl.ds(b * STEPS + k - 1, 1), :]
            column = cell & (NT - 1)
            column = jnp.where(column < HALF, column, NT + HALF - 1 - column)
            which = (tall == column).astype(jnp.float32).astype(jnp.bfloat16)
            at_row = short == (cell >> 9)
            parts = []
            for a in range(AX):
                spot = pl.multiple_of(a * NR + block * QR, 8)
                eu = hist_u[held, pl.ds(spot, QR), 0:HALF]
                ou = hist_u[held, pl.ds(spot, QR), HALF:]
                parts.append(jnp.concatenate([eu + ou, eu - ou], 1))
            uh, ul = split(jnp.concatenate(parts, 0))
            picked = mm(uh, which) + mm(ul, which)
            miss = jnp.sum(jnp.where(at_row, picked, 0.0), 0, keepdims=True) - value
            eh, el = split(jnp.where(at_row, miss, 0.0))
            dims = (((1,), (1,)), ((), ()))
            back = lax.dot_general(eh, which, dims, preferred_element_type=jnp.float32)
            back = back + lax.dot_general(el, which, dims, preferred_element_type=jnp.float32)
            plus, minus = back[:, 0:HALF], back[:, HALF:]
            grow = 0.5 / step_size
            for a in range(AX):
                spot = pl.multiple_of(a * NR + block * QR, 8)
                own = slice(a * QR, (a + 1) * QR)
                inject[k - 1, pl.ds(spot, QR), 0:HALF] = grow * (plus[own] + minus[own])
                inject[k - 1, pl.ds(spot, QR), HALF:] = grow * (plus[own] - minus[own])
            return total + miss * miss

        msum[...] += lax.fori_loop(0, BLOCKS // 2, one, jnp.zeros((1, OBS), jnp.float32), unroll=4)

    for a in range(AX):
        store_split(a)
    forward_step(0)

    def onward(k, carry):
        forward_step(k)
        sample(k)
        return carry

    lax.fori_loop(1, STEPS, onward, 0)
    for a in range(AX):
        rows = slice(a * NR, (a + 1) * NR)
        eu, ou = expand_u(a)
        hist_u[0, rows, 0:HALF] = eu
        hist_u[0, rows, HALF:] = ou
    sample(STEPS)
    miss_out[...] = jnp.broadcast_to(jnp.sum(msum[...], 1, keepdims=True), miss_out.shape)

    mine = pl.multiple_of(me * QR, 8)
    for a in range(AX):
        spot = pl.multiple_of(a * NR + mine, 8)
        cos_part = state[pl.ds(spot, QR), 0:HALF]
        sin_part = state[pl.ds(spot, QR), HALF:]
        plain_c = cos_part * lane(4) + sin_part * lane(5)
        plain_s = pltpu.roll(cos_part * lane(6) + sin_part * lane(7), 63, 1)
        at_lane = lax.broadcasted_iota(jnp.int32, (QR, 128), 1)
        final_out[a, :, 0:128] = plain_c[:, 0:128]
        final_out[a, :, 128:256] = jnp.where(at_lane < 64, plain_c[:, 128:], plain_s[:, 0:128])
        final_out[a, :, 256:384] = plain_s[:, 128:]

    chip = pl.multiple_of((me - core) * QR, 8)

    def gather_gradient(k):
        wc = jnp.zeros((2 * QR, HALF), jnp.float32)
        ws = wc
        for a in range(AX):
            spot = pl.multiple_of(a * NR + chip, 8)
            wc = wc + (step_size * PROFILE[a]) * state[pl.ds(spot, 2 * QR), 0:HALF]
            ws = ws + (step_size * PROFILE[a]) * state[pl.ds(spot, 2 * QR), HALF:]
        gsum[:, 0:HALF] += turns[k, 4:5, :] * wc + turns[k, 5:6, :] * ws
        gsum[:, HALF:] += turns[k, 6:7, :] * wc + turns[k, 7:8, :] * ws

    for a in range(AX):
        rows = slice(a * NR, (a + 1) * NR)
        eh, el = split(inject[STEPS - 1, rows, 0:HALF])
        oh, ol = split(inject[STEPS - 1, rows, HALF:])
        lc, ls = fold(mm3(eh, el, bch[0:HALF, :], bcl[0:HALF, :]), mm3(oh, ol, bsh[0:HALF, :], bsl[0:HALF, :]))
        state[rows, 0:HALF] = lc
        state[rows, HALF:] = ls
        store_split(a)

    def backward_step(k):
        couple(rtl)
        sw = jnp.concatenate([swirl[...], swirl[...]], 1)
        for a in range(AX):
            rows = slice(a * NR, (a + 1) * NR)
            eq, oq = expand_u(a)
            eu, ou = hist_u[k, rows, 0:HALF], hist_u[k, rows, HALF:]
            ev, ov = hist_v[k, rows, 0:HALF], hist_v[k, rows, HALF:]
            speed_e = sw + advection_gain * eu
            speed_o = advection_gain * ou
            tve = -(speed_e * eq + speed_o * oq)
            tvo = -(speed_e * oq + speed_o * eq)
            eq = advection_gain * eq
            oq = advection_gain * oq
            tue = inject[k - 1, rows, 0:HALF] - (ev * eq + ov * oq)
            tuo = inject[k - 1, rows, HALF:] - (ev * oq + ov * eq)
            ueh, uel = split(tue)
            uoh, uol = split(tuo)
            veh, vel = split(tve)
            voh, vol = split(tvo)
            pc = mm3(ueh, uel, bch[0:HALF, :], bcl[0:HALF, :]) + mm3(voh, vol, bch[HALF:, :], bcl[HALF:, :])
            ps = mm3(uoh, uol, bsh[0:HALF, :], bsl[0:HALF, :]) + mm3(veh, vel, bsh[HALF:, :], bsl[HALF:, :])
            pc, ps = fold(pc, ps)
            new_c = decay * state[rows, 0:HALF] + pc + rad[a, :, 0:HALF]
            new_s = decay * state[rows, HALF:] + ps + rad[a, :, HALF:]
            if a < AX - 1:
                after = slice((a + 1) * NR, (a + 2) * NR)
                new_c = new_c + reach * state[after, 0:HALF]
                new_s = new_s + reach * state[after, HALF:]
            state[rows, 0:HALF] = new_c
            state[rows, HALF:] = new_s
            store_split(a)

    def inward(i, carry):
        k = STEPS - 1 - i
        gather_gradient(k)
        backward_step(k)
        return carry

    lax.fori_loop(0, STEPS - 1, inward, 0)
    gather_gradient(0)
    gh, gl = split(gsum[...])
    grad_out[...] = mm3(gh, gl, gth[...], gtl[...])


def window_step(place, turns, radial_op, pieces):
    from_cos, from_sin = half_tables()
    whole = whole_table()
    tables = []
    for table in (from_cos, from_sin, 2.0 * step_size * from_cos.T, 2.0 * step_size * from_sin.T, whole.T, whole):
        tables += [jnp.asarray(part) for part in split_np(table)]
    operands = [place, turns, jnp.asarray(lane_rows()), radial_op, *tables, *pieces]
    vmem = pl.BlockSpec(memory_space=pltpu.VMEM)
    f32, bf16 = jnp.float32, jnp.bfloat16
    return pl.pallas_call(
        kernel,
        out_shape=(
            jax.ShapeDtypeStruct((AX, QR, 384), f32),
            jax.ShapeDtypeStruct((2 * QR, NT), f32),
            jax.ShapeDtypeStruct((8, 128), f32),
        ),
        in_specs=[pl.BlockSpec(memory_space=pltpu.SMEM)] + [vmem] * (len(operands) - 1),
        out_specs=(vmem, vmem, vmem),
        scratch_shapes=[
            pltpu.VMEM((ROWS, COEF), f32),
            pltpu.VMEM((AX, 3 * NR, COEF), bf16),
            pltpu.VMEM((AX, NR, COEF), f32),
            pltpu.VMEM((STEPS, ROWS, COEF), f32),
            pltpu.VMEM((STEPS, ROWS, COEF), f32),
            pltpu.VMEM((STEPS, ROWS, COEF), f32),
            pltpu.VMEM((NR, 3 * NR), bf16),
            pltpu.VMEM((NR, 3 * NR), bf16),
            pltpu.VMEM((NR, 128), f32),
            pltpu.VMEM((NR, COEF), f32),
            pltpu.VMEM((BLOCKS // 2 * STEPS, OBS), jnp.int32),
            pltpu.VMEM((BLOCKS // 2 * STEPS, OBS), f32),
            pltpu.VMEM((2 * QR, COEF), f32),
            pltpu.VMEM((1, OBS), f32),
        ],
        compiler_params=pltpu.CompilerParams(vmem_limit_bytes=VMEM_LIMIT),
    )(*operands)


def per_device(first_guess, forcing, swirl, radial_op, obs_index, obs_value, start_step):
    me = lax.axis_index("space")

    def space_swap(x, bits):
        return lax.ppermute(x, "space", [(i, i ^ bits) for i in range(BLOCKS)])

    def space_turn(x, d):
        return lax.ppermute(x, "space", [(i, i // 8 * 8 + (i + 2 * d) % 8) for i in range(BLOCKS)])

    def win_send(x, where):
        return lax.ppermute(x, "win", [(i, where(i)) for i in range(16)])

    extra = jnp.concatenate(
        [
            obs_index[0].astype(jnp.float32),
            obs_value[0],
            jnp.pad(swirl[None, :], ((0, 7), (0, OBS - QR))),
        ],
        0,
    )
    message = jnp.concatenate([first_guess[0, 0], first_guess[0, 1], forcing, extra], 1)
    other_x = space_swap(message, 8)
    both = jnp.concatenate([message, other_x], 0)
    pieces = [message, other_x] + [space_turn(both, d) for d in (1, 2, 3)]
    pieces += [space_swap(piece, 1) for piece in pieces]

    turns = turn_tables(start_step[0])
    final, grad, misses = window_step(me.astype(jnp.int32).reshape(1), turns, radial_op, pieces)

    core = me % 2
    for_other = lax.dynamic_slice_in_dim(grad, (1 - core) * QR, QR, 0)
    own = lax.dynamic_slice_in_dim(grad, core * QR, QR, 0)
    misfit = (misses + space_swap(misses, 1))[0, 0:1] * (0.5 / (STEPS * BLOCKS * OBS))
    total = own + space_swap(for_other, 1)
    near = [win_send(total, lambda i, f=f: i ^ f) for f in (1, 2, 3)]
    total = total + near[0] + near[1] + near[2]
    far = [win_send(total, lambda i, d=d: (i + 2 * d) % 16) for d in (2, 4, 6)]
    total = total + far[0] + far[1] + far[2]
    return final[None], misfit, total


def solution(mesh):
    return jax.shard_map(
        per_device,
        mesh=mesh,
        in_specs=(
            P("win", None, "space", None),
            P("space", None),
            P("space"),
            P(),
            P("win", None, "space"),
            P("win", None, "space"),
            P("win"),
        ),
        out_specs=(P("win", None, "space", None), P("win"), P("space", None)),
        check_vma=False,
    )
```

time: 719 us -> 139 us (0.19); the launches traced: 706 us -> 137 us
  blocking collectives: 133 us -> 0 us
  local copies, waits for them, and re-layouts: 125 us -> 4.56 us
  waiting for transfers between devices: 141 us -> 22.4 us
  matrix products: 115 us -> 0 us
  starting transfers between devices: 115 us -> 22.9 us
  Pallas kernels: 0 us -> 83.2 us
  other arithmetic: 63.8 us -> 1.08 us
  between operations: 13.1 us -> 3.27 us
    all_to_all x27 -> x0, waiting for transfers between devices: 141 us -> none  [the longest x15 85.4 us: radial(): lax.all_to_all(coupled, 'space', split_axis=1, concat_axis=2, tiled=True)]
    all_to_all x27 -> x0, starting transfers between devices: 115 us -> none  [the longest x15 68.5 us: radial(): lax.all_to_all(coupled, 'space', split_axis=1, concat_axis=2, tiled=True)]
    dot_general x56 -> x0, matrix products: 115 us -> none  [the longest x9 42.7 us: project(): return jnp.einsum('art,kt->ark', source_field, synthesis, precision=highest)]
    psum x2 -> x0, blocking collectives: 102 us -> none  [the longest x1 63.4 us: per_device(): forcing_gradient = lax.psum(gradient, 'win')]
    pallas_call x0 -> x1, Pallas kernels: none -> 83.2 us  [window_step(): pl.pallas_call(kernel, out_shape=(jax.ShapeDtypeStruct((AX, QR, 384), f32...]
    unnamed x359 -> x32, local copies, waits for them, and re-layouts: 61.4 us -> 1.63 us
    all_to_all x3 -> x0, blocking collectives: 31.2 us -> none  [radial(): lax.all_to_all(source_field, 'space', split_axis=2, concat_axis=1, tiled=...]
    all_to_all x30 -> x0, other arithmetic: 27.6 us -> none  [the longest x15 13.8 us: radial(): lax.all_to_all(source_field, 'space', split_axis=2, concat_axis=1, tiled=...]
  transfers between devices with their start and end apart: 27 -> 17, of which waited for: 24 -> 10; matrix products, arithmetic and copies ran while one was open for 8% -> 1% of each run, Pallas kernels for 0% -> 0%
where the time goes in v1:
time: 139 us; the launch traced here: 137 us
  Pallas kernels  83.2 us (60%)
  starting transfers between devices  22.9 us (16%)
  waiting for transfers between devices  22.4 us (16%)
  local copies, waits for them, and re-layouts  4.56 us (3%)
  between operations  3.27 us (2%)
    pallas_call x1, Pallas kernels, window_step(): pl.pallas_call(kernel, out_shape=(jax.ShapeDtypeStruct((AX, QR, 384), f32...  83.2 us
    ppermute x6, starting transfers between devices, win_send(): return lax.ppermute(x, 'win', [(i, where(i)) for i in range(16)])  14.1 us
    ppermute x3, waiting for transfers between devices, space_turn(): lax.ppermute(x, 'space', [(i, i // 8 * 8 + (i + 2 * d) % 8) for i in rang...  10.1 us
    ppermute x8, waiting for transfers between devices, space_swap(): return lax.ppermute(x, 'space', [(i, i ^ bits) for i in range(BLOCKS)])  7.69 us
    ppermute x3, starting transfers between devices, space_turn(): lax.ppermute(x, 'space', [(i, i // 8 * 8 + (i + 2 * d) % 8) for i in rang...  5.9 us
    ppermute x6, waiting for transfers between devices, win_send(): return lax.ppermute(x, 'win', [(i, where(i)) for i in range(16)])  4.58 us
    ppermute x8, starting transfers between devices, space_swap(): return lax.ppermute(x, 'space', [(i, i ^ bits) for i in range(BLOCKS)])  2.97 us
  transfers between devices with their start and end apart: 17, of which 10 were waited for; matrix products, arithmetic and copies ran while one was open for 1% of the time, Pallas kernels for 0%

profile of v1, /device:TPU:2, one launch (start us, length us, event | category | flops | bytes accessed | tf_op | source)
XLA Modules:
  0.0 137.5 jit_solution(5517780035176262633)
XLA Ops:
  0.7 0.8 slice_bitcast_fusion.1
  1.5 0.6 copy-done.15
  2.2 2.2 %collective-permute-start = (f32[24,1536]{1,0:T(8,128)S(1)}, f32[24,1536]{1,0:T(8,128)S(1)}, u32[]{:S(2)}, u32[]{:S(2)}) collective-permute-start(f32[24,1536]{1,0:T(8,128)S(1)} %maximum_maximum_fusion.p0), channel_id=1, source_target_pairs={{0,8},{1,9},{2,10},{3,11},{4,12},{5,13},{6,14},{7,15},{8,0},{9,1},... | collective-permute-start | bytes 442376 | tf_op jit(solution)/shard_map/ppermute | solution.py:420
  4.4 5.0 %collective-permute-done.p1 = f32[24,1536]{1,0:T(8,128)S(1)} collective-permute-done((f32[24,1536]{1,0:T(8,128)S(1)}, f32[24,1536]{1,0:T(8,128)S(1)}, u32[]{:S(2)}, u32[]{:S(2)}) %collective-permute-start) | collective-permute-done | bytes 147488 | tf_op jit(solution)/shard_map/ppermute | solution.py:420
  9.4 1.7 %collective-permute-start.1 = (f32[48,1536]{1,0:T(8,128)S(1)}, f32[48,1536]{1,0:T(8,128)S(1)}, u32[]{:S(2)}, u32[]{:S(2)}) collective-permute-start(f32[48,1536]{1,0:T(8,128)S(1)} %pad_maximum_fusion), channel_id=1, source_target_pairs={{0,2},{1,3},{2,4},{3,5},{4,6},{5,7},{6,0},{7,1},{8,10},{9,11},{10,... | collective-permute-start | bytes 884744 | tf_op jit(solution)/shard_map/ppermute | solution.py:423
  11.1 2.9 %collective-permute-start.2 = (f32[48,1536]{1,0:T(8,128)S(1)}, f32[48,1536]{1,0:T(8,128)S(1)}, u32[]{:S(2)}, u32[]{:S(2)}) collective-permute-start(f32[48,1536]{1,0:T(8,128)S(1)} %pad_maximum_fusion), channel_id=1, source_target_pairs={{0,4},{1,5},{2,6},{3,7},{4,0},{5,1},{6,2},{7,3},{8,12},{9,13},{10,... | collective-permute-start | bytes 884744 | tf_op jit(solution)/shard_map/ppermute | solution.py:423
  14.0 1.3 collective-permute-start.3
  16.0 3.5 %collective-permute-done.1.p2 = f32[48,1536]{1,0:T(8,128)S(1)} collective-permute-done((f32[48,1536]{1,0:T(8,128)S(1)}, f32[48,1536]{1,0:T(8,128)S(1)}, u32[]{:S(2)}, u32[]{:S(2)}) %collective-permute-start.1) | collective-permute-done | bytes 294944 | tf_op jit(solution)/shard_map/ppermute | solution.py:423
  19.5 6.6 %collective-permute-done.2.p3 = f32[48,1536]{1,0:T(8,128)S(1)} collective-permute-done((f32[48,1536]{1,0:T(8,128)S(1)}, f32[48,1536]{1,0:T(8,128)S(1)}, u32[]{:S(2)}, u32[]{:S(2)}) %collective-permute-start.2) | collective-permute-done | bytes 294944 | tf_op jit(solution)/shard_map/ppermute | solution.py:423
  26.2 0.5 collective-permute-start.8
  26.8 0.4 fusion.5
  27.2 0.7 stack.2.turns
  27.9 0.5 collective-permute-done.5.q1
  28.6 0.5 copy-done.10
  29.0 0.1 copy-done.5
  29.1 0.1 copy-done.6
  29.3 83.2 %shard_map.211 = (f32[2,24,384]{2,1,0:T(8,128)}, f32[48,512]{1,0:T(8,128)}, f32[8,128]{1,0:T(8,128)}) custom-call(s32[1]{0:T(128)} %bitcast.place, f32[8,8,256]{2,1,0:T(8,128)} %stack.2.turns, f32[16,256]{1,0:T(8,128)} %constant.93.clone.lanes, f32[384,384]{1,0:T(8,128)} %radial_op.1, bf16[256,512]{1,0:T(8,128)(2,1)} %constant.81.clone.tch, ...), custom_call_target="tpu_custom_call" | custom-call | tf_op jit(solution)/shard_map/pallas_call | solution.py:387
  112.5 0.9 constant_dynamic-slice_fusion
  113.5 1.1 collective-permute-done.10
  114.7 0.6 collective-permute-start.11
  115.3 1.9 %collective-permute-start.12 = (f32[24,512]{1,0:T(8,128)S(1)}, f32[24,512]{1,0:T(8,128)S(1)}, u32[]{:S(2)}, u32[]{:S(2)}) collective-permute-start(f32[24,512]{1,0:T(8,128)S(1)} %dynamic-slice_add_fusion), channel_id=1, source_target_pairs={{0,32},{16,48},{32,0},{48,16},{64,96},{80,112},{96,64},{112,80},{1... | collective-permute-start | bytes 147464 | tf_op jit(solution)/shard_map/ppermute | solution.py:426
  117.2 1.0 collective-permute-start.13
  118.2 0.6 collective-permute-done.11
  118.8 0.5 collective-permute-done.12
  119.4 2.8 %collective-permute-done.13 = f32[24,512]{1,0:T(8,128)S(1)} collective-permute-done((f32[24,512]{1,0:T(8,128)S(1)}, f32[24,512]{1,0:T(8,128)S(1)}, u32[]{:S(2)}, u32[]{:S(2)}) %collective-permute-start.13) | collective-permute-done | bytes 49184 | tf_op jit(solution)/shard_map/ppermute | solution.py:426
  122.2 3.3 %collective-permute-start.14 = (f32[24,512]{1,0:T(8,128)S(1)}, f32[24,512]{1,0:T(8,128)S(1)}, u32[]{:S(2)}, u32[]{:S(2)}) collective-permute-start(f32[24,512]{1,0:T(8,128)S(1)} %add_add_fusion.1), channel_id=1, source_target_pairs={{0,64},{16,80},{32,96},{48,112},{64,128},{80,144},{96,160},{112,17... | collective-permute-start | bytes 147464 | tf_op jit(solution)/shard_map/ppermute | solution.py:426
  125.5 4.5 %collective-permute-start.15 = (f32[24,512]{1,0:T(8,128)S(1)}, f32[24,512]{1,0:T(8,128)S(1)}, u32[]{:S(2)}, u32[]{:S(2)}) collective-permute-start(f32[24,512]{1,0:T(8,128)S(1)} %add_add_fusion.1), channel_id=1, source_target_pairs={{0,128},{16,144},{32,160},{48,176},{64,192},{80,208},{96,224},{112... | collective-permute-start | bytes 147464 | tf_op jit(solution)/shard_map/ppermute | solution.py:426
  130.0 2.7 %collective-permute-start.16 = (f32[24,512]{1,0:T(8,128)S(1)}, f32[24,512]{1,0:T(8,128)S(1)}, u32[]{:S(2)}, u32[]{:S(2)}) collective-permute-start(f32[24,512]{1,0:T(8,128)S(1)} %add_add_fusion.1), channel_id=1, source_target_pairs={{0,192},{16,208},{32,224},{48,240},{64,0},{80,16},{96,32},{112,48}... | collective-permute-start | bytes 147464 | tf_op jit(solution)/shard_map/ppermute | solution.py:426
  132.7 1.2 collective-permute-done.9
  133.9 0.5 slice.11
  135.1 0.6 collective-permute-done.16
  135.7 0.6 add_add_fusion
  (50 shorter events, 0.7 us)
Async XLA Ops:
  0.6 0.8 copy-start.13
  0.6 1.5 %copy-start.8 = (f32[24,512]{1,0:T(8,128)S(1)}, f32[24,512]{1,0:T(8,128)}, u32[]{:S(2)}) copy-start(f32[24,512]{1,0:T(8,128)} %param.21) | copy-start | bytes 147460
  1.5 0.7 copy-start.15
  1.5 0.7 copy-start.12
  2.2 13.1 %copy-start = (f32[24,1536]{1,0:T(8,128)}, f32[24,1536]{1,0:T(8,128)S(1)}, u32[]{:S(2)}) copy-start(f32[24,1536]{1,0:T(8,128)S(1)} %maximum_maximum_fusion.p0) | copy-start | bytes 442372
  2.2 7.2 %collective-permute-start = (f32[24,1536]{1,0:T(8,128)S(1)}, f32[24,1536]{1,0:T(8,128)S(1)}, u32[]{:S(2)}, u32[]{:S(2)}) collective-permute-start(f32[24,1536]{1,0:T(8,128)S(1)} %maximum_maximum_fusion.p0), channel_id=1, source_target_pairs={{0,8},{1,9},{2,10},{3,11},{4,12},{5,13},{6,14},{7,15},{8,0},{9,1},... | collective-permute-start | bytes 442376 | tf_op jit(solution)/shard_map/ppermute | solution.py:420
  9.4 17.3 %copy-start.1 = (f32[24,1536]{1,0:T(8,128)}, f32[24,1536]{1,0:T(8,128)S(1)}, u32[]{:S(2)}) copy-start(f32[24,1536]{1,0:T(8,128)S(1)} %collective-permute-done.p1) | copy-start | bytes 442372
  9.4 10.1 %collective-permute-start.1 = (f32[48,1536]{1,0:T(8,128)S(1)}, f32[48,1536]{1,0:T(8,128)S(1)}, u32[]{:S(2)}, u32[]{:S(2)}) collective-permute-start(f32[48,1536]{1,0:T(8,128)S(1)} %pad_maximum_fusion), channel_id=1, source_target_pairs={{0,2},{1,3},{2,4},{3,5},{4,6},{5,7},{6,0},{7,1},{8,10},{9,11},{10,... | collective-permute-start | bytes 884744 | tf_op jit(solution)/shard_map/ppermute | solution.py:423
  11.1 15.1 %collective-permute-start.2 = (f32[48,1536]{1,0:T(8,128)S(1)}, f32[48,1536]{1,0:T(8,128)S(1)}, u32[]{:S(2)}, u32[]{:S(2)}) collective-permute-start(f32[48,1536]{1,0:T(8,128)S(1)} %pad_maximum_fusion), channel_id=1, source_target_pairs={{0,4},{1,5},{2,6},{3,7},{4,0},{5,1},{6,2},{7,3},{8,12},{9,13},{10,... | collective-permute-start | bytes 884744 | tf_op jit(solution)/shard_map/ppermute | solution.py:423
  14.0 12.2 %collective-permute-start.3 = (f32[48,1536]{1,0:T(8,128)S(1)}, f32[48,1536]{1,0:T(8,128)S(1)}, u32[]{:S(2)}, u32[]{:S(2)}) collective-permute-start(f32[48,1536]{1,0:T(8,128)S(1)} %pad_maximum_fusion), channel_id=1, source_target_pairs={{0,6},{1,7},{2,0},{3,1},{4,2},{5,3},{6,4},{7,5},{8,14},{9,15},{10,... | collective-permute-start | bytes 884744 | tf_op jit(solution)/shard_map/ppermute | solution.py:423
  15.3 12.6 %collective-permute-start.4 = (f32[24,1536]{1,0:T(8,128)S(1)}, f32[24,1536]{1,0:T(8,128)S(1)}, u32[]{:S(2)}, u32[]{:S(2)}) collective-permute-start(f32[24,1536]{1,0:T(8,128)S(1)} %maximum_maximum_fusion.p0), channel_id=1, source_target_pairs={{0,1},{1,0},{2,3},{3,2},{4,5},{5,4},{6,7},{7,6},{8,9},{9,8},{10,11... | collective-permute-start | bytes 442376 | tf_op jit(solution)/shard_map/ppermute | solution.py:420
  19.5 8.9 %copy-start.2 = (f32[48,1536]{1,0:T(8,128)}, f32[48,1536]{1,0:T(8,128)S(1)}, u32[]{:S(2)}) copy-start(f32[48,1536]{1,0:T(8,128)S(1)} %collective-permute-done.1.p2) | copy-start | bytes 884740
  19.5 8.8 %collective-permute-start.6 = (f32[48,1536]{1,0:T(8,128)S(1)}, f32[48,1536]{1,0:T(8,128)S(1)}, u32[]{:S(2)}, u32[]{:S(2)}) collective-permute-start(f32[48,1536]{1,0:T(8,128)S(1)} %collective-permute-done.1.p2), channel_id=1, source_target_pairs={{0,1},{1,0},{2,3},{3,2},{4,5},{5,4},{6,7},{7,6},{8,9},{9,8},{10,11... | collective-permute-start | bytes 884744 | tf_op jit(solution)/shard_map/ppermute | solution.py:420
  26.1 2.3 %copy-start.3 = (f32[48,1536]{1,0:T(8,128)}, f32[48,1536]{1,0:T(8,128)S(1)}, u32[]{:S(2)}) copy-start(f32[48,1536]{1,0:T(8,128)S(1)} %collective-permute-done.2.p3) | copy-start | bytes 884740
  26.1 2.2 %collective-permute-start.7 = (f32[48,1536]{1,0:T(8,128)S(1)}, f32[48,1536]{1,0:T(8,128)S(1)}, u32[]{:S(2)}, u32[]{:S(2)}) collective-permute-start(f32[48,1536]{1,0:T(8,128)S(1)} %collective-permute-done.2.p3), channel_id=1, source_target_pairs={{0,1},{1,0},{2,3},{3,2},{4,5},{5,4},{6,7},{7,6},{8,9},{9,8},{10,11... | collective-permute-start | bytes 884744 | tf_op jit(solution)/shard_map/ppermute | solution.py:420
  26.2 2.3 %copy-start.4 = (f32[48,1536]{1,0:T(8,128)}, f32[48,1536]{1,0:T(8,128)S(1)}, u32[]{:S(2)}) copy-start(f32[48,1536]{1,0:T(8,128)S(1)} %collective-permute-done.3.p4) | copy-start | bytes 884740
  26.2 2.2 %collective-permute-start.8 = (f32[48,1536]{1,0:T(8,128)S(1)}, f32[48,1536]{1,0:T(8,128)S(1)}, u32[]{:S(2)}, u32[]{:S(2)}) collective-permute-start(f32[48,1536]{1,0:T(8,128)S(1)} %collective-permute-done.3.p4), channel_id=1, source_target_pairs={{0,1},{1,0},{2,3},{3,2},{4,5},{5,4},{6,7},{7,6},{8,9},{9,8},{10,11... | collective-permute-start | bytes 884744 | tf_op jit(solution)/shard_map/ppermute | solution.py:420
  26.7 1.7 %collective-permute-start.5 = (f32[24,1536]{1,0:T(8,128)S(1)}, f32[24,1536]{1,0:T(8,128)S(1)}, u32[]{:S(2)}, u32[]{:S(2)}) collective-permute-start(f32[24,1536]{1,0:T(8,128)S(1)} %collective-permute-done.p1), channel_id=1, source_target_pairs={{0,1},{1,0},{2,3},{3,2},{4,5},{5,4},{6,7},{7,6},{8,9},{9,8},{10,11... | collective-permute-start | bytes 442376 | tf_op jit(solution)/shard_map/ppermute | solution.py:420
  27.9 0.7 copy-start.9
  28.4 0.8 copy-start.5
  28.4 0.9 copy-start.6
  28.4 0.9 copy-start.7
  112.5 2.1 %copy-start.11 = (f32[48,512]{1,0:T(8,128)S(1)}, f32[48,512]{1,0:T(8,128)}, u32[]{:S(2)}) copy-start(f32[48,512]{1,0:T(8,128)} %get-tuple-element.8) | copy-start | bytes 294916
  113.4 1.2 collective-permute-start.10
  114.6 18.1 %copy-start.14 = (f32[8,128]{1,0:T(8,128)S(1)}, f32[8,128]{1,0:T(8,128)}, u32[]{:S(2)}) copy-start(f32[8,128]{1,0:T(8,128)} %get-tuple-element.7) | copy-start | bytes 12292
  114.7 4.2 %collective-permute-start.11 = (f32[24,512]{1,0:T(8,128)S(1)}, f32[24,512]{1,0:T(8,128)S(1)}, u32[]{:S(2)}, u32[]{:S(2)}) collective-permute-start(f32[24,512]{1,0:T(8,128)S(1)} %dynamic-slice_add_fusion), channel_id=1, source_target_pairs={{0,16},{16,0},{32,48},{48,32},{64,80},{80,64},{96,112},{112,96},{1... | collective-permute-start | bytes 147464 | tf_op jit(solution)/shard_map/ppermute | solution.py:426
  115.3 4.1 %collective-permute-start.12 = (f32[24,512]{1,0:T(8,128)S(1)}, f32[24,512]{1,0:T(8,128)S(1)}, u32[]{:S(2)}, u32[]{:S(2)}) collective-permute-start(f32[24,512]{1,0:T(8,128)S(1)} %dynamic-slice_add_fusion), channel_id=1, source_target_pairs={{0,32},{16,48},{32,0},{48,16},{64,96},{80,112},{96,64},{112,80},{1... | collective-permute-start | bytes 147464 | tf_op jit(solution)/shard_map/ppermute | solution.py:426
  117.2 5.0 %collective-permute-start.13 = (f32[24,512]{1,0:T(8,128)S(1)}, f32[24,512]{1,0:T(8,128)S(1)}, u32[]{:S(2)}, u32[]{:S(2)}) collective-permute-start(f32[24,512]{1,0:T(8,128)S(1)} %dynamic-slice_add_fusion), channel_id=1, source_target_pairs={{0,48},{16,32},{32,16},{48,0},{64,112},{80,96},{96,80},{112,64},{1... | collective-permute-start | bytes 147464 | tf_op jit(solution)/shard_map/ppermute | solution.py:426
  122.2 12.8 %collective-permute-start.14 = (f32[24,512]{1,0:T(8,128)S(1)}, f32[24,512]{1,0:T(8,128)S(1)}, u32[]{:S(2)}, u32[]{:S(2)}) collective-permute-start(f32[24,512]{1,0:T(8,128)S(1)} %add_add_fusion.1), channel_id=1, source_target_pairs={{0,64},{16,80},{32,96},{48,112},{64,128},{80,144},{96,160},{112,17... | collective-permute-start | bytes 147464 | tf_op jit(solution)/shard_map/ppermute | solution.py:426
  125.5 9.5 %collective-permute-start.15 = (f32[24,512]{1,0:T(8,128)S(1)}, f32[24,512]{1,0:T(8,128)S(1)}, u32[]{:S(2)}, u32[]{:S(2)}) collective-permute-start(f32[24,512]{1,0:T(8,128)S(1)} %add_add_fusion.1), channel_id=1, source_target_pairs={{0,128},{16,144},{32,160},{48,176},{64,192},{80,208},{96,224},{112... | collective-permute-start | bytes 147464 | tf_op jit(solution)/shard_map/ppermute | solution.py:426
  130.0 5.6 %collective-permute-start.16 = (f32[24,512]{1,0:T(8,128)S(1)}, f32[24,512]{1,0:T(8,128)S(1)}, u32[]{:S(2)}, u32[]{:S(2)}) collective-permute-start(f32[24,512]{1,0:T(8,128)S(1)} %add_add_fusion.1), channel_id=1, source_target_pairs={{0,192},{16,208},{32,224},{48,240},{64,0},{80,16},{96,32},{112,48}... | collective-permute-start | bytes 147464 | tf_op jit(solution)/shard_map/ppermute | solution.py:426
  132.7 1.2 collective-permute-start.9
  (1 other events, 0.7 us)

commit v2 on v1

--- a/solution.py
+++ b/solution.py
@@ -21,6 +21,8 @@
 OBS = 256
 ROWS = AX * NR
 COEF = 2 * HALF
+GROUP = 8
+CHUNK = 384
 VMEM_LIMIT = 60 * 1024 * 1024
 
 step_size = 0.25
@@ -128,7 +130,7 @@
 def kernel(
     place, turns, lanes, radial_op, tch, tcl, tsh, tsl, bch, bcl, bsh, bsl, fth, ftl, gth, gtl,
     p0, p1, p2, p3, p4, q0, q1, q2, q3, q4,
-    final_out, grad_out, miss_out,
+    final_out, keep_out, send_out,
     state, high, rad, hist_u, hist_v, inject, rl, rtl, swirl, forced, obs_i, obs_v, gsum, msum,
 ):
     me = place[0]
@@ -175,7 +177,6 @@
     rl[:, 0:NR], rl[:, NR:2 * NR], rl[:, 2 * NR:] = rh, rlow, rh
     th, tlow = split(scaled.T)
     rtl[:, 0:NR], rtl[:, NR:2 * NR], rtl[:, 2 * NR:] = th, tlow, th
-    inject[...] = jnp.zeros_like(inject)
     gsum[...] = jnp.zeros_like(gsum)
     msum[...] = jnp.zeros_like(msum)
 
@@ -183,41 +184,41 @@
     decay = lane(8)
     reach = step_size * axial_speed
 
-    def store_split(a):
-        h, l = split(state[a * NR:(a + 1) * NR, :])
-        high[a, 0:NR, :] = h
-        high[a, NR:2 * NR, :] = h
-        high[a, 2 * NR:, :] = l
+    def store_split(a, r):
+        h, l = split(state[a * NR + r:a * NR + r + CHUNK, :])
+        high[a, r:r + CHUNK, :] = h
+        high[a, NR + r:NR + r + CHUNK, :] = h
+        high[a, 2 * NR + r:2 * NR + r + CHUNK, :] = l
 
     def couple(operator):
         for a in range(AX):
             rad[a] = mm(operator[...], high[a])
 
-    def halves(a, part):
+    def halves(a, r, part):
         lanes_of = slice(0, HALF) if part == 0 else slice(HALF, COEF)
-        return high[a, 0:NR, lanes_of], high[a, 2 * NR:, lanes_of]
+        return high[a, r:r + CHUNK, lanes_of], high[a, 2 * NR + r:2 * NR + r + CHUNK, lanes_of]
 
     def fold(pc, ps):
         return pc + mark * ps, ps + mark * pc
 
-    def expand_u(a):
-        ch, cl = halves(a, 0)
-        sh, sl = halves(a, 1)
+    def expand_u(a, r):
+        ch, cl = halves(a, r, 0)
+        sh, sl = halves(a, r, 1)
         eu = mm3(ch, cl, tch[:, 0:HALF], tcl[:, 0:HALF])
         ou = mm3(sh, sl, tsh[:, 0:HALF], tsl[:, 0:HALF])
         return eu, ou
 
     def forward_step(k):
-        couple(rl)
-        body_c = turns[k, 0:1, :] * forced[:, 0:HALF] + turns[k, 1:2, :] * forced[:, HALF:COEF]
-        body_s = turns[k, 2:3, :] * forced[:, 0:HALF] + turns[k, 3:4, :] * forced[:, HALF:COEF]
+        expanded = [None, None]
+        fields = [None, None]
+        for a in range(AX - 1, -1, -1):
+            ch, cl = halves(a, 0, 0)
+            sh, sl = halves(a, 0, 1)
+            expanded[a] = (mm3(ch, cl, tch[...], tcl[...]), mm3(sh, sl, tsh[...], tsl[...]))
         sw = jnp.concatenate([swirl[...], swirl[...]], 1)
         for a in range(AX - 1, -1, -1):
             rows = slice(a * NR, (a + 1) * NR)
-            ch, cl = halves(a, 0)
-            sh, sl = halves(a, 1)
-            from_cos = mm3(ch, cl, tch[...], tcl[...])
-            from_sin = mm3(sh, sl, tsh[...], tsl[...])
+            from_cos, from_sin = expanded[a]
             eu, ov = from_cos[:, 0:HALF], from_cos[:, HALF:]
             ou, ev = from_sin[:, 0:HALF], from_sin[:, HALF:]
             hist_u[k, rows, 0:HALF] = eu
@@ -226,61 +227,88 @@
             hist_v[k, rows, HALF:] = ov
             speed_e = sw + advection_gain * eu
             speed_o = advection_gain * ou
-            ge = -(speed_e * ev + speed_o * ov)
-            go = -(speed_e * ov + speed_o * ev)
-            geh, gel = split(ge)
-            goh, gol = split(go)
+            fields[a] = split(-(speed_e * ev + speed_o * ov)) + split(-(speed_e * ov + speed_o * ev))
+            rad[a] = mm(rl[...], high[a])
+        for a in range(AX - 1, -1, -1):
+            rows = slice(a * NR, (a + 1) * NR)
+            geh, gel, goh, gol = fields[a]
             pc, ps = fold(mm3(geh, gel, bch[0:HALF, :], bcl[0:HALF, :]), mm3(goh, gol, bsh[0:HALF, :], bsl[0:HALF, :]))
+            force_c, force_s = forced[:, 0:HALF], forced[:, HALF:COEF]
+            body_c = turns[k, 0:1, :] * force_c + turns[k, 1:2, :] * force_s
+            body_s = turns[k, 2:3, :] * force_c + turns[k, 3:4, :] * force_s
             new_c = decay * state[rows, 0:HALF] + pc + PROFILE[a] * body_c + rad[a, :, 0:HALF]
             new_s = decay * state[rows, HALF:] + ps + PROFILE[a] * body_s + rad[a, :, HALF:]
             if a > 0:
-                before = slice((a - 1) * NR, a * NR)
+                before = slice(rows.start - NR, rows.stop - NR)
                 new_c = new_c + reach * state[before, 0:HALF]
                 new_s = new_s + reach * state[before, HALF:]
             state[rows, 0:HALF] = new_c
             state[rows, HALF:] = new_s
-            store_split(a)
-
-    tall = lax.broadcasted_iota(jnp.int32, (NT, OBS), 0)
+            store_split(a, 0)
+
+    tall = lax.broadcasted_iota(jnp.int32, (HALF, OBS), 0).astype(jnp.float32).astype(jnp.bfloat16)
     short = lax.broadcasted_iota(jnp.int32, (AX * QR, OBS), 0)
+    one_wide = jnp.ones((HALF, OBS), jnp.bfloat16)
+    zero_wide = jnp.zeros((HALF, OBS), jnp.bfloat16)
 
     def sample(k):
         held = k % STEPS
 
-        def one(b, total):
-            block = 2 * b + core
-            cell = obs_i[pl.ds(b * STEPS + k - 1, 1), :]
-            value = obs_v[pl.ds(b * STEPS + k - 1, 1), :]
-            column = cell & (NT - 1)
-            column = jnp.where(column < HALF, column, NT + HALF - 1 - column)
-            which = (tall == column).astype(jnp.float32).astype(jnp.bfloat16)
-            at_row = short == (cell >> 9)
-            parts = []
-            for a in range(AX):
-                spot = pl.multiple_of(a * NR + block * QR, 8)
-                eu = hist_u[held, pl.ds(spot, QR), 0:HALF]
-                ou = hist_u[held, pl.ds(spot, QR), HALF:]
-                parts.append(jnp.concatenate([eu + ou, eu - ou], 1))
-            uh, ul = split(jnp.concatenate(parts, 0))
-            picked = mm(uh, which) + mm(ul, which)
-            miss = jnp.sum(jnp.where(at_row, picked, 0.0), 0, keepdims=True) - value
-            eh, el = split(jnp.where(at_row, miss, 0.0))
-            dims = (((1,), (1,)), ((), ()))
-            back = lax.dot_general(eh, which, dims, preferred_element_type=jnp.float32)
-            back = back + lax.dot_general(el, which, dims, preferred_element_type=jnp.float32)
-            plus, minus = back[:, 0:HALF], back[:, HALF:]
-            grow = 0.5 / step_size
-            for a in range(AX):
-                spot = pl.multiple_of(a * NR + block * QR, 8)
-                own = slice(a * QR, (a + 1) * QR)
-                inject[k - 1, pl.ds(spot, QR), 0:HALF] = grow * (plus[own] + minus[own])
-                inject[k - 1, pl.ds(spot, QR), HALF:] = grow * (plus[own] - minus[own])
-            return total + miss * miss
-
-        msum[...] += lax.fori_loop(0, BLOCKS // 2, one, jnp.zeros((1, OBS), jnp.float32), unroll=4)
+        dims = (((1,), (1,)), ((), ()))
+
+        def group(first_block):
+            blocks = range(first_block, first_block + GROUP)
+            ats, values, whiches, picks = [], [], [], []
+            for b in blocks:
+                block = 2 * b + core
+                cell = obs_i[pl.ds(b * STEPS + k - 1, 1), :]
+                values.append(obs_v[pl.ds(b * STEPS + k - 1, 1), :])
+                column = cell & (NT - 1)
+                in_first = column < HALF
+                first = jnp.where(in_first, column, -1).astype(jnp.float32).astype(jnp.bfloat16)
+                second = jnp.where(in_first, -1, NT - 1 - column).astype(jnp.float32).astype(jnp.bfloat16)
+                which = jnp.concatenate(
+                    [jnp.where(tall == first, one_wide, zero_wide), jnp.where(tall == second, one_wide, zero_wide)], 0
+                )
+                whiches.append(which)
+                ats.append(short == (cell >> 9))
+                parts = []
+                for a in range(AX):
+                    spot = pl.multiple_of(a * NR + block * QR, 8)
+                    eu = hist_u[held, pl.ds(spot, QR), 0:HALF]
+                    ou = hist_u[held, pl.ds(spot, QR), HALF:]
+                    parts.append(jnp.concatenate([eu + ou, eu - ou], 1))
+                uh, ul = split(jnp.concatenate(parts, 0))
+                picks.append(mm(jnp.concatenate([uh, ul], 0), which))
+            errors, total = [], 0.0
+            for at_row, value, picked in zip(ats, values, picks):
+                picked = picked[0:AX * QR] + picked[AX * QR:]
+                miss = jnp.sum(jnp.where(at_row, picked, 0.0), 0, keepdims=True) - value
+                total = total + miss * miss
+                eh, el = split(jnp.where(at_row, miss, 0.0))
+                errors.append(jnp.concatenate([eh, el], 0))
+            backs = [
+                lax.dot_general(error, which, dims, preferred_element_type=jnp.float32)
+                for error, which in zip(errors, whiches)
+            ]
+            for b, back in zip(blocks, backs):
+                back = (0.5 / step_size) * (back[0:AX * QR] + back[AX * QR:])
+                plus, minus = back[:, 0:HALF], back[:, HALF:]
+                for a in range(AX):
+                    spot = pl.multiple_of(a * NR + (2 * b + core) * QR, 8)
+                    idle = pl.multiple_of(a * NR + (2 * b + 1 - core) * QR, 8)
+                    own = slice(a * QR, (a + 1) * QR)
+                    inject[k - 1, pl.ds(spot, QR), 0:HALF] = plus[own] + minus[own]
+                    inject[k - 1, pl.ds(spot, QR), HALF:] = plus[own] - minus[own]
+                    inject[k - 1, pl.ds(idle, QR), :] = jnp.zeros((QR, COEF), jnp.float32)
+            return total
+
+        for first_block in range(0, BLOCKS // 2, GROUP):
+            msum[...] += group(first_block)
 
     for a in range(AX):
-        store_split(a)
+        for r in range(0, NR, CHUNK):
+            store_split(a, r)
     forward_step(0)
 
     def onward(k, carry):
@@ -290,12 +318,13 @@
 
     lax.fori_loop(1, STEPS, onward, 0)
     for a in range(AX):
-        rows = slice(a * NR, (a + 1) * NR)
-        eu, ou = expand_u(a)
-        hist_u[0, rows, 0:HALF] = eu
-        hist_u[0, rows, HALF:] = ou
+        for r in range(0, NR, CHUNK):
+            rows = slice(a * NR + r, a * NR + r + CHUNK)
+            hist_u[0, rows, 0:HALF], hist_u[0, rows, HALF:] = expand_u(a, r)
     sample(STEPS)
-    miss_out[...] = jnp.broadcast_to(jnp.sum(msum[...], 1, keepdims=True), miss_out.shape)
+    missed = jnp.broadcast_to(jnp.sum(msum[...], 1, keepdims=True), (8, NT))
+    keep_out[QR:, :] = missed
+    send_out[QR:, :] = missed
 
     mine = pl.multiple_of(me * QR, 8)
     for a in range(AX):
@@ -309,59 +338,78 @@
         final_out[a, :, 128:256] = jnp.where(at_lane < 64, plain_c[:, 128:], plain_s[:, 0:128])
         final_out[a, :, 256:384] = plain_s[:, 128:]
 
-    chip = pl.multiple_of((me - core) * QR, 8)
+    chip = pl.multiple_of((me - core) * QR, 16)
 
     def gather_gradient(k):
         wc = jnp.zeros((2 * QR, HALF), jnp.float32)
         ws = wc
         for a in range(AX):
-            spot = pl.multiple_of(a * NR + chip, 8)
+            spot = pl.multiple_of(a * NR + chip, 16)
             wc = wc + (step_size * PROFILE[a]) * state[pl.ds(spot, 2 * QR), 0:HALF]
             ws = ws + (step_size * PROFILE[a]) * state[pl.ds(spot, 2 * QR), HALF:]
         gsum[:, 0:HALF] += turns[k, 4:5, :] * wc + turns[k, 5:6, :] * ws
         gsum[:, HALF:] += turns[k, 6:7, :] * wc + turns[k, 7:8, :] * ws
 
     for a in range(AX):
-        rows = slice(a * NR, (a + 1) * NR)
-        eh, el = split(inject[STEPS - 1, rows, 0:HALF])
-        oh, ol = split(inject[STEPS - 1, rows, HALF:])
-        lc, ls = fold(mm3(eh, el, bch[0:HALF, :], bcl[0:HALF, :]), mm3(oh, ol, bsh[0:HALF, :], bsl[0:HALF, :]))
-        state[rows, 0:HALF] = lc
-        state[rows, HALF:] = ls
-        store_split(a)
+        for r in range(0, NR, CHUNK):
+            rows = slice(a * NR + r, a * NR + r + CHUNK)
+            eh, el = split(inject[STEPS - 1, rows, 0:HALF])
+            oh, ol = split(inject[STEPS - 1, rows, HALF:])
+            lc, ls = fold(mm3(eh, el, bch[0:HALF, :], bcl[0:HALF, :]), mm3(oh, ol, bsh[0:HALF, :], bsl[0:HALF, :]))
+            state[rows, 0:HALF] = lc
+            state[rows, HALF:] = ls
+            store_split(a, r)
+
+    def pull_back(k, a, rows, sw, eq, oq, coupled):
+        eu, ou = hist_u[k, rows, 0:HALF], hist_u[k, rows, HALF:]
+        ev, ov = hist_v[k, rows, 0:HALF], hist_v[k, rows, HALF:]
+        speed_e = sw + advection_gain * eu
+        speed_o = advection_gain * ou
+        tve = -(speed_e * eq + speed_o * oq)
+        tvo = -(speed_e * oq + speed_o * eq)
+        eq = advection_gain * eq
+        oq = advection_gain * oq
+        tue = inject[k - 1, rows, 0:HALF] - (ev * eq + ov * oq)
+        tuo = inject[k - 1, rows, HALF:] - (ev * oq + ov * eq)
+        ueh, uel = split(tue)
+        uoh, uol = split(tuo)
+        veh, vel = split(tve)
+        voh, vol = split(tvo)
+        pc = mm3(ueh, uel, bch[0:HALF, :], bcl[0:HALF, :]) + mm3(voh, vol, bch[HALF:, :], bcl[HALF:, :])
+        ps = mm3(uoh, uol, bsh[0:HALF, :], bsl[0:HALF, :]) + mm3(veh, vel, bsh[HALF:, :], bsl[HALF:, :])
+        pc, ps = fold(pc, ps)
+        new_c = decay * state[rows, 0:HALF] + pc + coupled[:, 0:HALF]
+        new_s = decay * state[rows, HALF:] + ps + coupled[:, HALF:]
+        if a < AX - 1:
+            if isinstance(rows, slice):
+                after = slice(rows.start + NR, rows.stop + NR)
+            else:
+                after = pl.ds(pl.multiple_of((a + 1) * NR + chip, 8), 2 * QR)
+            new_c = new_c + reach * state[after, 0:HALF]
+            new_s = new_s + reach * state[after, HALF:]
+        state[rows, 0:HALF] = new_c
+        state[rows, HALF:] = new_s
 
     def backward_step(k):
         couple(rtl)
-        sw = jnp.concatenate([swirl[...], swirl[...]], 1)
         for a in range(AX):
-            rows = slice(a * NR, (a + 1) * NR)
-            eq, oq = expand_u(a)
-            eu, ou = hist_u[k, rows, 0:HALF], hist_u[k, rows, HALF:]
-            ev, ov = hist_v[k, rows, 0:HALF], hist_v[k, rows, HALF:]
-            speed_e = sw + advection_gain * eu
-            speed_o = advection_gain * ou
-            tve = -(speed_e * eq + speed_o * oq)
-            tvo = -(speed_e * oq + speed_o * eq)
-            eq = advection_gain * eq
-            oq = advection_gain * oq
-            tue = inject[k - 1, rows, 0:HALF] - (ev * eq + ov * oq)
-            tuo = inject[k - 1, rows, HALF:] - (ev * oq + ov * eq)
-            ueh, uel = split(tue)
-            uoh, uol = split(tuo)
-            veh, vel = split(tve)
-            voh, vol = split(tvo)
-            pc = mm3(ueh, uel, bch[0:HALF, :], bcl[0:HALF, :]) + mm3(voh, vol, bch[HALF:, :], bcl[HALF:, :])
-            ps = mm3(uoh, uol, bsh[0:HALF, :], bsl[0:HALF, :]) + mm3(veh, vel, bsh[HALF:, :], bsl[HALF:, :])
-            pc, ps = fold(pc, ps)
-            new_c = decay * state[rows, 0:HALF] + pc + rad[a, :, 0:HALF]
-            new_s = decay * state[rows, HALF:] + ps + rad[a, :, HALF:]
-            if a < AX - 1:
-                after = slice((a + 1) * NR, (a + 2) * NR)
-                new_c = new_c + reach * state[after, 0:HALF]
-                new_s = new_s + reach * state[after, HALF:]
-            state[rows, 0:HALF] = new_c
-            state[rows, HALF:] = new_s
-            store_split(a)
+            for r in range(0, NR, CHUNK):
+                sw = jnp.concatenate([swirl[r:r + CHUNK, :], swirl[r:r + CHUNK, :]], 1)
+                eq, oq = expand_u(a, r)
+                pull_back(k, a, slice(a * NR + r, a * NR + r + CHUNK), sw, eq, oq, rad[a, r:r + CHUNK, :])
+                store_split(a, r)
+
+    def backward_chip():
+        part = pl.ds(chip, 2 * QR)
+        sw = jnp.concatenate([swirl[part, :], swirl[part, :]], 1)
+        for a in range(AX):
+            rows = pl.ds(pl.multiple_of(a * NR + chip, 16), 2 * QR)
+            coupled = mm(rtl[part, :], high[a])
+            ahead = high[a, part, :]
+            rest = high[a, pl.ds(pl.multiple_of(2 * NR + chip, 16), 2 * QR), :]
+            eq = mm3(ahead[:, 0:HALF], rest[:, 0:HALF], tch[:, 0:HALF], tcl[:, 0:HALF])
+            oq = mm3(ahead[:, HALF:], rest[:, HALF:], tsh[:, 0:HALF], tsl[:, 0:HALF])
+            pull_back(1, a, rows, sw, eq, oq, coupled)
 
     def inward(i, carry):
         k = STEPS - 1 - i
@@ -369,10 +417,14 @@
         backward_step(k)
         return carry
 
-    lax.fori_loop(0, STEPS - 1, inward, 0)
+    lax.fori_loop(0, STEPS - 2, inward, 0)
+    gather_gradient(1)
+    backward_chip()
     gather_gradient(0)
     gh, gl = split(gsum[...])
-    grad_out[...] = mm3(gh, gl, gth[...], gtl[...])
+    gsum[...] = mm3(gh, gl, gth[...], gtl[...])
+    keep_out[0:QR, :] = gsum[pl.ds(pl.multiple_of(core * QR, 8), QR), :]
+    send_out[0:QR, :] = gsum[pl.ds(pl.multiple_of((1 - core) * QR, 8), QR), :]
 
 
 def window_step(place, turns, radial_op, pieces):
@@ -388,8 +440,8 @@
         kernel,
         out_shape=(
             jax.ShapeDtypeStruct((AX, QR, 384), f32),
-            jax.ShapeDtypeStruct((2 * QR, NT), f32),
-            jax.ShapeDtypeStruct((8, 128), f32),
+            jax.ShapeDtypeStruct((QR + 8, NT), f32),
+            jax.ShapeDtypeStruct((QR + 8, NT), f32),
         ),
         in_specs=[pl.BlockSpec(memory_space=pltpu.SMEM)] + [vmem] * (len(operands) - 1),
         out_specs=(vmem, vmem, vmem),
@@ -436,17 +488,16 @@
     message = jnp.concatenate([first_guess[0, 0], first_guess[0, 1], forcing, extra], 1)
     other_x = space_swap(message, 8)
     both = jnp.concatenate([message, other_x], 0)
-    pieces = [message, other_x] + [space_turn(both, d) for d in (1, 2, 3)]
+    turned = [space_turn(both, d) for d in (1, 2, 3)]
+    pieces = list(lax.optimization_barrier((message, other_x, *turned)))
     pieces += [space_swap(piece, 1) for piece in pieces]
 
     turns = turn_tables(start_step[0])
-    final, grad, misses = window_step(me.astype(jnp.int32).reshape(1), turns, radial_op, pieces)
-
-    core = me % 2
-    for_other = lax.dynamic_slice_in_dim(grad, (1 - core) * QR, QR, 0)
-    own = lax.dynamic_slice_in_dim(grad, core * QR, QR, 0)
-    misfit = (misses + space_swap(misses, 1))[0, 0:1] * (0.5 / (STEPS * BLOCKS * OBS))
-    total = own + space_swap(for_other, 1)
+    final, keep, send = window_step(me.astype(jnp.int32).reshape(1), turns, radial_op, pieces)
+
+    both_cores = keep + space_swap(send, 1)
+    misfit = both_cores[QR, 0:1] * (0.5 / (STEPS * BLOCKS * OBS))
+    total = both_cores[0:QR]
     near = [win_send(total, lambda i, f=f: i ^ f) for f in (1, 2, 3)]
     total = total + near[0] + near[1] + near[2]
     far = [win_send(total, lambda i, d=d: (i + 2 * d) % 16) for d in (2, 4, 6)]

time: 139 us -> 126 us (0.906)
  Pallas kernels: 83.2 us -> 67.2 us
  waiting for transfers between devices: 22.4 us -> 27.1 us
  other arithmetic: 1.08 us -> 2.62 us
  starting transfers between devices: 22.9 us -> 21.5 us
    pallas_call x1, Pallas kernels: 83.2 us -> 67.2 us  [window_step(): pl.pallas_call(kernel, out_shape=(jax.ShapeDtypeStruct((AX, QR, 384), f32...]
    ppermute x3, waiting for transfers between devices: 10.1 us -> 13.2 us  [space_turn(): lax.ppermute(x, 'space', [(i, i // 8 * 8 + (i + 2 * d) % 8) for i in rang...]
    ppermute x6, waiting for transfers between devices: 4.58 us -> 7.06 us  [win_send(): return lax.ppermute(x, 'win', [(i, where(i)) for i in range(16)])]
    ppermute x8 -> x7, waiting for transfers between devices: 7.69 us -> 6.92 us  [space_swap(): return lax.ppermute(x, 'space', [(i, i ^ bits) for i in range(BLOCKS)])]
    ppermute x8 -> x7, starting transfers between devices: 2.97 us -> 3.46 us  [space_swap(): return lax.ppermute(x, 'space', [(i, i ^ bits) for i in range(BLOCKS)])]
  transfers between devices with their start and end apart: 17 -> 16, of which waited for: 10 -> 9; matrix products, arithmetic and copies ran while one was open for 1% -> 1% of each run, Pallas kernels for 0% -> 0%
where the time goes in v2:
time: 126 us; the launch traced here: 125 us
  Pallas kernels  67.2 us (53%)
  waiting for transfers between devices  27.1 us (22%)
  starting transfers between devices  21.5 us (17%)
  local copies, waits for them, and re-layouts  3.67 us (3%)
  between operations  3.2 us (3%)
  other arithmetic  2.62 us (2%)
    pallas_call x1, Pallas kernels, window_step(): pl.pallas_call(kernel, out_shape=(jax.ShapeDtypeStruct((AX, QR, 384), f32...  67.2 us
    ppermute x6, starting transfers between devices, win_send(): return lax.ppermute(x, 'win', [(i, where(i)) for i in range(16)])  13.4 us
    ppermute x3, waiting for transfers between devices, space_turn(): lax.ppermute(x, 'space', [(i, i // 8 * 8 + (i + 2 * d) % 8) for i in rang...  13.2 us
    ppermute x6, waiting for transfers between devices, win_send(): return lax.ppermute(x, 'win', [(i, where(i)) for i in range(16)])  7.06 us
    ppermute x7, waiting for transfers between devices, space_swap(): return lax.ppermute(x, 'space', [(i, i ^ bits) for i in range(BLOCKS)])  6.92 us
    ppermute x3, starting transfers between devices, space_turn(): lax.ppermute(x, 'space', [(i, i // 8 * 8 + (i + 2 * d) % 8) for i in rang...  4.69 us
    ppermute x7, starting transfers between devices, space_swap(): return lax.ppermute(x, 'space', [(i, i ^ bits) for i in range(BLOCKS)])  3.46 us
  transfers between devices with their start and end apart: 16, of which 9 were waited for; matrix products, arithmetic and copies ran while one was open for 1% of the time, Pallas kernels for 0%

profile of v2, /device:TPU:2, one launch (start us, length us, event | category | flops | bytes accessed | tf_op | source)
XLA Modules:
  0.0 125.4 jit_solution(11528932292146437317)
XLA Ops:
  0.6 0.7 convert_bitcast_fusion
  1.3 0.8 slice_bitcast_fusion.1
  2.2 0.7 copy-done.11
  2.9 2.2 %collective-permute-start = (f32[24,1536]{1,0:T(8,128)S(1)}, f32[24,1536]{1,0:T(8,128)S(1)}, u32[]{:S(2)}, u32[]{:S(2)}) collective-permute-start(f32[24,1536]{1,0:T(8,128)S(1)} %maximum_maximum_fusion.p0), channel_id=1, source_target_pairs={{0,8},{1,9},{2,10},{3,11},{4,12},{5,13},{6,14},{7,15},{8,0},{9,1},... | collective-permute-start | bytes 442376 | tf_op jit(solution)/shard_map/ppermute | solution.py:472
  5.1 5.0 %collective-permute-done.p1 = f32[24,1536]{1,0:T(8,128)S(1)} collective-permute-done((f32[24,1536]{1,0:T(8,128)S(1)}, f32[24,1536]{1,0:T(8,128)S(1)}, u32[]{:S(2)}, u32[]{:S(2)}) %collective-permute-start) | collective-permute-done | bytes 147488 | tf_op jit(solution)/shard_map/ppermute | solution.py:472
  10.1 3.1 %collective-permute-start.3 = (f32[48,1536]{1,0:T(8,128)S(1)}, f32[48,1536]{1,0:T(8,128)S(1)}, u32[]{:S(2)}, u32[]{:S(2)}) collective-permute-start(f32[48,1536]{1,0:T(8,128)S(1)} %pad_maximum_fusion), channel_id=1, source_target_pairs={{0,6},{1,7},{2,0},{3,1},{4,2},{5,3},{6,4},{7,5},{8,14},{9,15},{10,... | collective-permute-start | bytes 884744 | tf_op jit(solution)/shard_map/ppermute | solution.py:475
  13.2 0.6 collective-permute-start.2
  13.8 1.0 collective-permute-start.1
  15.4 9.4 %collective-permute-done.3.p4 = f32[48,1536]{1,0:T(8,128)S(1)} collective-permute-done((f32[48,1536]{1,0:T(8,128)S(1)}, f32[48,1536]{1,0:T(8,128)S(1)}, u32[]{:S(2)}, u32[]{:S(2)}) %collective-permute-start.3) | collective-permute-done | bytes 294944 | tf_op jit(solution)/shard_map/ppermute | solution.py:475
  24.9 3.7 %collective-permute-done.1.p2 = f32[48,1536]{1,0:T(8,128)S(1)} collective-permute-done((f32[48,1536]{1,0:T(8,128)S(1)}, f32[48,1536]{1,0:T(8,128)S(1)}, u32[]{:S(2)}, u32[]{:S(2)}) %collective-permute-start.1) | collective-permute-done | bytes 294944 | tf_op jit(solution)/shard_map/ppermute | solution.py:475
  28.6 0.5 collective-permute-start.7
  29.1 0.5 collective-permute-start.4
  29.7 0.4 fusion.5
  30.1 0.7 stack.2.turns
  30.8 0.4 collective-permute-done.4.q0
  31.2 0.2 collective-permute-done.5.q1
  31.5 0.4 copy-done.9
  31.9 0.2 copy-done.10
  32.4 67.2 %shard_map.211 = (f32[2,24,384]{2,1,0:T(8,128)}, f32[32,512]{1,0:T(8,128)}, f32[32,512]{1,0:T(8,128)}) custom-call(s32[1]{0:T(128)} %bitcast.place, f32[8,8,256]{2,1,0:T(8,128)} %stack.2.turns, f32[16,256]{1,0:T(8,128)} %constant.76.clone.lanes, f32[384,384]{1,0:T(8,128)} %radial_op.1, bf16[256,512]{1,0:T(8,128)(2,1)} %constant.64.clone.tch, ...), custom_call_target="tpu_custom_call" | custom-call | tf_op jit(solution)/shard_map/pallas_call | solution.py:439
  99.7 0.1 collective-permute-start.9
  99.8 1.3 %collective-permute-done.9 = f32[32,512]{1,0:T(8,128)S(1)} collective-permute-done((f32[32,512]{1,0:T(8,128)}, f32[32,512]{1,0:T(8,128)S(1)}, u32[]{:S(2)}, u32[]{:S(2)}) %collective-permute-start.9) | collective-permute-done | bytes 65568 | tf_op jit(solution)/shard_map/ppermute | solution.py:472
  101.1 0.9 add.99
  102.0 2.0 %collective-permute-start.11 = (f32[24,512]{1,0:T(8,128)S(1)}, f32[24,512]{1,0:T(8,128)S(1)}, u32[]{:S(2)}, u32[]{:S(2)}) collective-permute-start(f32[24,512]{1,0:T(8,128)S(1)} %slice.17), channel_id=1, source_target_pairs={{0,32},{16,48},{32,0},{48,16},{64,96},{80,112},{96,64},{112,80},{1... | collective-permute-start | bytes 147464 | tf_op jit(solution)/shard_map/ppermute | solution.py:478
  104.1 1.5 %collective-permute-start.10 = (f32[24,512]{1,0:T(8,128)S(1)}, f32[24,512]{1,0:T(8,128)S(1)}, u32[]{:S(2)}, u32[]{:S(2)}) collective-permute-start(f32[24,512]{1,0:T(8,128)S(1)} %slice.17), channel_id=1, source_target_pairs={{0,16},{16,0},{32,48},{48,32},{64,80},{80,64},{96,112},{112,96},{1... | collective-permute-start | bytes 147464 | tf_op jit(solution)/shard_map/ppermute | solution.py:478
  105.6 0.6 collective-permute-done.11
  106.2 2.8 %collective-permute-done.12 = f32[24,512]{1,0:T(8,128)S(1)} collective-permute-done((f32[24,512]{1,0:T(8,128)S(1)}, f32[24,512]{1,0:T(8,128)S(1)}, u32[]{:S(2)}, u32[]{:S(2)}) %collective-permute-start.12) | collective-permute-done | bytes 49184 | tf_op jit(solution)/shard_map/ppermute | solution.py:478
  109.0 6.0 %collective-permute-start.15 = (f32[24,512]{1,0:T(8,128)S(1)}, f32[24,512]{1,0:T(8,128)S(1)}, u32[]{:S(2)}, u32[]{:S(2)}) collective-permute-start(f32[24,512]{1,0:T(8,128)S(1)} %add_add_fusion.1), channel_id=1, source_target_pairs={{0,192},{16,208},{32,224},{48,240},{64,0},{80,16},{96,32},{112,48}... | collective-permute-start | bytes 147464 | tf_op jit(solution)/shard_map/ppermute | solution.py:478
  115.0 1.0 collective-permute-start.14
  116.0 2.8 %collective-permute-start.13 = (f32[24,512]{1,0:T(8,128)S(1)}, f32[24,512]{1,0:T(8,128)S(1)}, u32[]{:S(2)}, u32[]{:S(2)}) collective-permute-start(f32[24,512]{1,0:T(8,128)S(1)} %add_add_fusion.1), channel_id=1, source_target_pairs={{0,64},{16,80},{32,96},{48,112},{64,128},{80,144},{96,160},{112,17... | collective-permute-start | bytes 147464 | tf_op jit(solution)/shard_map/ppermute | solution.py:478
  118.8 0.5 slice.16
  120.0 3.6 %collective-permute-done.14 = f32[24,512]{1,0:T(8,128)S(1)} collective-permute-done((f32[24,512]{1,0:T(8,128)S(1)}, f32[24,512]{1,0:T(8,128)S(1)}, u32[]{:S(2)}, u32[]{:S(2)}) %collective-permute-start.14) | collective-permute-done | bytes 49184 | tf_op jit(solution)/shard_map/ppermute | solution.py:478
  123.6 0.6 add_add_fusion
  (41 shorter events, 0.7 us)
Async XLA Ops:
  1.3 0.8 copy-start.12
  1.3 0.8 copy-start.8
  2.1 0.7 copy-start.11
  2.9 26.3 %copy-start = (f32[24,1536]{1,0:T(8,128)}, f32[24,1536]{1,0:T(8,128)S(1)}, u32[]{:S(2)}) copy-start(f32[24,1536]{1,0:T(8,128)S(1)} %maximum_maximum_fusion.p0) | copy-start | bytes 442372
  2.9 7.2 %collective-permute-start = (f32[24,1536]{1,0:T(8,128)S(1)}, f32[24,1536]{1,0:T(8,128)S(1)}, u32[]{:S(2)}, u32[]{:S(2)}) collective-permute-start(f32[24,1536]{1,0:T(8,128)S(1)} %maximum_maximum_fusion.p0), channel_id=1, source_target_pairs={{0,8},{1,9},{2,10},{3,11},{4,12},{5,13},{6,14},{7,15},{8,0},{9,1},... | collective-permute-start | bytes 442376 | tf_op jit(solution)/shard_map/ppermute | solution.py:472
  10.0 19.6 %copy-start.1 = (f32[24,1536]{1,0:T(8,128)}, f32[24,1536]{1,0:T(8,128)S(1)}, u32[]{:S(2)}) copy-start(f32[24,1536]{1,0:T(8,128)S(1)} %collective-permute-done.p1) | copy-start | bytes 442372
  10.1 14.8 %collective-permute-start.3 = (f32[48,1536]{1,0:T(8,128)S(1)}, f32[48,1536]{1,0:T(8,128)S(1)}, u32[]{:S(2)}, u32[]{:S(2)}) collective-permute-start(f32[48,1536]{1,0:T(8,128)S(1)} %pad_maximum_fusion), channel_id=1, source_target_pairs={{0,6},{1,7},{2,0},{3,1},{4,2},{5,3},{6,4},{7,5},{8,14},{9,15},{10,... | collective-permute-start | bytes 884744 | tf_op jit(solution)/shard_map/ppermute | solution.py:475
  13.2 11.7 %collective-permute-start.2 = (f32[48,1536]{1,0:T(8,128)S(1)}, f32[48,1536]{1,0:T(8,128)S(1)}, u32[]{:S(2)}, u32[]{:S(2)}) collective-permute-start(f32[48,1536]{1,0:T(8,128)S(1)} %pad_maximum_fusion), channel_id=1, source_target_pairs={{0,4},{1,5},{2,6},{3,7},{4,0},{5,1},{6,2},{7,3},{8,12},{9,13},{10,... | collective-permute-start | bytes 884744 | tf_op jit(solution)/shard_map/ppermute | solution.py:475
  13.8 14.8 %collective-permute-start.1 = (f32[48,1536]{1,0:T(8,128)S(1)}, f32[48,1536]{1,0:T(8,128)S(1)}, u32[]{:S(2)}, u32[]{:S(2)}) collective-permute-start(f32[48,1536]{1,0:T(8,128)S(1)} %pad_maximum_fusion), channel_id=1, source_target_pairs={{0,2},{1,3},{2,4},{3,5},{4,6},{5,7},{6,0},{7,1},{8,10},{9,11},{10,... | collective-permute-start | bytes 884744 | tf_op jit(solution)/shard_map/ppermute | solution.py:475
  24.9 6.6 %copy-start.2 = (f32[48,1536]{1,0:T(8,128)}, f32[48,1536]{1,0:T(8,128)S(1)}, u32[]{:S(2)}) copy-start(f32[48,1536]{1,0:T(8,128)S(1)} %collective-permute-done.3.p4) | copy-start | bytes 884740
  24.9 6.6 %copy-start.3 = (f32[48,1536]{1,0:T(8,128)}, f32[48,1536]{1,0:T(8,128)S(1)}, u32[]{:S(2)}) copy-start(f32[48,1536]{1,0:T(8,128)S(1)} %collective-permute-done.2.p3) | copy-start | bytes 884740
  28.6 2.9 %copy-start.4 = (f32[48,1536]{1,0:T(8,128)}, f32[48,1536]{1,0:T(8,128)S(1)}, u32[]{:S(2)}) copy-start(f32[48,1536]{1,0:T(8,128)S(1)} %collective-permute-done.1.p2) | copy-start | bytes 884740
  28.6 2.9 %collective-permute-start.6 = (f32[48,1536]{1,0:T(8,128)S(1)}, f32[48,1536]{1,0:T(8,128)S(1)}, u32[]{:S(2)}, u32[]{:S(2)}) collective-permute-start(f32[48,1536]{1,0:T(8,128)S(1)} %collective-permute-done.1.p2), channel_id=1, source_target_pairs={{0,1},{1,0},{2,3},{3,2},{4,5},{5,4},{6,7},{7,6},{8,9},{9,8},{10,11... | collective-permute-start | bytes 884744 | tf_op jit(solution)/shard_map/ppermute | solution.py:472
  28.6 2.8 %collective-permute-start.7 = (f32[48,1536]{1,0:T(8,128)S(1)}, f32[48,1536]{1,0:T(8,128)S(1)}, u32[]{:S(2)}, u32[]{:S(2)}) collective-permute-start(f32[48,1536]{1,0:T(8,128)S(1)} %collective-permute-done.2.p3), channel_id=1, source_target_pairs={{0,1},{1,0},{2,3},{3,2},{4,5},{5,4},{6,7},{7,6},{8,9},{9,8},{10,11... | collective-permute-start | bytes 884744 | tf_op jit(solution)/shard_map/ppermute | solution.py:472
  29.1 2.4 %collective-permute-start.8 = (f32[48,1536]{1,0:T(8,128)S(1)}, f32[48,1536]{1,0:T(8,128)S(1)}, u32[]{:S(2)}, u32[]{:S(2)}) collective-permute-start(f32[48,1536]{1,0:T(8,128)S(1)} %collective-permute-done.3.p4), channel_id=1, source_target_pairs={{0,1},{1,0},{2,3},{3,2},{4,5},{5,4},{6,7},{7,6},{8,9},{9,8},{10,11... | collective-permute-start | bytes 884744 | tf_op jit(solution)/shard_map/ppermute | solution.py:472
  29.1 2.1 %collective-permute-start.4 = (f32[24,1536]{1,0:T(8,128)S(1)}, f32[24,1536]{1,0:T(8,128)S(1)}, u32[]{:S(2)}, u32[]{:S(2)}) collective-permute-start(f32[24,1536]{1,0:T(8,128)S(1)} %maximum_maximum_fusion.p0), channel_id=1, source_target_pairs={{0,1},{1,0},{2,3},{3,2},{4,5},{5,4},{6,7},{7,6},{8,9},{9,8},{10,11... | collective-permute-start | bytes 442376 | tf_op jit(solution)/shard_map/ppermute | solution.py:472
  29.6 1.8 %collective-permute-start.5 = (f32[24,1536]{1,0:T(8,128)S(1)}, f32[24,1536]{1,0:T(8,128)S(1)}, u32[]{:S(2)}, u32[]{:S(2)}) collective-permute-start(f32[24,1536]{1,0:T(8,128)S(1)} %collective-permute-done.p1), channel_id=1, source_target_pairs={{0,1},{1,0},{2,3},{3,2},{4,5},{5,4},{6,7},{7,6},{8,9},{9,8},{10,11... | collective-permute-start | bytes 442376 | tf_op jit(solution)/shard_map/ppermute | solution.py:472
  31.2 0.6 copy-start.9
  31.4 0.7 copy-start.10
  31.4 0.8 copy-start.5
  31.5 0.9 copy-start.6
  31.5 0.9 copy-start.7
  99.7 1.5 %collective-permute-start.9 = (f32[32,512]{1,0:T(8,128)}, f32[32,512]{1,0:T(8,128)S(1)}, u32[]{:S(2)}, u32[]{:S(2)}) collective-permute-start(f32[32,512]{1,0:T(8,128)} %get-tuple-element.18), channel_id=1, source_target_pairs={{0,1},{1,0},{2,3},{3,2},{4,5},{5,4},{6,7},{7,6},{8,9},{9,8},{10,11... | collective-permute-start | bytes 196616 | tf_op jit(solution)/shard_map/ppermute | solution.py:472
  102.0 4.2 %collective-permute-start.11 = (f32[24,512]{1,0:T(8,128)S(1)}, f32[24,512]{1,0:T(8,128)S(1)}, u32[]{:S(2)}, u32[]{:S(2)}) collective-permute-start(f32[24,512]{1,0:T(8,128)S(1)} %slice.17), channel_id=1, source_target_pairs={{0,32},{16,48},{32,0},{48,16},{64,96},{80,112},{96,64},{112,80},{1... | collective-permute-start | bytes 147464 | tf_op jit(solution)/shard_map/ppermute | solution.py:478
  104.0 5.0 %collective-permute-start.12 = (f32[24,512]{1,0:T(8,128)S(1)}, f32[24,512]{1,0:T(8,128)S(1)}, u32[]{:S(2)}, u32[]{:S(2)}) collective-permute-start(f32[24,512]{1,0:T(8,128)S(1)} %slice.17), channel_id=1, source_target_pairs={{0,48},{16,32},{32,16},{48,0},{64,112},{80,96},{96,80},{112,64},{1... | collective-permute-start | bytes 147464 | tf_op jit(solution)/shard_map/ppermute | solution.py:478
  104.1 4.9 %collective-permute-start.10 = (f32[24,512]{1,0:T(8,128)S(1)}, f32[24,512]{1,0:T(8,128)S(1)}, u32[]{:S(2)}, u32[]{:S(2)}) collective-permute-start(f32[24,512]{1,0:T(8,128)S(1)} %slice.17), channel_id=1, source_target_pairs={{0,16},{16,0},{32,48},{48,32},{64,80},{80,64},{96,112},{112,96},{1... | collective-permute-start | bytes 147464 | tf_op jit(solution)/shard_map/ppermute | solution.py:478
  109.0 11.0 %collective-permute-start.15 = (f32[24,512]{1,0:T(8,128)S(1)}, f32[24,512]{1,0:T(8,128)S(1)}, u32[]{:S(2)}, u32[]{:S(2)}) collective-permute-start(f32[24,512]{1,0:T(8,128)S(1)} %add_add_fusion.1), channel_id=1, source_target_pairs={{0,192},{16,208},{32,224},{48,240},{64,0},{80,16},{96,32},{112,48}... | collective-permute-start | bytes 147464 | tf_op jit(solution)/shard_map/ppermute | solution.py:478
  115.0 8.6 %collective-permute-start.14 = (f32[24,512]{1,0:T(8,128)S(1)}, f32[24,512]{1,0:T(8,128)S(1)}, u32[]{:S(2)}, u32[]{:S(2)}) collective-permute-start(f32[24,512]{1,0:T(8,128)S(1)} %add_add_fusion.1), channel_id=1, source_target_pairs={{0,128},{16,144},{32,160},{48,176},{64,192},{80,208},{96,224},{112... | collective-permute-start | bytes 147464 | tf_op jit(solution)/shard_map/ppermute | solution.py:478
  116.0 7.6 %collective-permute-start.13 = (f32[24,512]{1,0:T(8,128)S(1)}, f32[24,512]{1,0:T(8,128)S(1)}, u32[]{:S(2)}, u32[]{:S(2)}) collective-permute-start(f32[24,512]{1,0:T(8,128)S(1)} %add_add_fusion.1), channel_id=1, source_target_pairs={{0,64},{16,80},{32,96},{48,112},{64,128},{80,144},{96,160},{112,17... | collective-permute-start | bytes 147464 | tf_op jit(solution)/shard_map/ppermute | solution.py:478

commit v3 on v2

--- a/solution.py
+++ b/solution.py
@@ -129,7 +129,7 @@
 
 def kernel(
     place, turns, lanes, radial_op, tch, tcl, tsh, tsl, bch, bcl, bsh, bsl, fth, ftl, gth, gtl,
-    p0, p1, p2, p3, p4, q0, q1, q2, q3, q4,
+    p0, p1, p2, p3, p4, p5, q0, q1, q2, q3, q4, q5,
     final_out, keep_out, send_out,
     state, high, rad, hist_u, hist_v, inject, rl, rtl, swirl, forced, obs_i, obs_v, gsum, msum,
 ):
@@ -145,8 +145,9 @@
         return x * 8 + y * 2 + c
 
     sources = [(p0, 0, 0, False, False), (p1, 0, 0, True, False), (q0, 0, 0, False, True), (q1, 0, 0, True, True)]
-    for d, (pd, qd) in enumerate(((p2, q2), (p3, q3), (p4, q4)), 1):
+    for d, pd, qd in ((1, p2, q2), (3, p3, q3)):
         sources += [(pd, 0, d, False, False), (pd, QR, d, True, False), (qd, 0, d, False, True), (qd, QR, d, True, True)]
+    sources += [(p4, 0, 2, False, False), (p5, 0, 2, True, False), (q4, 0, 2, False, True), (q5, 0, 2, True, True)]
 
     def lane(i):
         return lanes[i:i + 1, :]
@@ -208,6 +209,9 @@
         ou = mm3(sh, sl, tsh[:, 0:HALF], tsl[:, 0:HALF])
         return eu, ou
 
+    def slot_v(k):
+        return (k + STEPS - 2) % (STEPS - 1)
+
     def forward_step(k):
         expanded = [None, None]
         fields = [None, None]
@@ -223,8 +227,8 @@
             ou, ev = from_sin[:, 0:HALF], from_sin[:, HALF:]
             hist_u[k, rows, 0:HALF] = eu
             hist_u[k, rows, HALF:] = ou
-            hist_v[k, rows, 0:HALF] = ev
-            hist_v[k, rows, HALF:] = ov
+            hist_v[slot_v(k), rows, 0:HALF] = ev
+            hist_v[slot_v(k), rows, HALF:] = ov
             speed_e = sw + advection_gain * eu
             speed_o = advection_gain * ou
             fields[a] = split(-(speed_e * ev + speed_o * ov)) + split(-(speed_e * ov + speed_o * ev))
@@ -361,8 +365,11 @@
             store_split(a, r)
 
     def pull_back(k, a, rows, sw, eq, oq, coupled):
+        gather_back(a, rows, weigh(k, rows, sw, eq, oq), coupled)
+
+    def weigh(k, rows, sw, eq, oq):
         eu, ou = hist_u[k, rows, 0:HALF], hist_u[k, rows, HALF:]
-        ev, ov = hist_v[k, rows, 0:HALF], hist_v[k, rows, HALF:]
+        ev, ov = hist_v[slot_v(k), rows, 0:HALF], hist_v[slot_v(k), rows, HALF:]
         speed_e = sw + advection_gain * eu
         speed_o = advection_gain * ou
         tve = -(speed_e * eq + speed_o * oq)
@@ -371,10 +378,10 @@
         oq = advection_gain * oq
         tue = inject[k - 1, rows, 0:HALF] - (ev * eq + ov * oq)
         tuo = inject[k - 1, rows, HALF:] - (ev * oq + ov * eq)
-        ueh, uel = split(tue)
-        uoh, uol = split(tuo)
-        veh, vel = split(tve)
-        voh, vol = split(tvo)
+        return split(tue) + split(tuo) + split(tve) + split(tvo)
+
+    def gather_back(a, rows, fields, coupled):
+        ueh, uel, uoh, uol, veh, vel, voh, vol = fields
         pc = mm3(ueh, uel, bch[0:HALF, :], bcl[0:HALF, :]) + mm3(voh, vol, bch[HALF:, :], bcl[HALF:, :])
         ps = mm3(uoh, uol, bsh[0:HALF, :], bsl[0:HALF, :]) + mm3(veh, vel, bsh[HALF:, :], bsl[HALF:, :])
         pc, ps = fold(pc, ps)
@@ -391,13 +398,17 @@
         state[rows, HALF:] = new_s
 
     def backward_step(k):
-        couple(rtl)
+        synthesized = [expand_u(a, 0) for a in range(AX)]
+        sw = jnp.concatenate([swirl[...], swirl[...]], 1)
+        fields = []
         for a in range(AX):
-            for r in range(0, NR, CHUNK):
-                sw = jnp.concatenate([swirl[r:r + CHUNK, :], swirl[r:r + CHUNK, :]], 1)
-                eq, oq = expand_u(a, r)
-                pull_back(k, a, slice(a * NR + r, a * NR + r + CHUNK), sw, eq, oq, rad[a, r:r + CHUNK, :])
-                store_split(a, r)
+            rows = slice(a * NR, (a + 1) * NR)
+            fields.append(weigh(k, rows, sw, *synthesized[a]))
+            rad[a] = mm(rtl[...], high[a])
+        for a in range(AX):
+            rows = slice(a * NR, (a + 1) * NR)
+            gather_back(a, rows, fields[a], rad[a])
+            store_split(a, 0)
 
     def backward_chip():
         part = pl.ds(chip, 2 * QR)
@@ -450,7 +461,7 @@
             pltpu.VMEM((AX, 3 * NR, COEF), bf16),
             pltpu.VMEM((AX, NR, COEF), f32),
             pltpu.VMEM((STEPS, ROWS, COEF), f32),
-            pltpu.VMEM((STEPS, ROWS, COEF), f32),
+            pltpu.VMEM((STEPS - 1, ROWS, COEF), f32),
             pltpu.VMEM((STEPS, ROWS, COEF), f32),
             pltpu.VMEM((NR, 3 * NR), bf16),
             pltpu.VMEM((NR, 3 * NR), bf16),
@@ -488,9 +499,15 @@
     message = jnp.concatenate([first_guess[0, 0], first_guess[0, 1], forcing, extra], 1)
     other_x = space_swap(message, 8)
     both = jnp.concatenate([message, other_x], 0)
-    turned = [space_turn(both, d) for d in (1, 2, 3)]
-    pieces = list(lax.optimization_barrier((message, other_x, *turned)))
-    pieces += [space_swap(piece, 1) for piece in pieces]
+    left, right = space_turn(both, 1), space_turn(both, 3)
+    message, other_x, left, right, ahead, behind = lax.optimization_barrier(
+        (message, other_x, left, right, left[:QR], right[QR:])
+    )
+    opposite = [space_turn(ahead, 1), space_turn(behind, 3)]
+    near_pieces = [message, other_x, left, right]
+    swapped = [space_swap(piece, 1) for piece in near_pieces]
+    opposite, swapped = lax.optimization_barrier((opposite, swapped))
+    pieces = near_pieces + opposite + swapped + [space_swap(piece, 1) for piece in opposite]
 
     turns = turn_tables(start_step[0])
     final, keep, send = window_step(me.astype(jnp.int32).reshape(1), turns, radial_op, pieces)

time: 126 us -> 124 us (0.984)
  Pallas kernels: 67.2 us -> 64.9 us
  starting transfers between devices: 21.5 us -> 23.4 us
  waiting for transfers between devices: 27.1 us -> 25.3 us
    pallas_call x1, Pallas kernels: 67.2 us -> 64.9 us  [window_step(): pl.pallas_call(kernel, out_shape=(jax.ShapeDtypeStruct((AX, QR, 384), f32...]
    ppermute x3 -> x4, starting transfers between devices: 4.69 us -> 6.39 us  [space_turn(): lax.ppermute(x, 'space', [(i, i // 8 * 8 + (i + 2 * d) % 8) for i in rang...]
    ppermute x3 -> x4, waiting for transfers between devices: 13.2 us -> 12 us  [space_turn(): lax.ppermute(x, 'space', [(i, i // 8 * 8 + (i + 2 * d) % 8) for i in rang...]
    ppermute x7 -> x8, waiting for transfers between devices: 6.92 us -> 6.25 us  [space_swap(): return lax.ppermute(x, 'space', [(i, i ^ bits) for i in range(BLOCKS)])]
    ppermute x7 -> x8, starting transfers between devices: 3.46 us -> 3.68 us  [space_swap(): return lax.ppermute(x, 'space', [(i, i ^ bits) for i in range(BLOCKS)])]
  transfers between devices with their start and end apart: 16 -> 18, of which waited for: 9 -> 9; matrix products, arithmetic and copies ran while one was open for 1% -> 1% of each run, Pallas kernels for 0% -> 0%
where the time goes in v3:
time: 124 us; the launch traced here: 123 us
  Pallas kernels  64.9 us (52%)
  waiting for transfers between devices  25.3 us (20%)
  starting transfers between devices  23.4 us (19%)
  local copies, waits for them, and re-layouts  3.42 us (3%)
  between operations  3.3 us (3%)
  other arithmetic  2.62 us (2%)
    pallas_call x1, Pallas kernels, window_step(): pl.pallas_call(kernel, out_shape=(jax.ShapeDtypeStruct((AX, QR, 384), f32...  64.9 us
    ppermute x6, starting transfers between devices, win_send(): return lax.ppermute(x, 'win', [(i, where(i)) for i in range(16)])  13.4 us
    ppermute x4, waiting for transfers between devices, space_turn(): lax.ppermute(x, 'space', [(i, i // 8 * 8 + (i + 2 * d) % 8) for i in rang...  12 us
    ppermute x6, waiting for transfers between devices, win_send(): return lax.ppermute(x, 'win', [(i, where(i)) for i in range(16)])  7.02 us
    ppermute x4, starting transfers between devices, space_turn(): lax.ppermute(x, 'space', [(i, i // 8 * 8 + (i + 2 * d) % 8) for i in rang...  6.39 us
    ppermute x8, waiting for transfers between devices, space_swap(): return lax.ppermute(x, 'space', [(i, i ^ bits) for i in range(BLOCKS)])  6.25 us
    ppermute x8, starting transfers between devices, space_swap(): return lax.ppermute(x, 'space', [(i, i ^ bits) for i in range(BLOCKS)])  3.68 us
  transfers between devices with their start and end apart: 18, of which 9 were waited for; matrix products, arithmetic and copies ran while one was open for 1% of the time, Pallas kernels for 0%

profile of v3, /device:TPU:2, one launch (start us, length us, event | category | flops | bytes accessed | tf_op | source)
XLA Modules:
  0.0 123.0 jit_solution(16091300806277691378)
XLA Ops:
  0.6 0.7 convert_bitcast_fusion
  1.3 0.8 slice_bitcast_fusion.1
  2.2 0.7 copy-done.13
  2.9 2.2 %collective-permute-start = (f32[24,1536]{1,0:T(8,128)S(1)}, f32[24,1536]{1,0:T(8,128)S(1)}, u32[]{:S(2)}, u32[]{:S(2)}) collective-permute-start(f32[24,1536]{1,0:T(8,128)S(1)} %maximum_maximum_fusion.p0), channel_id=1, source_target_pairs={{0,8},{1,9},{2,10},{3,11},{4,12},{5,13},{6,14},{7,15},{8,0},{9,1},... | collective-permute-start | bytes 442376 | tf_op jit(solution)/shard_map/ppermute | solution.py:483
  5.1 5.0 %collective-permute-done.p1 = f32[24,1536]{1,0:T(8,128)S(1)} collective-permute-done((f32[24,1536]{1,0:T(8,128)S(1)}, f32[24,1536]{1,0:T(8,128)S(1)}, u32[]{:S(2)}, u32[]{:S(2)}) %collective-permute-start) | collective-permute-done | bytes 147488 | tf_op jit(solution)/shard_map/ppermute | solution.py:483
  10.1 3.1 %collective-permute-start.2 = (f32[48,1536]{1,0:T(8,128)S(1)}, f32[48,1536]{1,0:T(8,128)S(1)}, u32[]{:S(2)}, u32[]{:S(2)}) collective-permute-start(f32[48,1536]{1,0:T(8,128)S(1)} %pad_maximum_fusion), channel_id=1, source_target_pairs={{0,6},{1,7},{2,0},{3,1},{4,2},{5,3},{6,4},{7,5},{8,14},{9,15},{10,... | collective-permute-start | bytes 884744 | tf_op jit(solution)/shard_map/ppermute | solution.py:486
  13.2 5.4 %collective-permute-done.2.p3 = f32[48,1536]{1,0:T(8,128)S(1)} collective-permute-done((f32[48,1536]{1,0:T(8,128)S(1)}, f32[48,1536]{1,0:T(8,128)S(1)}, u32[]{:S(2)}, u32[]{:S(2)}) %collective-permute-start.2) | collective-permute-done | bytes 294944 | tf_op jit(solution)/shard_map/ppermute | solution.py:486
  18.6 3.4 %collective-permute-done.1.p2 = f32[48,1536]{1,0:T(8,128)S(1)} collective-permute-done((f32[48,1536]{1,0:T(8,128)S(1)}, f32[48,1536]{1,0:T(8,128)S(1)}, u32[]{:S(2)}, u32[]{:S(2)}) %collective-permute-start.1) | collective-permute-done | bytes 294944 | tf_op jit(solution)/shard_map/ppermute | solution.py:486
  22.1 0.1 collective-permute-start.7
  22.2 0.5 collective-permute-start.8
  23.3 3.2 %collective-permute-start.4 = (f32[24,1536]{1,0:T(8,128)S(1)}, f32[24,1536]{1,0:T(8,128)S(1)}, u32[]{:S(2)}, u32[]{:S(2)}) collective-permute-start(f32[24,1536]{1,0:T(8,128)S(1)} %slice.25), channel_id=1, source_target_pairs={{0,6},{1,7},{2,0},{3,1},{4,2},{5,3},{6,4},{7,5},{8,14},{9,15},{10,... | collective-permute-start | bytes 442376 | tf_op jit(solution)/shard_map/ppermute | solution.py:486
  26.6 1.9 %collective-permute-done.3.p4 = f32[24,1536]{1,0:T(8,128)S(1)} collective-permute-done((f32[24,1536]{1,0:T(8,128)S(1)}, f32[24,1536]{1,0:T(8,128)S(1)}, u32[]{:S(2)}, u32[]{:S(2)}) %collective-permute-start.3) | collective-permute-done | bytes 147488 | tf_op jit(solution)/shard_map/ppermute | solution.py:486
  28.5 1.4 %collective-permute-done.4.p5 = f32[24,1536]{1,0:T(8,128)S(1)} collective-permute-done((f32[24,1536]{1,0:T(8,128)S(1)}, f32[24,1536]{1,0:T(8,128)S(1)}, u32[]{:S(2)}, u32[]{:S(2)}) %collective-permute-start.4) | collective-permute-done | bytes 147488 | tf_op jit(solution)/shard_map/ppermute | solution.py:486
  29.9 0.2 collective-permute-start.9
  30.1 0.4 collective-permute-start.10
  30.5 0.4 fusion.5
  30.9 0.7 stack.2.turns
  31.7 0.6 copy-done.11
  32.3 64.9 %shard_map.211 = (f32[2,24,384]{2,1,0:T(8,128)}, f32[32,512]{1,0:T(8,128)}, f32[32,512]{1,0:T(8,128)}) custom-call(s32[1]{0:T(128)} %bitcast.place, f32[8,8,256]{2,1,0:T(8,128)} %stack.2.turns, f32[16,256]{1,0:T(8,128)} %constant.76.clone.lanes, f32[384,384]{1,0:T(8,128)} %radial_op.1, bf16[256,512]{1,0:T(8,128)(2,1)} %constant.64.clone.tch, ...), custom_call_target="tpu_custom_call" | custom-call | tf_op jit(solution)/shard_map/pallas_call | solution.py:450
  97.2 0.3 collective-permute-start.11
  97.5 1.3 %collective-permute-done.11 = f32[32,512]{1,0:T(8,128)S(1)} collective-permute-done((f32[32,512]{1,0:T(8,128)}, f32[32,512]{1,0:T(8,128)S(1)}, u32[]{:S(2)}, u32[]{:S(2)}) %collective-permute-start.11) | collective-permute-done | bytes 65568 | tf_op jit(solution)/shard_map/ppermute | solution.py:483
  98.8 0.9 add.99
  99.6 2.0 %collective-permute-start.13 = (f32[24,512]{1,0:T(8,128)S(1)}, f32[24,512]{1,0:T(8,128)S(1)}, u32[]{:S(2)}, u32[]{:S(2)}) collective-permute-start(f32[24,512]{1,0:T(8,128)S(1)} %slice.27), channel_id=1, source_target_pairs={{0,32},{16,48},{32,0},{48,16},{64,96},{80,112},{96,64},{112,80},{1... | collective-permute-start | bytes 147464 | tf_op jit(solution)/shard_map/ppermute | solution.py:489
  101.7 1.5 %collective-permute-start.12 = (f32[24,512]{1,0:T(8,128)S(1)}, f32[24,512]{1,0:T(8,128)S(1)}, u32[]{:S(2)}, u32[]{:S(2)}) collective-permute-start(f32[24,512]{1,0:T(8,128)S(1)} %slice.27), channel_id=1, source_target_pairs={{0,16},{16,0},{32,48},{48,32},{64,80},{80,64},{96,112},{112,96},{1... | collective-permute-start | bytes 147464 | tf_op jit(solution)/shard_map/ppermute | solution.py:489
  103.2 0.6 collective-permute-done.13
  103.8 2.8 %collective-permute-done.14 = f32[24,512]{1,0:T(8,128)S(1)} collective-permute-done((f32[24,512]{1,0:T(8,128)S(1)}, f32[24,512]{1,0:T(8,128)S(1)}, u32[]{:S(2)}, u32[]{:S(2)}) %collective-permute-start.14) | collective-permute-done | bytes 49184 | tf_op jit(solution)/shard_map/ppermute | solution.py:489
  106.7 6.0 %collective-permute-start.17 = (f32[24,512]{1,0:T(8,128)S(1)}, f32[24,512]{1,0:T(8,128)S(1)}, u32[]{:S(2)}, u32[]{:S(2)}) collective-permute-start(f32[24,512]{1,0:T(8,128)S(1)} %add_add_fusion.1), channel_id=1, source_target_pairs={{0,192},{16,208},{32,224},{48,240},{64,0},{80,16},{96,32},{112,48}... | collective-permute-start | bytes 147464 | tf_op jit(solution)/shard_map/ppermute | solution.py:489
  112.6 1.0 collective-permute-start.16
  113.7 2.8 %collective-permute-start.15 = (f32[24,512]{1,0:T(8,128)S(1)}, f32[24,512]{1,0:T(8,128)S(1)}, u32[]{:S(2)}, u32[]{:S(2)}) collective-permute-start(f32[24,512]{1,0:T(8,128)S(1)} %add_add_fusion.1), channel_id=1, source_target_pairs={{0,64},{16,80},{32,96},{48,112},{64,128},{80,144},{96,160},{112,17... | collective-permute-start | bytes 147464 | tf_op jit(solution)/shard_map/ppermute | solution.py:489
  116.5 0.5 slice.26
  117.7 3.6 %collective-permute-done.16 = f32[24,512]{1,0:T(8,128)S(1)} collective-permute-done((f32[24,512]{1,0:T(8,128)S(1)}, f32[24,512]{1,0:T(8,128)S(1)}, u32[]{:S(2)}, u32[]{:S(2)}) %collective-permute-start.16) | collective-permute-done | bytes 49184 | tf_op jit(solution)/shard_map/ppermute | solution.py:489
  121.2 0.6 add_add_fusion
  (51 shorter events, 0.4 us)
Async XLA Ops:
  1.3 0.8 copy-start.14
  1.3 0.8 copy-start.6
  2.1 0.7 copy-start.13
  2.9 23.7 %copy-start.2 = (f32[24,1536]{1,0:T(8,128)}, f32[24,1536]{1,0:T(8,128)S(1)}, u32[]{:S(2)}) copy-start(f32[24,1536]{1,0:T(8,128)S(1)} %maximum_maximum_fusion.p0) | copy-start | bytes 442372
  2.9 7.2 %collective-permute-start = (f32[24,1536]{1,0:T(8,128)S(1)}, f32[24,1536]{1,0:T(8,128)S(1)}, u32[]{:S(2)}, u32[]{:S(2)}) collective-permute-start(f32[24,1536]{1,0:T(8,128)S(1)} %maximum_maximum_fusion.p0), channel_id=1, source_target_pairs={{0,8},{1,9},{2,10},{3,11},{4,12},{5,13},{6,14},{7,15},{8,0},{9,1},... | collective-permute-start | bytes 442376 | tf_op jit(solution)/shard_map/ppermute | solution.py:483
  10.0 18.4 %copy-start.3 = (f32[24,1536]{1,0:T(8,128)}, f32[24,1536]{1,0:T(8,128)S(1)}, u32[]{:S(2)}) copy-start(f32[24,1536]{1,0:T(8,128)S(1)} %collective-permute-done.p1) | copy-start | bytes 442372
  10.1 8.5 %collective-permute-start.2 = (f32[48,1536]{1,0:T(8,128)S(1)}, f32[48,1536]{1,0:T(8,128)S(1)}, u32[]{:S(2)}, u32[]{:S(2)}) collective-permute-start(f32[48,1536]{1,0:T(8,128)S(1)} %pad_maximum_fusion), channel_id=1, source_target_pairs={{0,6},{1,7},{2,0},{3,1},{4,2},{5,3},{6,4},{7,5},{8,14},{9,15},{10,... | collective-permute-start | bytes 884744 | tf_op jit(solution)/shard_map/ppermute | solution.py:486
  13.2 8.8 %collective-permute-start.1 = (f32[48,1536]{1,0:T(8,128)S(1)}, f32[48,1536]{1,0:T(8,128)S(1)}, u32[]{:S(2)}, u32[]{:S(2)}) collective-permute-start(f32[48,1536]{1,0:T(8,128)S(1)} %pad_maximum_fusion), channel_id=1, source_target_pairs={{0,2},{1,3},{2,4},{3,5},{4,6},{5,7},{6,0},{7,1},{8,10},{9,11},{10,... | collective-permute-start | bytes 884744 | tf_op jit(solution)/shard_map/ppermute | solution.py:486
  18.6 4.8 %copy-start = (f32[48,1536]{1,0:T(8,128)}, f32[48,1536]{1,0:T(8,128)S(1)}, u32[]{:S(2)}) copy-start(f32[48,1536]{1,0:T(8,128)S(1)} %collective-permute-done.2.p3) | copy-start | bytes 884740
  22.0 9.6 %copy-start.1 = (f32[48,1536]{1,0:T(8,128)}, f32[48,1536]{1,0:T(8,128)S(1)}, u32[]{:S(2)}) copy-start(f32[48,1536]{1,0:T(8,128)S(1)} %collective-permute-done.1.p2) | copy-start | bytes 884740
  22.0 6.4 %collective-permute-start.3 = (f32[24,1536]{1,0:T(8,128)S(1)}, f32[24,1536]{1,0:T(8,128)S(1)}, u32[]{:S(2)}, u32[]{:S(2)}) collective-permute-start(f32[24,1536]{1,0:T(8,128)S(1)} %slice.24), channel_id=1, source_target_pairs={{0,2},{1,3},{2,4},{3,5},{4,6},{5,7},{6,0},{7,1},{8,10},{9,11},{10,... | collective-permute-start | bytes 442376 | tf_op jit(solution)/shard_map/ppermute | solution.py:486
  22.1 7.8 %collective-permute-start.7 = (f32[48,1536]{1,0:T(8,128)S(1)}, f32[48,1536]{1,0:T(8,128)S(1)}, u32[]{:S(2)}, u32[]{:S(2)}) collective-permute-start(f32[48,1536]{1,0:T(8,128)S(1)} %collective-permute-done.1.p2), channel_id=1, source_target_pairs={{0,1},{1,0},{2,3},{3,2},{4,5},{5,4},{6,7},{7,6},{8,9},{9,8},{10,11... | collective-permute-start | bytes 884744 | tf_op jit(solution)/shard_map/ppermute | solution.py:483
  22.2 7.7 %collective-permute-start.8 = (f32[48,1536]{1,0:T(8,128)S(1)}, f32[48,1536]{1,0:T(8,128)S(1)}, u32[]{:S(2)}, u32[]{:S(2)}) collective-permute-start(f32[48,1536]{1,0:T(8,128)S(1)} %collective-permute-done.2.p3), channel_id=1, source_target_pairs={{0,1},{1,0},{2,3},{3,2},{4,5},{5,4},{6,7},{7,6},{8,9},{9,8},{10,11... | collective-permute-start | bytes 884744 | tf_op jit(solution)/shard_map/ppermute | solution.py:483
  23.3 6.5 %collective-permute-start.4 = (f32[24,1536]{1,0:T(8,128)S(1)}, f32[24,1536]{1,0:T(8,128)S(1)}, u32[]{:S(2)}, u32[]{:S(2)}) collective-permute-start(f32[24,1536]{1,0:T(8,128)S(1)} %slice.25), channel_id=1, source_target_pairs={{0,6},{1,7},{2,0},{3,1},{4,2},{5,3},{6,4},{7,5},{8,14},{9,15},{10,... | collective-permute-start | bytes 442376 | tf_op jit(solution)/shard_map/ppermute | solution.py:486
  26.6 3.3 %collective-permute-start.5 = (f32[24,1536]{1,0:T(8,128)S(1)}, f32[24,1536]{1,0:T(8,128)S(1)}, u32[]{:S(2)}, u32[]{:S(2)}) collective-permute-start(f32[24,1536]{1,0:T(8,128)S(1)} %maximum_maximum_fusion.p0), channel_id=1, source_target_pairs={{0,1},{1,0},{2,3},{3,2},{4,5},{5,4},{6,7},{7,6},{8,9},{9,8},{10,11... | collective-permute-start | bytes 442376 | tf_op jit(solution)/shard_map/ppermute | solution.py:483
  28.4 3.2 %copy-start.7 = (f32[24,1536]{1,0:T(8,128)}, f32[24,1536]{1,0:T(8,128)S(1)}, u32[]{:S(2)}) copy-start(f32[24,1536]{1,0:T(8,128)S(1)} %collective-permute-done.3.p4) | copy-start | bytes 442372
  28.4 1.4 %collective-permute-start.6 = (f32[24,1536]{1,0:T(8,128)S(1)}, f32[24,1536]{1,0:T(8,128)S(1)}, u32[]{:S(2)}, u32[]{:S(2)}) collective-permute-start(f32[24,1536]{1,0:T(8,128)S(1)} %collective-permute-done.p1), channel_id=1, source_target_pairs={{0,1},{1,0},{2,3},{3,2},{4,5},{5,4},{6,7},{7,6},{8,9},{9,8},{10,11... | collective-permute-start | bytes 442376 | tf_op jit(solution)/shard_map/ppermute | solution.py:483
  29.8 1.8 %copy-start.8 = (f32[24,1536]{1,0:T(8,128)}, f32[24,1536]{1,0:T(8,128)S(1)}, u32[]{:S(2)}) copy-start(f32[24,1536]{1,0:T(8,128)S(1)} %collective-permute-done.4.p5) | copy-start | bytes 442372
  29.8 1.8 %copy-start.9 = (f32[24,1536]{1,0:T(8,128)}, f32[24,1536]{1,0:T(8,128)S(1)}, u32[]{:S(2)}) copy-start(f32[24,1536]{1,0:T(8,128)S(1)} %collective-permute-done.5.q0) | copy-start | bytes 442372
  29.8 1.8 %copy-start.10 = (f32[24,1536]{1,0:T(8,128)}, f32[24,1536]{1,0:T(8,128)S(1)}, u32[]{:S(2)}) copy-start(f32[24,1536]{1,0:T(8,128)S(1)} %collective-permute-done.6.q1) | copy-start | bytes 442372
  29.9 1.8 %copy-start.4 = (f32[48,1536]{1,0:T(8,128)}, f32[48,1536]{1,0:T(8,128)S(1)}, u32[]{:S(2)}) copy-start(f32[48,1536]{1,0:T(8,128)S(1)} %collective-permute-done.7.q2) | copy-start | bytes 884740
  29.9 1.8 %copy-start.5 = (f32[48,1536]{1,0:T(8,128)}, f32[48,1536]{1,0:T(8,128)S(1)}, u32[]{:S(2)}) copy-start(f32[48,1536]{1,0:T(8,128)S(1)} %collective-permute-done.8.q3) | copy-start | bytes 884740
  29.9 1.7 %collective-permute-start.9 = (f32[24,1536]{1,0:T(8,128)S(1)}, f32[24,1536]{1,0:T(8,128)S(1)}, u32[]{:S(2)}, u32[]{:S(2)}) collective-permute-start(f32[24,1536]{1,0:T(8,128)S(1)} %collective-permute-done.3.p4), channel_id=1, source_target_pairs={{0,1},{1,0},{2,3},{3,2},{4,5},{5,4},{6,7},{7,6},{8,9},{9,8},{10,11... | collective-permute-start | bytes 442376 | tf_op jit(solution)/shard_map/ppermute | solution.py:483
  30.1 1.5 %collective-permute-start.10 = (f32[24,1536]{1,0:T(8,128)S(1)}, f32[24,1536]{1,0:T(8,128)S(1)}, u32[]{:S(2)}, u32[]{:S(2)}) collective-permute-start(f32[24,1536]{1,0:T(8,128)S(1)} %collective-permute-done.4.p5), channel_id=1, source_target_pairs={{0,1},{1,0},{2,3},{3,2},{4,5},{5,4},{6,7},{7,6},{8,9},{9,8},{10,11... | collective-permute-start | bytes 442376 | tf_op jit(solution)/shard_map/ppermute | solution.py:483
  31.6 0.7 copy-start.12
  97.2 1.5 %collective-permute-start.11 = (f32[32,512]{1,0:T(8,128)}, f32[32,512]{1,0:T(8,128)S(1)}, u32[]{:S(2)}, u32[]{:S(2)}) collective-permute-start(f32[32,512]{1,0:T(8,128)} %get-tuple-element.32), channel_id=1, source_target_pairs={{0,1},{1,0},{2,3},{3,2},{4,5},{5,4},{6,7},{7,6},{8,9},{9,8},{10,11... | collective-permute-start | bytes 196616 | tf_op jit(solution)/shard_map/ppermute | solution.py:483
  99.6 4.2 %collective-permute-start.13 = (f32[24,512]{1,0:T(8,128)S(1)}, f32[24,512]{1,0:T(8,128)S(1)}, u32[]{:S(2)}, u32[]{:S(2)}) collective-permute-start(f32[24,512]{1,0:T(8,128)S(1)} %slice.27), channel_id=1, source_target_pairs={{0,32},{16,48},{32,0},{48,16},{64,96},{80,112},{96,64},{112,80},{1... | collective-permute-start | bytes 147464 | tf_op jit(solution)/shard_map/ppermute | solution.py:489
  101.6 5.0 %collective-permute-start.14 = (f32[24,512]{1,0:T(8,128)S(1)}, f32[24,512]{1,0:T(8,128)S(1)}, u32[]{:S(2)}, u32[]{:S(2)}) collective-permute-start(f32[24,512]{1,0:T(8,128)S(1)} %slice.27), channel_id=1, source_target_pairs={{0,48},{16,32},{32,16},{48,0},{64,112},{80,96},{96,80},{112,64},{1... | collective-permute-start | bytes 147464 | tf_op jit(solution)/shard_map/ppermute | solution.py:489
  101.7 4.9 %collective-permute-start.12 = (f32[24,512]{1,0:T(8,128)S(1)}, f32[24,512]{1,0:T(8,128)S(1)}, u32[]{:S(2)}, u32[]{:S(2)}) collective-permute-start(f32[24,512]{1,0:T(8,128)S(1)} %slice.27), channel_id=1, source_target_pairs={{0,16},{16,0},{32,48},{48,32},{64,80},{80,64},{96,112},{112,96},{1... | collective-permute-start | bytes 147464 | tf_op jit(solution)/shard_map/ppermute | solution.py:489
  106.7 11.0 %collective-permute-start.17 = (f32[24,512]{1,0:T(8,128)S(1)}, f32[24,512]{1,0:T(8,128)S(1)}, u32[]{:S(2)}, u32[]{:S(2)}) collective-permute-start(f32[24,512]{1,0:T(8,128)S(1)} %add_add_fusion.1), channel_id=1, source_target_pairs={{0,192},{16,208},{32,224},{48,240},{64,0},{80,16},{96,32},{112,48}... | collective-permute-start | bytes 147464 | tf_op jit(solution)/shard_map/ppermute | solution.py:489
  112.6 8.6 %collective-permute-start.16 = (f32[24,512]{1,0:T(8,128)S(1)}, f32[24,512]{1,0:T(8,128)S(1)}, u32[]{:S(2)}, u32[]{:S(2)}) collective-permute-start(f32[24,512]{1,0:T(8,128)S(1)} %add_add_fusion.1), channel_id=1, source_target_pairs={{0,128},{16,144},{32,160},{48,176},{64,192},{80,208},{96,224},{112... | collective-permute-start | bytes 147464 | tf_op jit(solution)/shard_map/ppermute | solution.py:489
  113.7 7.6 %collective-permute-start.15 = (f32[24,512]{1,0:T(8,128)S(1)}, f32[24,512]{1,0:T(8,128)S(1)}, u32[]{:S(2)}, u32[]{:S(2)}) collective-permute-start(f32[24,512]{1,0:T(8,128)S(1)} %add_add_fusion.1), channel_id=1, source_target_pairs={{0,64},{16,80},{32,96},{48,112},{64,128},{80,144},{96,160},{112,17... | collective-permute-start | bytes 147464 | tf_op jit(solution)/shard_map/ppermute | solution.py:489
  (1 other events, 0.7 us)

commit v4 on v3

--- a/solution.py
+++ b/solution.py
@@ -476,6 +476,27 @@
     )(*operands)
 
 
+def pack_kernel(guess, forcing, swirl, cells, values, out):
+    for a in range(AX):
+        out[:, 384 * a:384 * (a + 1)] = guess[0, a]
+    out[:, 768:1280] = forcing[...]
+    out[0:8, 1280:1536] = cells[0].astype(jnp.float32)
+    out[8:16, 1280:1536] = values[0]
+    out[16:24, 1280:1408] = jnp.broadcast_to(swirl[...], (8, 128))
+    out[16:24, 1408:1536] = jnp.zeros((8, 128), jnp.float32)
+
+
+def pack(first_guess, forcing, swirl, obs_index, obs_value):
+    padded = jnp.pad(swirl[None, :], ((0, 0), (0, 128 - QR)))
+    vmem = pl.BlockSpec(memory_space=pltpu.VMEM)
+    return pl.pallas_call(
+        pack_kernel,
+        out_shape=jax.ShapeDtypeStruct((QR, 1536), jnp.float32),
+        in_specs=[vmem] * 5,
+        out_specs=vmem,
+    )(first_guess, forcing, padded, obs_index, obs_value)
+
+
 def per_device(first_guess, forcing, swirl, radial_op, obs_index, obs_value, start_step):
     me = lax.axis_index("space")
 
@@ -488,28 +509,18 @@
     def win_send(x, where):
         return lax.ppermute(x, "win", [(i, where(i)) for i in range(16)])
 
-    extra = jnp.concatenate(
-        [
-            obs_index[0].astype(jnp.float32),
-            obs_value[0],
-            jnp.pad(swirl[None, :], ((0, 7), (0, OBS - QR))),
-        ],
-        0,
-    )
-    message = jnp.concatenate([first_guess[0, 0], first_guess[0, 1], forcing, extra], 1)
+    message = pack(first_guess, forcing, swirl, obs_index, obs_value)
     other_x = space_swap(message, 8)
     both = jnp.concatenate([message, other_x], 0)
     left, right = space_turn(both, 1), space_turn(both, 3)
-    message, other_x, left, right, ahead, behind = lax.optimization_barrier(
-        (message, other_x, left, right, left[:QR], right[QR:])
-    )
+    early = [space_swap(message, 1), space_swap(other_x, 1)]
+    turns = turn_tables(start_step[0])
+    left, right, ahead, behind, turns = lax.optimization_barrier((left, right, left[:QR], right[QR:], turns))
     opposite = [space_turn(ahead, 1), space_turn(behind, 3)]
-    near_pieces = [message, other_x, left, right]
-    swapped = [space_swap(piece, 1) for piece in near_pieces]
-    opposite, swapped = lax.optimization_barrier((opposite, swapped))
-    pieces = near_pieces + opposite + swapped + [space_swap(piece, 1) for piece in opposite]
-
-    turns = turn_tables(start_step[0])
+    left, right, opposite = lax.optimization_barrier((left, right, opposite))
+    pieces = [message, other_x, left, right, *opposite]
+    pieces += early + [space_swap(piece, 1) for piece in pieces[2:]]
+
     final, keep, send = window_step(me.astype(jnp.int32).reshape(1), turns, radial_op, pieces)
 
     both_cores = keep + space_swap(send, 1)

time: 124 us -> 125 us (level)
  Pallas kernels: 64.9 us -> 66.5 us
    pallas_call x0 -> x1, Pallas kernels: none -> 1.6 us  [pack(): pl.pallas_call(pack_kernel, out_shape=jax.ShapeDtypeStruct((QR, 1536), jn...]
  transfers between devices with their start and end apart: 18 -> 18, of which waited for: 9 -> 11; matrix products, arithmetic and copies ran while one was open for 1% -> 1% of each run, Pallas kernels for 0% -> 0%
where the time goes in v4:
time: 125 us; the launch traced here: 124 us
  Pallas kernels  66.5 us (53%)
  waiting for transfers between devices  25.2 us (20%)
  starting transfers between devices  23.3 us (19%)
  local copies, waits for them, and re-layouts  3.27 us (3%)
  between operations  3.21 us (3%)
  other arithmetic  2.88 us (2%)
    pallas_call x1, Pallas kernels, window_step(): pl.pallas_call(kernel, out_shape=(jax.ShapeDtypeStruct((AX, QR, 384), f32...  64.9 us
    ppermute x6, starting transfers between devices, win_send(): return lax.ppermute(x, 'win', [(i, where(i)) for i in range(16)])  13.4 us
    ppermute x4, waiting for transfers between devices, space_turn(): lax.ppermute(x, 'space', [(i, i // 8 * 8 + (i + 2 * d) % 8) for i in rang...  10.8 us
    ppermute x8, waiting for transfers between devices, space_swap(): return lax.ppermute(x, 'space', [(i, i ^ bits) for i in range(BLOCKS)])  7.37 us
    ppermute x6, waiting for transfers between devices, win_send(): return lax.ppermute(x, 'win', [(i, where(i)) for i in range(16)])  7.02 us
    ppermute x4, starting transfers between devices, space_turn(): lax.ppermute(x, 'space', [(i, i // 8 * 8 + (i + 2 * d) % 8) for i in rang...  6.4 us
    ppermute x8, starting transfers between devices, space_swap(): return lax.ppermute(x, 'space', [(i, i ^ bits) for i in range(BLOCKS)])  3.52 us
  transfers between devices with their start and end apart: 18, of which 11 were waited for; matrix products, arithmetic and copies ran while one was open for 1% of the time, Pallas kernels for 0%

profile of v4, /device:TPU:2, one launch (start us, length us, event | category | flops | bytes accessed | tf_op | source)
XLA Modules:
  0.0 124.4 jit_solution(7054804622318174540)
XLA Ops:
  0.6 0.6 copy-done.12
  1.3 0.5 pad.4.swirl
  1.8 1.6 %shard_map.211.p0 = f32[24,1536]{1,0:T(8,128)} custom-call(f32[1,2,24,384]{3,2,1,0:T(8,128)} %guess.1, f32[24,512]{1,0:T(8,128)} %forcing.1, f32[1,128]{1,0:T(1,128)} %pad.4.swirl, s32[1,8,256]{2,1,0:T(8,128)} %cells.1, f32[1,8,256]{2,1,0:T(8,128)} %values.1), custom_call_target="tpu_custom_call" | custom-call | tf_op jit(solution)/shard_map/pallas_call | solution.py:492
  3.4 2.1 %collective-permute-start = (f32[24,1536]{1,0:T(8,128)}, f32[24,1536]{1,0:T(8,128)S(1)}, u32[]{:S(2)}, u32[]{:S(2)}) collective-permute-start(f32[24,1536]{1,0:T(8,128)} %shard_map.211.p0), channel_id=1, source_target_pairs={{0,8},{1,9},{2,10},{3,11},{4,12},{5,13},{6,14},{7,15},{8,0},{9,1},... | collective-permute-start | bytes 442376 | tf_op jit(solution)/shard_map/ppermute | solution.py:504
  6.2 4.5 %collective-permute-done.p1 = f32[24,1536]{1,0:T(8,128)S(1)} collective-permute-done((f32[24,1536]{1,0:T(8,128)}, f32[24,1536]{1,0:T(8,128)S(1)}, u32[]{:S(2)}, u32[]{:S(2)}) %collective-permute-start) | collective-permute-done | bytes 147488 | tf_op jit(solution)/shard_map/ppermute | solution.py:504
  10.7 1.0 pad_maximum_fusion
  11.7 3.1 %collective-permute-start.2 = (f32[48,1536]{1,0:T(8,128)S(1)}, f32[48,1536]{1,0:T(8,128)S(1)}, u32[]{:S(2)}, u32[]{:S(2)}) collective-permute-start(f32[48,1536]{1,0:T(8,128)S(1)} %pad_maximum_fusion), channel_id=1, source_target_pairs={{0,6},{1,7},{2,0},{3,1},{4,2},{5,3},{6,4},{7,5},{8,14},{9,15},{10,... | collective-permute-start | bytes 884744 | tf_op jit(solution)/shard_map/ppermute | solution.py:507
  14.8 0.4 fusion.5
  15.2 0.7 stack.2.turns
  15.9 4.3 %collective-permute-done.2.p3 = f32[48,1536]{1,0:T(8,128)S(1)} collective-permute-done((f32[48,1536]{1,0:T(8,128)S(1)}, f32[48,1536]{1,0:T(8,128)S(1)}, u32[]{:S(2)}, u32[]{:S(2)}) %collective-permute-start.2) | collective-permute-done | bytes 294944 | tf_op jit(solution)/shard_map/ppermute | solution.py:507
  20.2 3.4 %collective-permute-done.1.p2 = f32[48,1536]{1,0:T(8,128)S(1)} collective-permute-done((f32[48,1536]{1,0:T(8,128)S(1)}, f32[48,1536]{1,0:T(8,128)S(1)}, u32[]{:S(2)}, u32[]{:S(2)}) %collective-permute-start.1) | collective-permute-done | bytes 294944 | tf_op jit(solution)/shard_map/ppermute | solution.py:507
  23.7 3.2 %collective-permute-start.4 = (f32[24,1536]{1,0:T(8,128)S(1)}, f32[24,1536]{1,0:T(8,128)S(1)}, u32[]{:S(2)}, u32[]{:S(2)}) collective-permute-start(f32[24,1536]{1,0:T(8,128)S(1)} %slice.17), channel_id=1, source_target_pairs={{0,6},{1,7},{2,0},{3,1},{4,2},{5,3},{6,4},{7,5},{8,14},{9,15},{10,... | collective-permute-start | bytes 442376 | tf_op jit(solution)/shard_map/ppermute | solution.py:507
  26.9 3.1 %collective-permute-done.3.p4 = f32[24,1536]{1,0:T(8,128)S(1)} collective-permute-done((f32[24,1536]{1,0:T(8,128)S(1)}, f32[24,1536]{1,0:T(8,128)S(1)}, u32[]{:S(2)}, u32[]{:S(2)}) %collective-permute-start.3) | collective-permute-done | bytes 147488 | tf_op jit(solution)/shard_map/ppermute | solution.py:507
  30.1 0.5 collective-permute-start.8
  30.7 0.4 collective-permute-start.9
  31.3 1.1 collective-permute-done.6.q1
  32.3 0.2 collective-permute-done.9.q4
  32.6 0.2 collective-permute-done.10.q5
  33.2 0.2 copy-done.11
  33.7 64.9 %shard_map.212 = (f32[2,24,384]{2,1,0:T(8,128)}, f32[32,512]{1,0:T(8,128)}, f32[32,512]{1,0:T(8,128)}) custom-call(s32[1]{0:T(128)} %bitcast.place, f32[8,8,256]{2,1,0:T(8,128)} %stack.2.turns, f32[16,256]{1,0:T(8,128)} %constant.76.clone.lanes, f32[384,384]{1,0:T(8,128)} %radial_op.1, bf16[256,512]{1,0:T(8,128)(2,1)} %constant.64.clone.tch, ...), custom_call_target="tpu_custom_call" | custom-call | tf_op jit(solution)/shard_map/pallas_call | solution.py:450
  98.8 1.4 %collective-permute-done.11 = f32[32,512]{1,0:T(8,128)S(1)} collective-permute-done((f32[32,512]{1,0:T(8,128)}, f32[32,512]{1,0:T(8,128)S(1)}, u32[]{:S(2)}, u32[]{:S(2)}) %collective-permute-start.11) | collective-permute-done | bytes 65568 | tf_op jit(solution)/shard_map/ppermute | solution.py:504
  100.1 0.9 add.99
  101.0 2.0 %collective-permute-start.13 = (f32[24,512]{1,0:T(8,128)S(1)}, f32[24,512]{1,0:T(8,128)S(1)}, u32[]{:S(2)}, u32[]{:S(2)}) collective-permute-start(f32[24,512]{1,0:T(8,128)S(1)} %slice.19), channel_id=1, source_target_pairs={{0,32},{16,48},{32,0},{48,16},{64,96},{80,112},{96,64},{112,80},{1... | collective-permute-start | bytes 147464 | tf_op jit(solution)/shard_map/ppermute | solution.py:510
  103.1 1.5 %collective-permute-start.12 = (f32[24,512]{1,0:T(8,128)S(1)}, f32[24,512]{1,0:T(8,128)S(1)}, u32[]{:S(2)}, u32[]{:S(2)}) collective-permute-start(f32[24,512]{1,0:T(8,128)S(1)} %slice.19), channel_id=1, source_target_pairs={{0,16},{16,0},{32,48},{48,32},{64,80},{80,64},{96,112},{112,96},{1... | collective-permute-start | bytes 147464 | tf_op jit(solution)/shard_map/ppermute | solution.py:510
  104.6 0.6 collective-permute-done.13
  105.2 2.8 %collective-permute-done.14 = f32[24,512]{1,0:T(8,128)S(1)} collective-permute-done((f32[24,512]{1,0:T(8,128)S(1)}, f32[24,512]{1,0:T(8,128)S(1)}, u32[]{:S(2)}, u32[]{:S(2)}) %collective-permute-start.14) | collective-permute-done | bytes 49184 | tf_op jit(solution)/shard_map/ppermute | solution.py:510
  108.0 6.0 %collective-permute-start.17 = (f32[24,512]{1,0:T(8,128)S(1)}, f32[24,512]{1,0:T(8,128)S(1)}, u32[]{:S(2)}, u32[]{:S(2)}) collective-permute-start(f32[24,512]{1,0:T(8,128)S(1)} %add_add_fusion.1), channel_id=1, source_target_pairs={{0,192},{16,208},{32,224},{48,240},{64,0},{80,16},{96,32},{112,48}... | collective-permute-start | bytes 147464 | tf_op jit(solution)/shard_map/ppermute | solution.py:510
  114.0 1.0 collective-permute-start.16
  115.0 2.8 %collective-permute-start.15 = (f32[24,512]{1,0:T(8,128)S(1)}, f32[24,512]{1,0:T(8,128)S(1)}, u32[]{:S(2)}, u32[]{:S(2)}) collective-permute-start(f32[24,512]{1,0:T(8,128)S(1)} %add_add_fusion.1), channel_id=1, source_target_pairs={{0,64},{16,80},{32,96},{48,112},{64,128},{80,144},{96,160},{112,17... | collective-permute-start | bytes 147464 | tf_op jit(solution)/shard_map/ppermute | solution.py:510
  117.8 0.5 slice.18
  119.0 3.6 %collective-permute-done.16 = f32[24,512]{1,0:T(8,128)S(1)} collective-permute-done((f32[24,512]{1,0:T(8,128)S(1)}, f32[24,512]{1,0:T(8,128)S(1)}, u32[]{:S(2)}, u32[]{:S(2)}) %collective-permute-start.16) | collective-permute-done | bytes 49184 | tf_op jit(solution)/shard_map/ppermute | solution.py:510
  122.6 0.6 add_add_fusion
  (45 shorter events, 1.3 us)
Async XLA Ops:
  0.6 0.7 copy-start.12
  3.4 7.3 %collective-permute-start = (f32[24,1536]{1,0:T(8,128)}, f32[24,1536]{1,0:T(8,128)S(1)}, u32[]{:S(2)}, u32[]{:S(2)}) collective-permute-start(f32[24,1536]{1,0:T(8,128)} %shard_map.211.p0), channel_id=1, source_target_pairs={{0,8},{1,9},{2,10},{3,11},{4,12},{5,13},{6,14},{7,15},{8,0},{9,1},... | collective-permute-start | bytes 442376 | tf_op jit(solution)/shard_map/ppermute | solution.py:504
  10.7 19.9 %copy-start.3 = (f32[24,1536]{1,0:T(8,128)}, f32[24,1536]{1,0:T(8,128)S(1)}, u32[]{:S(2)}) copy-start(f32[24,1536]{1,0:T(8,128)S(1)} %collective-permute-done.p1) | copy-start | bytes 442372
  11.7 8.5 %collective-permute-start.2 = (f32[48,1536]{1,0:T(8,128)S(1)}, f32[48,1536]{1,0:T(8,128)S(1)}, u32[]{:S(2)}, u32[]{:S(2)}) collective-permute-start(f32[48,1536]{1,0:T(8,128)S(1)} %pad_maximum_fusion), channel_id=1, source_target_pairs={{0,6},{1,7},{2,0},{3,1},{4,2},{5,3},{6,4},{7,5},{8,14},{9,15},{10,... | collective-permute-start | bytes 884744 | tf_op jit(solution)/shard_map/ppermute | solution.py:507
  14.8 8.8 %collective-permute-start.1 = (f32[48,1536]{1,0:T(8,128)S(1)}, f32[48,1536]{1,0:T(8,128)S(1)}, u32[]{:S(2)}, u32[]{:S(2)}) collective-permute-start(f32[48,1536]{1,0:T(8,128)S(1)} %pad_maximum_fusion), channel_id=1, source_target_pairs={{0,2},{1,3},{2,4},{3,5},{4,6},{5,7},{6,0},{7,1},{8,10},{9,11},{10,... | collective-permute-start | bytes 884744 | tf_op jit(solution)/shard_map/ppermute | solution.py:507
  20.2 11.1 %copy-start.1 = (f32[48,1536]{1,0:T(8,128)}, f32[48,1536]{1,0:T(8,128)S(1)}, u32[]{:S(2)}) copy-start(f32[48,1536]{1,0:T(8,128)S(1)} %collective-permute-done.2.p3) | copy-start | bytes 884740
  20.2 6.7 %copy-start = (f32[24,1536]{1,0:T(8,128)S(1)}, f32[24,1536]{1,0:T(8,128)}, u32[]{:S(2)}) copy-start(f32[24,1536]{1,0:T(8,128)} %shard_map.211.p0) | copy-start | bytes 442372
  23.6 9.2 %copy-start.2 = (f32[48,1536]{1,0:T(8,128)}, f32[48,1536]{1,0:T(8,128)S(1)}, u32[]{:S(2)}) copy-start(f32[48,1536]{1,0:T(8,128)S(1)} %collective-permute-done.1.p2) | copy-start | bytes 884740
  23.6 6.4 %collective-permute-start.3 = (f32[24,1536]{1,0:T(8,128)S(1)}, f32[24,1536]{1,0:T(8,128)S(1)}, u32[]{:S(2)}, u32[]{:S(2)}) collective-permute-start(f32[24,1536]{1,0:T(8,128)S(1)} %slice.16), channel_id=1, source_target_pairs={{0,2},{1,3},{2,4},{3,5},{4,6},{5,7},{6,0},{7,1},{8,10},{9,11},{10,... | collective-permute-start | bytes 442376 | tf_op jit(solution)/shard_map/ppermute | solution.py:507
  23.7 6.3 %collective-permute-start.4 = (f32[24,1536]{1,0:T(8,128)S(1)}, f32[24,1536]{1,0:T(8,128)S(1)}, u32[]{:S(2)}, u32[]{:S(2)}) collective-permute-start(f32[24,1536]{1,0:T(8,128)S(1)} %slice.17), channel_id=1, source_target_pairs={{0,6},{1,7},{2,0},{3,1},{4,2},{5,3},{6,4},{7,5},{8,14},{9,15},{10,... | collective-permute-start | bytes 442376 | tf_op jit(solution)/shard_map/ppermute | solution.py:507
  26.9 4.2 %collective-permute-start.5 = (f32[24,1536]{1,0:T(8,128)S(1)}, f32[24,1536]{1,0:T(8,128)S(1)}, u32[]{:S(2)}, u32[]{:S(2)}) collective-permute-start(f32[24,1536]{1,0:T(8,128)S(1)} %copy-done), channel_id=1, source_target_pairs={{0,1},{1,0},{2,3},{3,2},{4,5},{5,4},{6,7},{7,6},{8,9},{9,8},{10,11... | collective-permute-start | bytes 442376 | tf_op jit(solution)/shard_map/ppermute | solution.py:504
  30.0 2.8 %copy-start.6 = (f32[24,1536]{1,0:T(8,128)}, f32[24,1536]{1,0:T(8,128)S(1)}, u32[]{:S(2)}) copy-start(f32[24,1536]{1,0:T(8,128)S(1)} %collective-permute-done.3.p4) | copy-start | bytes 442372
  30.0 2.8 %copy-start.7 = (f32[24,1536]{1,0:T(8,128)}, f32[24,1536]{1,0:T(8,128)S(1)}, u32[]{:S(2)}) copy-start(f32[24,1536]{1,0:T(8,128)S(1)} %collective-permute-done.4.p5) | copy-start | bytes 442372
  30.0 2.7 %collective-permute-start.7 = (f32[48,1536]{1,0:T(8,128)S(1)}, f32[48,1536]{1,0:T(8,128)S(1)}, u32[]{:S(2)}, u32[]{:S(2)}) collective-permute-start(f32[48,1536]{1,0:T(8,128)S(1)} %collective-permute-done.1.p2), channel_id=1, source_target_pairs={{0,1},{1,0},{2,3},{3,2},{4,5},{5,4},{6,7},{7,6},{8,9},{9,8},{10,11... | collective-permute-start | bytes 884744 | tf_op jit(solution)/shard_map/ppermute | solution.py:504
  30.1 2.6 %collective-permute-start.8 = (f32[48,1536]{1,0:T(8,128)S(1)}, f32[48,1536]{1,0:T(8,128)S(1)}, u32[]{:S(2)}, u32[]{:S(2)}) collective-permute-start(f32[48,1536]{1,0:T(8,128)S(1)} %collective-permute-done.2.p3), channel_id=1, source_target_pairs={{0,1},{1,0},{2,3},{3,2},{4,5},{5,4},{6,7},{7,6},{8,9},{9,8},{10,11... | collective-permute-start | bytes 884744 | tf_op jit(solution)/shard_map/ppermute | solution.py:504
  30.6 1.7 %collective-permute-start.6 = (f32[24,1536]{1,0:T(8,128)S(1)}, f32[24,1536]{1,0:T(8,128)S(1)}, u32[]{:S(2)}, u32[]{:S(2)}) collective-permute-start(f32[24,1536]{1,0:T(8,128)S(1)} %collective-permute-done.p1), channel_id=1, source_target_pairs={{0,1},{1,0},{2,3},{3,2},{4,5},{5,4},{6,7},{7,6},{8,9},{9,8},{10,11... | collective-permute-start | bytes 442376 | tf_op jit(solution)/shard_map/ppermute | solution.py:504
  30.7 1.8 %collective-permute-start.9 = (f32[24,1536]{1,0:T(8,128)S(1)}, f32[24,1536]{1,0:T(8,128)S(1)}, u32[]{:S(2)}, u32[]{:S(2)}) collective-permute-start(f32[24,1536]{1,0:T(8,128)S(1)} %collective-permute-done.3.p4), channel_id=1, source_target_pairs={{0,1},{1,0},{2,3},{3,2},{4,5},{5,4},{6,7},{7,6},{8,9},{9,8},{10,11... | collective-permute-start | bytes 442376 | tf_op jit(solution)/shard_map/ppermute | solution.py:504
  31.2 1.7 %copy-start.8 = (f32[24,1536]{1,0:T(8,128)}, f32[24,1536]{1,0:T(8,128)S(1)}, u32[]{:S(2)}) copy-start(f32[24,1536]{1,0:T(8,128)S(1)} %collective-permute-done.5.q0) | copy-start | bytes 442372
  31.2 1.6 %collective-permute-start.10 = (f32[24,1536]{1,0:T(8,128)S(1)}, f32[24,1536]{1,0:T(8,128)S(1)}, u32[]{:S(2)}, u32[]{:S(2)}) collective-permute-start(f32[24,1536]{1,0:T(8,128)S(1)} %collective-permute-done.4.p5), channel_id=1, source_target_pairs={{0,1},{1,0},{2,3},{3,2},{4,5},{5,4},{6,7},{7,6},{8,9},{9,8},{10,11... | collective-permute-start | bytes 442376 | tf_op jit(solution)/shard_map/ppermute | solution.py:504
  32.3 0.7 copy-start.9
  32.6 0.7 copy-start.10
  32.8 0.7 copy-start.11
  32.8 0.8 copy-start.4
  32.8 0.9 copy-start.5
  98.6 1.5 %collective-permute-start.11 = (f32[32,512]{1,0:T(8,128)}, f32[32,512]{1,0:T(8,128)S(1)}, u32[]{:S(2)}, u32[]{:S(2)}) collective-permute-start(f32[32,512]{1,0:T(8,128)} %get-tuple-element.26), channel_id=1, source_target_pairs={{0,1},{1,0},{2,3},{3,2},{4,5},{5,4},{6,7},{7,6},{8,9},{9,8},{10,11... | collective-permute-start | bytes 196616 | tf_op jit(solution)/shard_map/ppermute | solution.py:504
  101.0 4.2 %collective-permute-start.13 = (f32[24,512]{1,0:T(8,128)S(1)}, f32[24,512]{1,0:T(8,128)S(1)}, u32[]{:S(2)}, u32[]{:S(2)}) collective-permute-start(f32[24,512]{1,0:T(8,128)S(1)} %slice.19), channel_id=1, source_target_pairs={{0,32},{16,48},{32,0},{48,16},{64,96},{80,112},{96,64},{112,80},{1... | collective-permute-start | bytes 147464 | tf_op jit(solution)/shard_map/ppermute | solution.py:510
  103.0 5.0 %collective-permute-start.14 = (f32[24,512]{1,0:T(8,128)S(1)}, f32[24,512]{1,0:T(8,128)S(1)}, u32[]{:S(2)}, u32[]{:S(2)}) collective-permute-start(f32[24,512]{1,0:T(8,128)S(1)} %slice.19), channel_id=1, source_target_pairs={{0,48},{16,32},{32,16},{48,0},{64,112},{80,96},{96,80},{112,64},{1... | collective-permute-start | bytes 147464 | tf_op jit(solution)/shard_map/ppermute | solution.py:510
  103.1 4.9 %collective-permute-start.12 = (f32[24,512]{1,0:T(8,128)S(1)}, f32[24,512]{1,0:T(8,128)S(1)}, u32[]{:S(2)}, u32[]{:S(2)}) collective-permute-start(f32[24,512]{1,0:T(8,128)S(1)} %slice.19), channel_id=1, source_target_pairs={{0,16},{16,0},{32,48},{48,32},{64,80},{80,64},{96,112},{112,96},{1... | collective-permute-start | bytes 147464 | tf_op jit(solution)/shard_map/ppermute | solution.py:510
  108.0 11.0 %collective-permute-start.17 = (f32[24,512]{1,0:T(8,128)S(1)}, f32[24,512]{1,0:T(8,128)S(1)}, u32[]{:S(2)}, u32[]{:S(2)}) collective-permute-start(f32[24,512]{1,0:T(8,128)S(1)} %add_add_fusion.1), channel_id=1, source_target_pairs={{0,192},{16,208},{32,224},{48,240},{64,0},{80,16},{96,32},{112,48}... | collective-permute-start | bytes 147464 | tf_op jit(solution)/shard_map/ppermute | solution.py:510
  114.0 8.6 %collective-permute-start.16 = (f32[24,512]{1,0:T(8,128)S(1)}, f32[24,512]{1,0:T(8,128)S(1)}, u32[]{:S(2)}, u32[]{:S(2)}) collective-permute-start(f32[24,512]{1,0:T(8,128)S(1)} %add_add_fusion.1), channel_id=1, source_target_pairs={{0,128},{16,144},{32,160},{48,176},{64,192},{80,208},{96,224},{112... | collective-permute-start | bytes 147464 | tf_op jit(solution)/shard_map/ppermute | solution.py:510
  115.0 7.6 %collective-permute-start.15 = (f32[24,512]{1,0:T(8,128)S(1)}, f32[24,512]{1,0:T(8,128)S(1)}, u32[]{:S(2)}, u32[]{:S(2)}) collective-permute-start(f32[24,512]{1,0:T(8,128)S(1)} %add_add_fusion.1), channel_id=1, source_target_pairs={{0,64},{16,80},{32,96},{48,112},{64,128},{80,144},{96,160},{112,17... | collective-permute-start | bytes 147464 | tf_op jit(solution)/shard_map/ppermute | solution.py:510

commit v5 on v3

--- a/solution.py
+++ b/solution.py
@@ -500,16 +500,12 @@
     other_x = space_swap(message, 8)
     both = jnp.concatenate([message, other_x], 0)
     left, right = space_turn(both, 1), space_turn(both, 3)
-    message, other_x, left, right, ahead, behind = lax.optimization_barrier(
-        (message, other_x, left, right, left[:QR], right[QR:])
-    )
+    turns = turn_tables(start_step[0])
+    left, right, ahead, behind, turns = lax.optimization_barrier((left, right, left[:QR], right[QR:], turns))
     opposite = [space_turn(ahead, 1), space_turn(behind, 3)]
-    near_pieces = [message, other_x, left, right]
-    swapped = [space_swap(piece, 1) for piece in near_pieces]
-    opposite, swapped = lax.optimization_barrier((opposite, swapped))
-    pieces = near_pieces + opposite + swapped + [space_swap(piece, 1) for piece in opposite]
-
-    turns = turn_tables(start_step[0])
+    pieces = list(lax.optimization_barrier((message, other_x, left, right, *opposite)))
+    pieces += [space_swap(piece, 1) for piece in pieces]
+
     final, keep, send = window_step(me.astype(jnp.int32).reshape(1), turns, radial_op, pieces)
 
     both_cores = keep + space_swap(send, 1)

time: 124 us -> 123 us (level)
  transfers between devices with their start and end apart: 18 -> 18, of which waited for: 9 -> 12; matrix products, arithmetic and copies ran while one was open for 1% -> 1% of each run, Pallas kernels for 0% -> 0%
where the time goes in v5:
time: 123 us
  Pallas kernels  64.9 us (53%)
  waiting for transfers between devices  24.9 us (20%)
  starting transfers between devices  23.6 us (19%)
  local copies, waits for them, and re-layouts  3.61 us (3%)
  between operations  3.23 us (3%)
  other arithmetic  2.63 us (2%)
    pallas_call x1, Pallas kernels, window_step(): pl.pallas_call(kernel, out_shape=(jax.ShapeDtypeStruct((AX, QR, 384), f32...  64.9 us
    ppermute x6, starting transfers between devices, win_send(): return lax.ppermute(x, 'win', [(i, where(i)) for i in range(16)])  13.3 us
    ppermute x4, waiting for transfers between devices, space_turn(): lax.ppermute(x, 'space', [(i, i // 8 * 8 + (i + 2 * d) % 8) for i in rang...  10.8 us
    ppermute x6, waiting for transfers between devices, win_send(): return lax.ppermute(x, 'win', [(i, where(i)) for i in range(16)])  7.12 us
    ppermute x8, waiting for transfers between devices, space_swap(): return lax.ppermute(x, 'space', [(i, i ^ bits) for i in range(BLOCKS)])  7.02 us
    ppermute x4, starting transfers between devices, space_turn(): lax.ppermute(x, 'space', [(i, i // 8 * 8 + (i + 2 * d) % 8) for i in rang...  6.4 us
    ppermute x8, starting transfers between devices, space_swap(): return lax.ppermute(x, 'space', [(i, i ^ bits) for i in range(BLOCKS)])  3.96 us
  transfers between devices with their start and end apart: 18, of which 12 were waited for; matrix products, arithmetic and copies ran while one was open for 1% of the time, Pallas kernels for 0%

profile of v5, /device:TPU:2, one launch (start us, length us, event | category | flops | bytes accessed | tf_op | source)
XLA Modules:
  0.0 123.0 jit_solution(13441597301254506718)
XLA Ops:
  0.6 0.7 convert_bitcast_fusion
  1.3 0.8 slice_bitcast_fusion.1
  2.2 0.7 copy-done.13
  2.9 2.2 %collective-permute-start = (f32[24,1536]{1,0:T(8,128)S(1)}, f32[24,1536]{1,0:T(8,128)S(1)}, u32[]{:S(2)}, u32[]{:S(2)}) collective-permute-start(f32[24,1536]{1,0:T(8,128)S(1)} %maximum_maximum_fusion.p0), channel_id=1, source_target_pairs={{0,8},{1,9},{2,10},{3,11},{4,12},{5,13},{6,14},{7,15},{8,0},{9,1},... | collective-permute-start | bytes 442376 | tf_op jit(solution)/shard_map/ppermute | solution.py:483
  5.7 4.3 %collective-permute-done.p1 = f32[24,1536]{1,0:T(8,128)S(1)} collective-permute-done((f32[24,1536]{1,0:T(8,128)S(1)}, f32[24,1536]{1,0:T(8,128)S(1)}, u32[]{:S(2)}, u32[]{:S(2)}) %collective-permute-start) | collective-permute-done | bytes 147488 | tf_op jit(solution)/shard_map/ppermute | solution.py:483
  10.1 3.1 %collective-permute-start.2 = (f32[48,1536]{1,0:T(8,128)S(1)}, f32[48,1536]{1,0:T(8,128)S(1)}, u32[]{:S(2)}, u32[]{:S(2)}) collective-permute-start(f32[48,1536]{1,0:T(8,128)S(1)} %pad_maximum_fusion), channel_id=1, source_target_pairs={{0,6},{1,7},{2,0},{3,1},{4,2},{5,3},{6,4},{7,5},{8,14},{9,15},{10,... | collective-permute-start | bytes 884744 | tf_op jit(solution)/shard_map/ppermute | solution.py:486
  13.2 0.4 fusion.5
  13.6 0.7 stack.2.turns
  14.3 4.3 %collective-permute-done.2.p3 = f32[48,1536]{1,0:T(8,128)S(1)} collective-permute-done((f32[48,1536]{1,0:T(8,128)S(1)}, f32[48,1536]{1,0:T(8,128)S(1)}, u32[]{:S(2)}, u32[]{:S(2)}) %collective-permute-start.2) | collective-permute-done | bytes 294944 | tf_op jit(solution)/shard_map/ppermute | solution.py:486
  18.6 3.4 %collective-permute-done.1.p2 = f32[48,1536]{1,0:T(8,128)S(1)} collective-permute-done((f32[48,1536]{1,0:T(8,128)S(1)}, f32[48,1536]{1,0:T(8,128)S(1)}, u32[]{:S(2)}, u32[]{:S(2)}) %collective-permute-start.1) | collective-permute-done | bytes 294944 | tf_op jit(solution)/shard_map/ppermute | solution.py:486
  22.1 3.2 %collective-permute-start.4 = (f32[24,1536]{1,0:T(8,128)S(1)}, f32[24,1536]{1,0:T(8,128)S(1)}, u32[]{:S(2)}, u32[]{:S(2)}) collective-permute-start(f32[24,1536]{1,0:T(8,128)S(1)} %slice.25), channel_id=1, source_target_pairs={{0,6},{1,7},{2,0},{3,1},{4,2},{5,3},{6,4},{7,5},{8,14},{9,15},{10,... | collective-permute-start | bytes 442376 | tf_op jit(solution)/shard_map/ppermute | solution.py:486
  25.3 3.1 %collective-permute-done.3.p4 = f32[24,1536]{1,0:T(8,128)S(1)} collective-permute-done((f32[24,1536]{1,0:T(8,128)S(1)}, f32[24,1536]{1,0:T(8,128)S(1)}, u32[]{:S(2)}, u32[]{:S(2)}) %collective-permute-start.3) | collective-permute-done | bytes 147488 | tf_op jit(solution)/shard_map/ppermute | solution.py:486
  28.5 0.5 collective-permute-start.7
  29.1 0.4 collective-permute-start.6
  29.7 0.2 collective-permute-done.5.q0
  30.1 0.9 collective-permute-done.6.q1
  31.0 0.2 collective-permute-done.9.q4
  31.2 0.2 collective-permute-done.10.q5
  32.3 64.9 %shard_map.211 = (f32[2,24,384]{2,1,0:T(8,128)}, f32[32,512]{1,0:T(8,128)}, f32[32,512]{1,0:T(8,128)}) custom-call(s32[1]{0:T(128)} %bitcast.place, f32[8,8,256]{2,1,0:T(8,128)} %stack.2.turns, f32[16,256]{1,0:T(8,128)} %constant.76.clone.lanes, f32[384,384]{1,0:T(8,128)} %radial_op.1, bf16[256,512]{1,0:T(8,128)(2,1)} %constant.64.clone.tch, ...), custom_call_target="tpu_custom_call" | custom-call | tf_op jit(solution)/shard_map/pallas_call | solution.py:450
  97.2 0.4 collective-permute-start.11
  97.6 1.2 collective-permute-done.11
  98.7 0.9 add.99
  99.6 2.0 %collective-permute-start.13 = (f32[24,512]{1,0:T(8,128)S(1)}, f32[24,512]{1,0:T(8,128)S(1)}, u32[]{:S(2)}, u32[]{:S(2)}) collective-permute-start(f32[24,512]{1,0:T(8,128)S(1)} %slice.27), channel_id=1, source_target_pairs={{0,32},{16,48},{32,0},{48,16},{64,96},{80,112},{96,64},{112,80},{1... | collective-permute-start | bytes 147464 | tf_op jit(solution)/shard_map/ppermute | solution.py:489
  101.7 1.5 %collective-permute-start.12 = (f32[24,512]{1,0:T(8,128)S(1)}, f32[24,512]{1,0:T(8,128)S(1)}, u32[]{:S(2)}, u32[]{:S(2)}) collective-permute-start(f32[24,512]{1,0:T(8,128)S(1)} %slice.27), channel_id=1, source_target_pairs={{0,16},{16,0},{32,48},{48,32},{64,80},{80,64},{96,112},{112,96},{1... | collective-permute-start | bytes 147464 | tf_op jit(solution)/shard_map/ppermute | solution.py:489
  103.2 0.6 collective-permute-done.13
  103.8 2.8 %collective-permute-done.14 = f32[24,512]{1,0:T(8,128)S(1)} collective-permute-done((f32[24,512]{1,0:T(8,128)S(1)}, f32[24,512]{1,0:T(8,128)S(1)}, u32[]{:S(2)}, u32[]{:S(2)}) %collective-permute-start.14) | collective-permute-done | bytes 49184 | tf_op jit(solution)/shard_map/ppermute | solution.py:489
  106.7 5.9 %collective-permute-start.17 = (f32[24,512]{1,0:T(8,128)S(1)}, f32[24,512]{1,0:T(8,128)S(1)}, u32[]{:S(2)}, u32[]{:S(2)}) collective-permute-start(f32[24,512]{1,0:T(8,128)S(1)} %add_add_fusion.1), channel_id=1, source_target_pairs={{0,192},{16,208},{32,224},{48,240},{64,0},{80,16},{96,32},{112,48}... | collective-permute-start | bytes 147464 | tf_op jit(solution)/shard_map/ppermute | solution.py:489
  112.6 1.0 collective-permute-start.16
  113.6 2.8 %collective-permute-start.15 = (f32[24,512]{1,0:T(8,128)S(1)}, f32[24,512]{1,0:T(8,128)S(1)}, u32[]{:S(2)}, u32[]{:S(2)}) collective-permute-start(f32[24,512]{1,0:T(8,128)S(1)} %add_add_fusion.1), channel_id=1, source_target_pairs={{0,64},{16,80},{32,96},{48,112},{64,128},{80,144},{96,160},{112,17... | collective-permute-start | bytes 147464 | tf_op jit(solution)/shard_map/ppermute | solution.py:489
  116.4 0.5 slice.26
  117.6 3.6 %collective-permute-done.16 = f32[24,512]{1,0:T(8,128)S(1)} collective-permute-done((f32[24,512]{1,0:T(8,128)S(1)}, f32[24,512]{1,0:T(8,128)S(1)}, u32[]{:S(2)}, u32[]{:S(2)}) %collective-permute-start.16) | collective-permute-done | bytes 49184 | tf_op jit(solution)/shard_map/ppermute | solution.py:489
  121.2 0.6 add_add_fusion
  (51 shorter events, 1.7 us)
Async XLA Ops:
  1.3 0.8 copy-start.14
  1.3 0.8 copy-start.6
  2.1 0.7 copy-start.13
  2.9 25.6 %copy-start.2 = (f32[24,1536]{1,0:T(8,128)}, f32[24,1536]{1,0:T(8,128)S(1)}, u32[]{:S(2)}) copy-start(f32[24,1536]{1,0:T(8,128)S(1)} %maximum_maximum_fusion.p0) | copy-start | bytes 442372
  2.9 7.2 %collective-permute-start = (f32[24,1536]{1,0:T(8,128)S(1)}, f32[24,1536]{1,0:T(8,128)S(1)}, u32[]{:S(2)}, u32[]{:S(2)}) collective-permute-start(f32[24,1536]{1,0:T(8,128)S(1)} %maximum_maximum_fusion.p0), channel_id=1, source_target_pairs={{0,8},{1,9},{2,10},{3,11},{4,12},{5,13},{6,14},{7,15},{8,0},{9,1},... | collective-permute-start | bytes 442376 | tf_op jit(solution)/shard_map/ppermute | solution.py:483
  10.0 19.1 %copy-start.3 = (f32[24,1536]{1,0:T(8,128)}, f32[24,1536]{1,0:T(8,128)S(1)}, u32[]{:S(2)}) copy-start(f32[24,1536]{1,0:T(8,128)S(1)} %collective-permute-done.p1) | copy-start | bytes 442372
  10.1 8.5 %collective-permute-start.2 = (f32[48,1536]{1,0:T(8,128)S(1)}, f32[48,1536]{1,0:T(8,128)S(1)}, u32[]{:S(2)}, u32[]{:S(2)}) collective-permute-start(f32[48,1536]{1,0:T(8,128)S(1)} %pad_maximum_fusion), channel_id=1, source_target_pairs={{0,6},{1,7},{2,0},{3,1},{4,2},{5,3},{6,4},{7,5},{8,14},{9,15},{10,... | collective-permute-start | bytes 884744 | tf_op jit(solution)/shard_map/ppermute | solution.py:486
  13.2 8.8 %collective-permute-start.1 = (f32[48,1536]{1,0:T(8,128)S(1)}, f32[48,1536]{1,0:T(8,128)S(1)}, u32[]{:S(2)}, u32[]{:S(2)}) collective-permute-start(f32[48,1536]{1,0:T(8,128)S(1)} %pad_maximum_fusion), channel_id=1, source_target_pairs={{0,2},{1,3},{2,4},{3,5},{4,6},{5,7},{6,0},{7,1},{8,10},{9,11},{10,... | collective-permute-start | bytes 884744 | tf_op jit(solution)/shard_map/ppermute | solution.py:486
  18.6 10.5 %copy-start = (f32[48,1536]{1,0:T(8,128)}, f32[48,1536]{1,0:T(8,128)S(1)}, u32[]{:S(2)}) copy-start(f32[48,1536]{1,0:T(8,128)S(1)} %collective-permute-done.2.p3) | copy-start | bytes 884740
  22.0 9.4 %copy-start.1 = (f32[48,1536]{1,0:T(8,128)}, f32[48,1536]{1,0:T(8,128)S(1)}, u32[]{:S(2)}) copy-start(f32[48,1536]{1,0:T(8,128)S(1)} %collective-permute-done.1.p2) | copy-start | bytes 884740
  22.0 6.4 %collective-permute-start.3 = (f32[24,1536]{1,0:T(8,128)S(1)}, f32[24,1536]{1,0:T(8,128)S(1)}, u32[]{:S(2)}, u32[]{:S(2)}) collective-permute-start(f32[24,1536]{1,0:T(8,128)S(1)} %slice.24), channel_id=1, source_target_pairs={{0,2},{1,3},{2,4},{3,5},{4,6},{5,7},{6,0},{7,1},{8,10},{9,11},{10,... | collective-permute-start | bytes 442376 | tf_op jit(solution)/shard_map/ppermute | solution.py:486
  22.1 6.3 %collective-permute-start.4 = (f32[24,1536]{1,0:T(8,128)S(1)}, f32[24,1536]{1,0:T(8,128)S(1)}, u32[]{:S(2)}, u32[]{:S(2)}) collective-permute-start(f32[24,1536]{1,0:T(8,128)S(1)} %slice.25), channel_id=1, source_target_pairs={{0,6},{1,7},{2,0},{3,1},{4,2},{5,3},{6,4},{7,5},{8,14},{9,15},{10,... | collective-permute-start | bytes 442376 | tf_op jit(solution)/shard_map/ppermute | solution.py:486
  28.4 3.0 %copy-start.7 = (f32[24,1536]{1,0:T(8,128)}, f32[24,1536]{1,0:T(8,128)S(1)}, u32[]{:S(2)}) copy-start(f32[24,1536]{1,0:T(8,128)S(1)} %collective-permute-done.3.p4) | copy-start | bytes 442372
  28.4 3.0 %copy-start.8 = (f32[24,1536]{1,0:T(8,128)}, f32[24,1536]{1,0:T(8,128)S(1)}, u32[]{:S(2)}) copy-start(f32[24,1536]{1,0:T(8,128)S(1)} %collective-permute-done.4.p5) | copy-start | bytes 442372
  28.4 1.5 %collective-permute-start.5 = (f32[24,1536]{1,0:T(8,128)S(1)}, f32[24,1536]{1,0:T(8,128)S(1)}, u32[]{:S(2)}, u32[]{:S(2)}) collective-permute-start(f32[24,1536]{1,0:T(8,128)S(1)} %maximum_maximum_fusion.p0), channel_id=1, source_target_pairs={{0,1},{1,0},{2,3},{3,2},{4,5},{5,4},{6,7},{7,6},{8,9},{9,8},{10,11... | collective-permute-start | bytes 442376 | tf_op jit(solution)/shard_map/ppermute | solution.py:483
  28.5 2.8 %collective-permute-start.7 = (f32[48,1536]{1,0:T(8,128)S(1)}, f32[48,1536]{1,0:T(8,128)S(1)}, u32[]{:S(2)}, u32[]{:S(2)}) collective-permute-start(f32[48,1536]{1,0:T(8,128)S(1)} %collective-permute-done.1.p2), channel_id=1, source_target_pairs={{0,1},{1,0},{2,3},{3,2},{4,5},{5,4},{6,7},{7,6},{8,9},{9,8},{10,11... | collective-permute-start | bytes 884744 | tf_op jit(solution)/shard_map/ppermute | solution.py:483
  29.0 2.3 %collective-permute-start.8 = (f32[48,1536]{1,0:T(8,128)S(1)}, f32[48,1536]{1,0:T(8,128)S(1)}, u32[]{:S(2)}, u32[]{:S(2)}) collective-permute-start(f32[48,1536]{1,0:T(8,128)S(1)} %collective-permute-done.2.p3), channel_id=1, source_target_pairs={{0,1},{1,0},{2,3},{3,2},{4,5},{5,4},{6,7},{7,6},{8,9},{9,8},{10,11... | collective-permute-start | bytes 884744 | tf_op jit(solution)/shard_map/ppermute | solution.py:483
  29.1 1.8 %collective-permute-start.6 = (f32[24,1536]{1,0:T(8,128)S(1)}, f32[24,1536]{1,0:T(8,128)S(1)}, u32[]{:S(2)}, u32[]{:S(2)}) collective-permute-start(f32[24,1536]{1,0:T(8,128)S(1)} %collective-permute-done.p1), channel_id=1, source_target_pairs={{0,1},{1,0},{2,3},{3,2},{4,5},{5,4},{6,7},{7,6},{8,9},{9,8},{10,11... | collective-permute-start | bytes 442376 | tf_op jit(solution)/shard_map/ppermute | solution.py:483
  29.6 1.6 %collective-permute-start.9 = (f32[24,1536]{1,0:T(8,128)S(1)}, f32[24,1536]{1,0:T(8,128)S(1)}, u32[]{:S(2)}, u32[]{:S(2)}) collective-permute-start(f32[24,1536]{1,0:T(8,128)S(1)} %collective-permute-done.3.p4), channel_id=1, source_target_pairs={{0,1},{1,0},{2,3},{3,2},{4,5},{5,4},{6,7},{7,6},{8,9},{9,8},{10,11... | collective-permute-start | bytes 442376 | tf_op jit(solution)/shard_map/ppermute | solution.py:483
  29.9 1.5 %copy-start.9 = (f32[24,1536]{1,0:T(8,128)}, f32[24,1536]{1,0:T(8,128)S(1)}, u32[]{:S(2)}) copy-start(f32[24,1536]{1,0:T(8,128)S(1)} %collective-permute-done.5.q0) | copy-start | bytes 442372
  29.9 1.5 %collective-permute-start.10 = (f32[24,1536]{1,0:T(8,128)S(1)}, f32[24,1536]{1,0:T(8,128)S(1)}, u32[]{:S(2)}, u32[]{:S(2)}) collective-permute-start(f32[24,1536]{1,0:T(8,128)S(1)} %collective-permute-done.4.p5), channel_id=1, source_target_pairs={{0,1},{1,0},{2,3},{3,2},{4,5},{5,4},{6,7},{7,6},{8,9},{9,8},{10,11... | collective-permute-start | bytes 442376 | tf_op jit(solution)/shard_map/ppermute | solution.py:483
  31.0 0.7 copy-start.10
  31.2 0.7 copy-start.11
  31.4 0.8 copy-start.4
  31.4 0.9 copy-start.5
  97.2 1.5 %collective-permute-start.11 = (f32[32,512]{1,0:T(8,128)}, f32[32,512]{1,0:T(8,128)S(1)}, u32[]{:S(2)}, u32[]{:S(2)}) collective-permute-start(f32[32,512]{1,0:T(8,128)} %get-tuple-element.30), channel_id=1, source_target_pairs={{0,1},{1,0},{2,3},{3,2},{4,5},{5,4},{6,7},{7,6},{8,9},{9,8},{10,11... | collective-permute-start | bytes 196616 | tf_op jit(solution)/shard_map/ppermute | solution.py:483
  99.6 4.2 %collective-permute-start.13 = (f32[24,512]{1,0:T(8,128)S(1)}, f32[24,512]{1,0:T(8,128)S(1)}, u32[]{:S(2)}, u32[]{:S(2)}) collective-permute-start(f32[24,512]{1,0:T(8,128)S(1)} %slice.27), channel_id=1, source_target_pairs={{0,32},{16,48},{32,0},{48,16},{64,96},{80,112},{96,64},{112,80},{1... | collective-permute-start | bytes 147464 | tf_op jit(solution)/shard_map/ppermute | solution.py:489
  101.6 5.0 %collective-permute-start.14 = (f32[24,512]{1,0:T(8,128)S(1)}, f32[24,512]{1,0:T(8,128)S(1)}, u32[]{:S(2)}, u32[]{:S(2)}) collective-permute-start(f32[24,512]{1,0:T(8,128)S(1)} %slice.27), channel_id=1, source_target_pairs={{0,48},{16,32},{32,16},{48,0},{64,112},{80,96},{96,80},{112,64},{1... | collective-permute-start | bytes 147464 | tf_op jit(solution)/shard_map/ppermute | solution.py:489
  101.7 5.0 %collective-permute-start.12 = (f32[24,512]{1,0:T(8,128)S(1)}, f32[24,512]{1,0:T(8,128)S(1)}, u32[]{:S(2)}, u32[]{:S(2)}) collective-permute-start(f32[24,512]{1,0:T(8,128)S(1)} %slice.27), channel_id=1, source_target_pairs={{0,16},{16,0},{32,48},{48,32},{64,80},{80,64},{96,112},{112,96},{1... | collective-permute-start | bytes 147464 | tf_op jit(solution)/shard_map/ppermute | solution.py:489
  106.7 10.9 %collective-permute-start.17 = (f32[24,512]{1,0:T(8,128)S(1)}, f32[24,512]{1,0:T(8,128)S(1)}, u32[]{:S(2)}, u32[]{:S(2)}) collective-permute-start(f32[24,512]{1,0:T(8,128)S(1)} %add_add_fusion.1), channel_id=1, source_target_pairs={{0,192},{16,208},{32,224},{48,240},{64,0},{80,16},{96,32},{112,48}... | collective-permute-start | bytes 147464 | tf_op jit(solution)/shard_map/ppermute | solution.py:489
  112.6 8.6 %collective-permute-start.16 = (f32[24,512]{1,0:T(8,128)S(1)}, f32[24,512]{1,0:T(8,128)S(1)}, u32[]{:S(2)}, u32[]{:S(2)}) collective-permute-start(f32[24,512]{1,0:T(8,128)S(1)} %add_add_fusion.1), channel_id=1, source_target_pairs={{0,128},{16,144},{32,160},{48,176},{64,192},{80,208},{96,224},{112... | collective-permute-start | bytes 147464 | tf_op jit(solution)/shard_map/ppermute | solution.py:489
  113.6 7.6 %collective-permute-start.15 = (f32[24,512]{1,0:T(8,128)S(1)}, f32[24,512]{1,0:T(8,128)S(1)}, u32[]{:S(2)}, u32[]{:S(2)}) collective-permute-start(f32[24,512]{1,0:T(8,128)S(1)} %add_add_fusion.1), channel_id=1, source_target_pairs={{0,64},{16,80},{32,96},{48,112},{64,128},{80,144},{96,160},{112,17... | collective-permute-start | bytes 147464 | tf_op jit(solution)/shard_map/ppermute | solution.py:489
  (1 other events, 0.7 us)
